TPU v7x, 256 devices: a whole 4x4x8 slice. The times are simulated.
256 devices in a mesh: row: 16 (over y, z_hi), col: 16 (over x, z_lo, core).
Axes of the slice: x: 4, y: 4, z: 8 (z_hi: 4, z_lo: 2; z = z_hi * 2 + z_lo), core: 2. Of those that a mesh axis runs over, the one named last changes fastest.
Arguments:
- queries: bfloat16 [192, 768, 128], P('row', 'col'), may hold values from -6 to 6
- keys_values: bfloat16 [192, 768, 256], P('row', 'col'), may hold values from -6 to 6
- out_grad: bfloat16 [192, 768, 128], P('row', 'col'), may hold values from -48 to 48
- pair_bias: bfloat16 [4, 768, 768], P(None, 'row', 'col'), may hold values from -6 to 6
- log_norm: float32 [4, 192, 768], P(None, 'row', 'col'), may hold values from 7.2 to 8.6
- delta_rows: float32 [4, 192, 768], P(None, 'row', 'col'), may hold values from -96 to 96
- token_valid: int32 [768], replicated, may hold values from 0 to 1, as said below
Outputs:
- query_grad: bfloat16 [192, 768, 128], P('row', 'col')
- kv_grad: bfloat16 [768, 192, 256], P('col', 'row')
- bias_grad: float32 [4, 768, 768], P(None, 'row', 'col')
Inputs may be any that keep to these rules, and one draw needn't show every extreme that they name: `token_valid`: 1 for the first tokens and 0 for a padded tail; at least 384 ones and at least one 0.
All inputs are finite; a program needn't handle non-finite values.
Results may differ from a plain program's by a relative error of at most 0.025.
Values may be sent and summed in bfloat16 or wider, within the bound.
No kernel may reach another device: no remote copies, remote signals or barrier semaphores. Data moves between devices by JAX's collectives and lax.ppermute only.
A program may use at most 64 MiB of HBM per device.

v0:
```python
import jax
import jax.numpy as jnp
from jax import lax
from jax.sharding import PartitionSpec as P


def spread(block, axis, holder):
    block = jnp.where(lax.axis_index(axis) == holder, block, jnp.zeros_like(block))
    return lax.psum(block, axis)


def spans(amount):
    stride = amount
    while stride > 384 and stride % 2 == 0:
        stride = stride // 2
    return [(offset, stride) for offset in range(0, amount, stride)]


def block_terms(
    query_heads,
    grad_heads,
    norm_rows,
    delta_now,
    kv_piece,
    bias_piece,
    mask_piece,
    head_count,
    inv_root,
):
    row_count, amount, double = kv_piece.shape
    channels = double // 2
    head_size = channels // head_count
    key_heads = kv_piece[:, :, :channels].reshape(row_count, amount, head_count, head_size)
    value_heads = kv_piece[:, :, channels:].reshape(row_count, amount, head_count, head_size)
    scores = (
        jnp.einsum("ijhd,ikhd->ihjk", query_heads, key_heads, preferred_element_type=jnp.float32)
        * inv_root
    )
    scores = scores + bias_piece.astype(jnp.float32)[None] + mask_piece[None, None, None, :]
    probs = jnp.exp(scores - norm_rows[..., None])
    prob_grad = jnp.einsum(
        "ijhd,ikhd->ihjk", grad_heads, value_heads, preferred_element_type=jnp.float32
    )
    score_grad = probs * (prob_grad - delta_now[..., None])
    return (key_heads, probs.astype(jnp.bfloat16), score_grad, score_grad.astype(jnp.bfloat16))


def key_terms(query_heads, grad_heads, probs_low, score_low, inv_root):
    key_part = (
        jnp.einsum("ihjk,ijhd->kihd", score_low, query_heads, preferred_element_type=jnp.float32)
        * inv_root
    )
    value_part = jnp.einsum(
        "ihjk,ijhd->kihd", probs_low, grad_heads, preferred_element_type=jnp.float32
    )
    amount, row_count = (key_part.shape[0], key_part.shape[1])
    return jnp.concatenate(
        [key_part.reshape(amount, row_count, -1), value_part.reshape(amount, row_count, -1)],
        axis=-1,
    )


def on_device(queries, keys_values, out_grad, pair_bias, log_norm, delta_rows, token_valid):
    row_count, col_count, channels = queries.shape
    head_count = pair_bias.shape[0]
    head_size = channels // head_count
    inv_root = head_size ** (-0.5)
    n_rows = lax.axis_size("row")
    n_cols = lax.axis_size("col")
    row_per_col = n_rows // n_cols
    row_index = lax.axis_index("row")
    col_index = lax.axis_index("col")
    key_count = col_count * n_cols
    mask_bias = jnp.where(token_valid == 1, 0.0, -10000.0).astype(jnp.float32)
    bias_band = lax.all_gather(pair_bias, "col", axis=2, tiled=True)
    offset = 0
    pieces = spread(bias_band, "row", col_index * row_per_col + offset)
    query_heads = queries.reshape(row_count, col_count, head_count, head_size)
    grad_heads = out_grad.reshape(row_count, col_count, head_count, head_size)
    norm_rows = jnp.transpose(log_norm, (1, 0, 2))
    delta_now = jnp.transpose(delta_rows, (1, 0, 2))

    def terms(kv_piece, first_row):
        amount = kv_piece.shape[1]
        bias_piece = lax.dynamic_slice_in_dim(pieces, first_row, amount, 2)
        mask_piece = lax.dynamic_slice_in_dim(mask_bias, first_row, amount, 0)
        return block_terms(
            query_heads,
            grad_heads,
            norm_rows,
            delta_now,
            kv_piece,
            bias_piece,
            mask_piece,
            head_count,
            inv_root,
        )

    query_zero = jnp.zeros((row_count, col_count, head_count, head_size), jnp.float32)
    bias_zero = jnp.zeros((head_count, col_count, key_count), jnp.float32)
    gathered = lax.all_gather(keys_values, "col", axis=1, tiled=True)
    query_acc, bias_acc = (query_zero, bias_zero)
    for offset, stride in spans(key_count):
        segment = gathered[:, offset : offset + stride]
        key_heads, probs_low, score_grad, score_low = terms(segment, offset)
        add_query_acc = query_acc
        add_bias_acc = bias_acc
        add_query_acc = (
            add_query_acc
            + jnp.einsum(
                "ihjk,ikhd->ijhd", score_low, key_heads, preferred_element_type=jnp.float32
            )
            * inv_root
        )
        add_amount = score_grad.shape[3]
        current = lax.dynamic_slice_in_dim(add_bias_acc, offset, add_amount, 2)
        add_bias_acc = lax.dynamic_update_slice_in_dim(
            add_bias_acc, current + jnp.sum(score_grad, axis=0), offset, 2
        )
        query_acc = add_query_acc
        bias_acc = add_bias_acc
    first_row = jnp.int32(0)
    amount = col_count * lax.axis_size("col")
    outputs = []
    for offset, stride in spans(amount):
        segment = lax.dynamic_slice_in_dim(gathered, offset, stride, 1)
        key_heads, probs_low, score_grad, score_low = terms(segment, first_row + offset)
        outputs.append(key_terms(query_heads, grad_heads, probs_low, score_low, inv_root))
    kv_grad = lax.psum_scatter(
        jnp.concatenate(outputs, axis=0).astype(jnp.bfloat16),
        "col",
        scatter_dimension=0,
        tiled=True,
    )
    query_grad = query_acc.reshape(row_count, col_count, channels).astype(jnp.bfloat16)
    summed = lax.psum(bias_acc.astype(jnp.bfloat16), "row").astype(jnp.float32)
    owner_band = spread(summed.astype(jnp.bfloat16), "col", row_index // row_per_col).astype(
        summed.dtype
    )
    tile_rows = key_count // n_rows
    bias_grad = lax.dynamic_slice(
        owner_band,
        (0, row_index % row_per_col * tile_rows, col_index * col_count),
        (head_count, tile_rows, col_count),
    )
    return (query_grad, kv_grad, bias_grad)


def solution(mesh):
    placed = (
        P("row", "col", None),
        P("row", "col", None),
        P("row", "col", None),
        P(None, "row", "col"),
        P(None, "row", "col"),
        P(None, "row", "col"),
        P(),
    )
    return jax.shard_map(
        on_device,
        mesh=mesh,
        in_specs=placed,
        out_specs=(P("row", "col", None), P("col", "row", None), P(None, "row", "col")),
        check_vma=False,
    )
```

profile of v0, /device:TPU:32, one launch (start us, length us, event | category | flops | bytes accessed | tf_op | source)
XLA Modules:
  0.0 582.0 jit_solution(9771586334644392346)
XLA Ops:
  8.0 0.0 copy-start.14
  8.0 0.0 copy-start.15
  8.0 0.0 copy-start.19
  8.0 0.0 all-reduce.4.cloned.1.call-start
  8.1 1.0 copy.71
  9.1 20.4 %all_gather.7 = bf16[4,48,768]{1,0,2:T(4,128)(2,1)S(1)} all-gather(bf16[4,48,48]{1,0,2:T(4,128)(2,1)S(1)} %copy.71), channel_id=1, replica_groups=mesh['row'=16,'col'=16] {'col'}, dimensions={2}, use_global_device_ids=true | all-gather | bytes 313344 | tf_op jit(solution)/shard_map/all_gather | solution.py:75
  29.5 0.5 copy.72
  30.0 0.7 broadcast_select_fusion.1
  30.8 0.0 all-reduce.4.cloned.1.call-update
  30.8 0.0 all-gather.2.cloned.1.call-start
  30.8 0.5 all-gather.2.cloned.1.call-update
  31.4 0.0 all-reduce.6.cloned.1.call-start
  31.4 0.0 copy-done.14
  31.4 0.9 copy.69
  32.4 0.0 copy-done.15
  32.4 1.0 copy.73
  33.4 0.0 copy-done.19
  33.4 161.4 %all-reduce.4.cloned.1.call-done = bf16[4,48,768]{2,1,0:T(8,128)(2,1)} async-done(((bf16[4,48,768]{2,1,0:T(8,128)(2,1)}), bf16[4,48,768]{2,1,0:T(8,128)(2,1)}) %all-reduce.4.cloned.1.call-update) | async-done | bytes 294928 | tf_op jit(solution)/shard_map/psum | solution.py:9
  194.8 1.8 slice_convert_fusion
  196.7 3.8 fusion.29
  200.4 2.4 copy.76
  202.8 1.4 copy.75
  204.2 1.4 copy.74
  205.6 1.4 copy.70
  207.1 2.1 fusion.33
  209.2 0.0 copy-done.9
  209.2 0.0 copy-done.12
  209.2 0.0 copy-done.17
  209.2 2.1 fusion.14
  211.3 2.4 copy.78
  213.7 3.8 fusion.32
  217.5 0.0 copy-done.2
  217.5 0.5 multiply_convert_fusion.1
  218.0 0.8 copy-done.4
  218.8 1.4 copy.77
  220.2 0.0 copy-done.1
  220.2 0.0 copy-done.3
  220.2 0.0 copy-start.18
  220.2 0.7 fusion.34
  220.9 0.3 copy-done.10
  221.2 0.1 copy-done.11
  221.3 0.0 copy-done.18
  221.3 2.1 fusion.17
  223.4 0.0 copy-done.13
  223.4 2.4 fusion.31
  225.8 3.0 copy.80
  228.8 1.6 pad_maximum_fusion
  230.4 0.0 all-reduce.6.cloned.1.call-update
  230.5 0.0 all-reduce.8.cloned.1.call-start
  230.5 1.5 multiply_convert_fusion
  232.1 2.5 copy.79
  234.6 152.5 %all-reduce.6.cloned.1.call-done = bf16[4,48,768]{2,1,0:T(8,128)(2,1)} async-done(((bf16[4,48,768]{2,1,0:T(8,128)(2,1)}), bf16[4,48,768]{2,1,0:T(8,128)(2,1)}) %all-reduce.6.cloned.1.call-update) | async-done | bytes 294928 | tf_op jit(solution)/shard_map/psum | solution.py:136
  387.0 0.7 broadcast_select_fusion
  387.8 0.0 all-reduce.8.cloned.1.call-update
  387.8 0.0 reduce-scatter.2.cloned.1.call-start
  387.9 3.7 maximum_maximum_fusion
  391.5 0.0 reduce-scatter.2.cloned.1.call-update
  391.5 1.2 copy-done
  392.8 2.3 fusion.25
  395.1 0.7 fusion.21
  395.9 0.8 copy.81
  396.7 104.2 %all-reduce.8.cloned.1.call-done = bf16[4,48,768]{2,1,0:T(8,128)(2,1)} async-done(((bf16[4,48,768]{2,1,0:T(8,128)(2,1)}), bf16[4,48,768]{2,1,0:T(8,128)(2,1)}) %all-reduce.8.cloned.1.call-update) | async-done | bytes 294928 | tf_op jit(solution)/shard_map/psum | solution.py:9
  500.9 1.6 dynamic-slice_convert_fusion
  502.5 71.8 %reduce-scatter.2.cloned.1.call-done = bf16[48,12,256]{2,0,1:T(8,128)(2,1)} async-done(((bf16[768,12,256]{2,0,1:T(8,128)(2,1)}), bf16[48,12,256]{2,0,1:T(8,128)(2,1)}) %reduce-scatter.2.cloned.1.call-update) | async-done | bytes 294928 | tf_op jit(solution)/shard_map/reduce_scatter | solution.py:129
  (26 shorter events, 0.1 us)
Async XLA Ops:
  8.0 23.4 %copy-start.14 = (bf16[12,48,128]{2,1,0:T(8,128)(2,1)S(1)}, bf16[12,48,128]{2,1,0:T(8,128)(2,1)}, u32[]{:S(2)}) copy-start(bf16[12,48,128]{2,1,0:T(8,128)(2,1)} %param.7) | copy-start | bytes 442372
  8.0 24.4 %copy-start.15 = (bf16[12,48,128]{2,1,0:T(8,128)(2,1)S(1)}, bf16[12,48,128]{2,1,0:T(8,128)(2,1)}, u32[]{:S(2)}) copy-start(bf16[12,48,128]{2,1,0:T(8,128)(2,1)} %param.9) | copy-start | bytes 442372
  8.0 25.3 %copy-start.19 = (s32[768]{0:T(1024)S(1)}, s32[768]{0:T(1024)}, u32[]{:S(2)}) copy-start(s32[768]{0:T(1024)} %param.13) | copy-start | bytes 9220
  8.0 186.8 %all-reduce.4.cloned.1.call-start = ((), (), s32[]{:S(2)}) async-start(), calls=%async_computation.2 | async-start | bytes 589824 | tf_op jit(solution)/shard_map/psum | solution.py:9
  30.8 165.9 %all-gather.2.cloned.1.call-start = ((), (), s32[]{:S(2)}) async-start(), calls=%async_computation.1 | async-start | bytes 5013504 | tf_op jit(solution)/shard_map/all_gather | solution.py:101
  31.4 355.7 %all-reduce.6.cloned.1.call-start = ((), (), s32[]{:S(2)}) async-start(), calls=%async_computation.4 | async-start | bytes 589824 | tf_op jit(solution)/shard_map/psum | solution.py:136
  207.1 2.1 copy-start.9
  207.1 2.2 copy-start.12
  207.1 2.2 copy-start.17
  213.7 3.8 copy-start.2
  217.5 1.3 copy-start.4
  217.5 2.7 copy-start.1
  217.5 2.7 copy-start.3
  220.2 1.0 copy-start.10
  220.2 1.1 copy-start.11
  220.2 1.1 copy-start.18
  221.3 2.1 copy-start.13
  221.3 2.1 copy-start.20
  225.8 6.3 %copy-start.5 = (bf16[12,4,48,384]{3,2,1,0:T(8,128)(2,1)}, bf16[12,4,48,384]{3,2,1,0:T(8,128)(2,1)S(1)}, u32[]{:S(2)}) copy-start(bf16[12,4,48,384]{3,2,1,0:T(8,128)(2,1)S(1)} %get-tuple-element.27) | copy-start | bytes 5308420
  225.8 3.0 copy-start.16
  230.5 270.5 %all-reduce.8.cloned.1.call-start = ((), (), s32[]{:S(2)}) async-start(), calls=%async_computation.5 | async-start | bytes 589824 | tf_op jit(solution)/shard_map/psum | solution.py:9
  232.1 155.8 %copy-start.7 = (bf16[384,12,128]{2,0,1:T(8,128)(2,1)S(1)}, bf16[384,12,128]{2,0,1:T(8,128)(2,1)}, u32[]{:S(2)}) copy-start(bf16[384,12,128]{2,0,1:T(8,128)(2,1)} %copy.78) | copy-start | bytes 3538948
  232.1 155.8 %copy-start.8 = (bf16[384,12,128]{2,0,1:T(8,128)(2,1)S(1)}, bf16[384,12,128]{2,0,1:T(8,128)(2,1)}, u32[]{:S(2)}) copy-start(bf16[384,12,128]{2,0,1:T(8,128)(2,1)} %copy.77) | copy-start | bytes 3538948
  387.8 186.6 %reduce-scatter.2.cloned.1.call-start = ((), (), s32[]{:S(2)}) async-start(), calls=%async_computation.3 | async-start | bytes 5013504 | tf_op jit(solution)/shard_map/reduce_scatter | solution.py:129
  391.5 1.3 copy-start
  392.8 2.3 copy-start.6
Sparse Core Ops, SparseCore 0:
  30.9 163.8 all-reduce.3
  230.6 156.3 all-reduce.5
Sparse Core Ops, SparseCore 1:
  33.1 43.7 all-gather.1
  387.9 113.0 all-reduce.7
  504.1 70.2 reduce-scatter.1
where the time goes:
time: 586 us; the launch traced here: 582 us
  waiting for transfers between devices  491 us (84%)
  local copies, waits for them, and re-layouts  26.4 us (5%)
  blocking collectives  20.4 us (3%)
  matrix products  18.3 us (3%)
  between operations  15.8 us (3%)
  other arithmetic  10.2 us (2%)
    psum x2, waiting for transfers between devices, spread(): return lax.psum(block, axis)  266 us
    psum x1, waiting for transfers between devices, on_device(): summed = lax.psum(bias_acc.astype(jnp.bfloat16), 'row').astype(jnp.float32)  152 us
    reduce_scatter x1, waiting for transfers between devices, on_device(): lax.psum_scatter(jnp.concatenate(outputs, axis=0).astype(jnp.bfloat16), '...  71.8 us
    all_gather x1, blocking collectives, on_device(): bias_band = lax.all_gather(pair_bias, 'col', axis=2, tiled=True)  20.4 us
  transfers between devices with their start and end apart: 5, of which 4 were waited for; matrix products, arithmetic and copies ran while one was open for 3% of the time, Pallas kernels for 0%

commit v1 on v0

v1 whole, which is shorter than its diff:
```python
import functools
import math

import jax
import jax.numpy as jnp
from jax import lax
from jax.experimental import pallas as pl
from jax.experimental.pallas import tpu as pltpu
from jax.sharding import Mesh, PartitionSpec as P

BF = jnp.bfloat16
F32 = jnp.float32
LANES = 128


def call(body, name, out_shape, scratch=(), smem=(), n_in=1, limit=48 << 20):
    in_specs = [
        pl.BlockSpec(memory_space=pltpu.SMEM if i in smem else pltpu.VMEM) for i in range(n_in)
    ]
    out_specs = jax.tree.map(lambda _: pl.BlockSpec(memory_space=pltpu.VMEM), out_shape)
    return pl.pallas_call(
        body,
        name=name,
        out_shape=out_shape,
        in_specs=in_specs,
        out_specs=out_specs,
        scratch_shapes=list(scratch),
        compiler_params=pltpu.CompilerParams(vmem_limit_bytes=limit),
    )


def pack_kernel(root, q_ref, kv_ref, g_ref, bias_ref, norm_ref, delta_ref, mask_ref, out_ref, rows):
    heads, cols, _ = bias_ref.shape
    n_i, _, width = q_ref.shape
    size = width // heads
    pairs = n_i // 2
    for h in range(heads):
        lo, hi = h * size, (h + 1) * size
        for p in range(pairs):
            out_ref[h, p] = jnp.concatenate(
                [
                    q_ref[2 * p, :, lo:hi],
                    g_ref[2 * p, :, lo:hi],
                    q_ref[2 * p + 1, :, lo:hi],
                    g_ref[2 * p + 1, :, lo:hi],
                ],
                axis=-1,
            )
            out_ref[h, pairs + p] = jnp.concatenate(
                [
                    kv_ref[2 * p, :, lo:hi],
                    kv_ref[2 * p, :, width + lo : width + hi],
                    kv_ref[2 * p + 1, :, lo:hi],
                    kv_ref[2 * p + 1, :, width + lo : width + hi],
                ],
                axis=-1,
            )
        rows[...] = jnp.zeros_like(rows)
        norm = norm_ref[h] * root
        high = norm.astype(BF).astype(F32)
        rows[0:n_i, 0:cols] = high
        rows[16 : 16 + n_i, 0:cols] = norm - high
        delta = delta_ref[h]
        high = delta.astype(BF).astype(F32)
        rows[32 : 32 + n_i, 0:cols] = high
        rows[48 : 48 + n_i, 0:cols] = delta - high
        turned = jnp.transpose(rows[...])[0:cols]
        tile = bias_ref[h].astype(F32) + mask_ref[...]
        out_ref[h, 2 * pairs] = jnp.concatenate(
            [turned[:, 0:64], tile, jnp.zeros((cols, 64 - cols), F32)], axis=-1
        ).astype(BF)


def unpack_kernel(got_ref, a_ref, bias_ref):
    parts, blocks, cols, _ = got_ref.shape
    pairs = blocks // 2
    for p in range(pairs):
        a_ref[p] = got_ref[:, p].reshape(parts * cols, LANES)
    a_ref[pairs] = got_ref[:, blocks - 1].reshape(parts * cols, LANES)
    pieces = [got_ref[x, blocks - 1, :, 64 : 64 + cols].astype(F32) for x in range(parts)]
    pieces.append(jnp.zeros((cols, bias_ref.shape[2] - parts * cols), F32))
    band = jnp.concatenate(pieces, axis=-1).astype(BF)
    for r in range(bias_ref.shape[0]):
        bias_ref[r] = band


def main_kernel(
    inv_root,
    place_ref,
    got_ref,
    a0_ref,
    a1_ref,
    a2_ref,
    a3_ref,
    bias_ref,
    dq_ref,
    dkv_ref,
    dbias_ref,
    rows,
    bias_t,
    acc,
    dq_t,
):
    parts, blocks, cols, _ = got_ref.shape
    pairs = blocks // 2
    keys = parts * cols
    total = 4 * keys
    size = 32
    log2e = math.log2(math.e)
    zl, core = place_ref[0], place_ref[1]

    def row_of(b, x):
        return x * 4 + jnp.bitwise_xor(zl, b // 2) * 2 + jnp.bitwise_xor(core, b % 2)

    for b in range(4):
        for x in range(parts):
            at = b * keys + x * cols
            rows[at : at + cols] = bias_ref[row_of(b, x)].astype(F32)
    for t in range(0, total, LANES):
        bias_t[:, t : t + LANES] = (
            jnp.transpose(rows[t : t + LANES])[0:keys] * log2e
        )
    acc[...] = jnp.zeros_like(acc)
    lane = lax.broadcasted_iota(jnp.int32, (keys, LANES), 1)
    quarter = lax.broadcasted_iota(jnp.int32, (total, LANES), 1) // size
    a_refs = (a0_ref, a1_ref, a2_ref, a3_ref)
    extra = jnp.concatenate([a[pairs] for a in a_refs], axis=0)
    scale_row = jnp.where((lane // size) % 2 == 0, inv_root, 1.0)
    chunk = 256
    for p in range(pairs):
        qp = jnp.concatenate([a[p] for a in a_refs], axis=0)
        qx = jnp.concatenate([qp, extra], axis=1)
        kp = got_ref[:, pairs + p].reshape(keys, LANES)
        kt = jnp.transpose(kp.astype(F32)).astype(BF)
        zero = jnp.zeros_like(kp)
        left = []
        for s in range(4):
            i = 2 * p + s // 2
            base = 32 * (s % 2)
            ones = jnp.where((lane == base + i) | (lane == base + 16 + i), -1.0, 0.0).astype(BF)
            left.append(
                jnp.concatenate([jnp.where(lane // size == s, kp, zero), ones], axis=1)
            )
        qm = [jnp.where(quarter == s, qp, jnp.zeros_like(qp)) for s in range(4)]
        out = jnp.zeros((keys, LANES), F32)
        for t in range(0, total, chunk):
            here = qx[t : t + chunk]
            for e in range(2):
                scores = lax.dot_general(
                    left[2 * e], here, (((1,), (1,)), ((), ())), preferred_element_type=F32
                )
                grads = lax.dot_general(
                    left[2 * e + 1], here, (((1,), (1,)), ((), ())), preferred_element_type=F32
                )
                probs = jnp.exp2(scores * (inv_root * log2e) + bias_t[:, t : t + chunk])
                ds = probs * grads
                acc[:, t : t + chunk] += ds
                ds_low = ds.astype(BF)
                out += jnp.dot(ds_low, qm[2 * e][t : t + chunk], preferred_element_type=F32)
                out += jnp.dot(
                    probs.astype(BF), qm[2 * e + 1][t : t + chunk], preferred_element_type=F32
                )
                i = 2 * p + e
                dq_t[i * size : (i + 1) * size, t : t + chunk] = jnp.dot(
                    kt[2 * e * size : (2 * e + 1) * size], ds_low, preferred_element_type=F32
                )
        dkv_ref[p] = (out * scale_row).astype(BF)
    for quad in range(2 * pairs // 4):
        turned = jnp.transpose(dq_t[quad * LANES : (quad + 1) * LANES]) * inv_root
        for b in range(4):
            dq_ref[b, quad] = turned[b * keys : (b + 1) * keys].astype(BF)
    for t in range(0, total, LANES):
        rows[t : t + LANES, 0:keys] = jnp.transpose(acc[:, t : t + LANES])
    for b in range(4):
        for x in range(parts):
            at = b * keys + x * cols
            dbias_ref[row_of(b, x)] = rows[at : at + cols].astype(BF)


def merge_kernel(dq_ref, r1_ref, r2_ref, r3_ref, dkv_ref, db_ref, out_ref):
    parts, _, cols, _ = out_ref.shape
    quads = dq_ref.shape[0]
    pairs = dkv_ref.shape[0]
    total = (
        dq_ref[...].astype(F32)
        + r1_ref[...].astype(F32)
        + r2_ref[...].astype(F32)
        + r3_ref[...].astype(F32)
    ).astype(BF)
    bias = db_ref[0].astype(F32)
    for r in range(1, db_ref.shape[0]):
        bias = bias + db_ref[r].astype(F32)
    for x in range(parts):
        lo, hi = x * cols, (x + 1) * cols
        for quad in range(quads):
            out_ref[x, quad] = total[quad, lo:hi]
        for p in range(pairs):
            out_ref[x, quads + p] = dkv_ref[p, lo:hi]
        out_ref[x, quads + pairs] = jnp.concatenate(
            [bias[:, lo:hi], jnp.zeros((cols, LANES - cols), F32)], axis=-1
        ).astype(BF)


def final_kernel(got_ref, dq_ref, dkv_ref, db_ref, turn):
    heads, blocks, cols, _ = got_ref.shape
    size = 32
    n_i = dq_ref.shape[0]
    quads = n_i // 4
    pairs = n_i // 2
    for i in range(n_i):
        at = (i % 4) * size
        dq_ref[i] = jnp.concatenate(
            [got_ref[h, i // 4, :, at : at + size] for h in range(heads)], axis=-1
        )
        at = (i % 2) * 2 * size
        row = jnp.concatenate(
            [got_ref[h, quads + i // 2, :, at : at + size] for h in range(heads)]
            + [got_ref[h, quads + i // 2, :, at + size : at + 2 * size] for h in range(heads)],
            axis=-1,
        )
        turn[:, i, :] = row.astype(F32)
    dkv_ref[...] = turn[:, 0:n_i, :].astype(BF)
    for h in range(heads):
        db_ref[h] = got_ref[h, blocks - 1, :, 0:cols].astype(F32)


def on_device(queries, keys_values, out_grad, pair_bias, log_norm, delta_rows, token_valid):
    n_i, cols, width = queries.shape
    heads = pair_bias.shape[0]
    size = width // heads
    pairs = n_i // 2
    quads = n_i // 4
    n_rows = lax.axis_size("row")
    parts = lax.axis_size("x")
    keys = parts * cols
    wide = 2 * LANES
    x_at, zl, core = lax.axis_index("x"), lax.axis_index("zl"), lax.axis_index("core")
    place = jnp.stack([zl, core]).astype(jnp.int32)
    valid = lax.dynamic_slice_in_dim(token_valid, ((x_at * 2 + zl) * 2 + core) * cols, cols, 0)
    mask = jnp.where(valid == 1, 0.0, -10000.0).astype(F32)[None]
    struct = jax.ShapeDtypeStruct

    packed = call(
        functools.partial(pack_kernel, math.sqrt(size)),
        "pack",
        struct((heads, 2 * pairs + 1, cols, LANES), BF),
        scratch=[pltpu.VMEM((64, LANES), F32)],
        n_in=7,
    )(queries, keys_values, out_grad, pair_bias, log_norm, delta_rows, mask)
    got = lax.all_to_all(packed, "x", 0, 0, tiled=True)
    own, band = call(
        unpack_kernel,
        "unpack",
        (struct((pairs + 1, keys, LANES), BF), struct((n_rows, cols, wide), BF)),
    )(got)
    swap = [(0, 1), (1, 0)]
    over_core = lax.ppermute(own, "core", swap)
    over_zl = lax.ppermute(own, "zl", swap)
    bias_rows = lax.all_to_all(band, "row", 0, 0, tiled=True)
    over_both = lax.ppermute(over_zl, "core", swap)
    dq, dkv, dbias = call(
        functools.partial(main_kernel, size**-0.5),
        "main",
        (
            struct((4, quads, keys, LANES), BF),
            struct((pairs, keys, LANES), BF),
            struct((n_rows, cols, wide), BF),
        ),
        scratch=[
            pltpu.VMEM((4 * keys, wide), F32),
            pltpu.VMEM((keys, 4 * keys), F32),
            pltpu.VMEM((keys, 4 * keys), F32),
            pltpu.VMEM((n_i * size, 4 * keys), F32),
        ],
        smem=(0,),
        n_in=7,
    )(place, got, own, over_core, over_zl, over_both, bias_rows)
    both = [(0, 3), (1, 2), (2, 1), (3, 0)]
    r1 = lax.ppermute(dq[1], "core", swap)
    r2 = lax.ppermute(dq[2], "zl", swap)
    r3 = lax.ppermute(dq[3], ("zl", "core"), both)
    parts_in = lax.all_to_all(dbias, "row", 0, 0, tiled=True)
    merged = call(
        merge_kernel,
        "merge",
        struct((parts, quads + pairs + 1, cols, LANES), BF),
        n_in=6,
    )(dq[0], r1, r2, r3, dkv, parts_in)
    back = lax.all_to_all(merged, "x", 0, 0, tiled=True)
    query_grad, kv_grad, bias_grad = call(
        final_kernel,
        "final",
        (
            struct((n_i, cols, width), BF),
            struct((cols, n_i, 2 * width), BF),
            struct((heads, cols, cols), F32),
        ),
        scratch=[pltpu.VMEM((cols, 16, 2 * width), F32)],
    )(back)
    return query_grad, kv_grad, bias_grad


def solution(mesh):
    fine = Mesh(mesh.devices.reshape(16, 4, 2, 2), ("row", "x", "zl", "core"))
    col = ("x", "zl", "core")
    placed = (
        P("row", col, None),
        P("row", col, None),
        P("row", col, None),
        P(None, "row", col),
        P(None, "row", col),
        P(None, "row", col),
        P(),
    )
    return jax.shard_map(
        on_device,
        mesh=fine,
        in_specs=placed,
        out_specs=(P("row", col, None), P(col, "row", None), P(None, "row", col)),
        check_vma=False,
    )
```

time: 586 us -> 101 us (0.17)
  waiting for transfers between devices: 491 us -> 32 us
  starting transfers between devices: 0.21 us -> 22.3 us
  local copies, waits for them, and re-layouts: 26.4 us -> 5.03 us
  matrix products: 18.3 us -> 0 us
  between operations: 15.8 us -> 0.7 us
  Pallas kernels: 0 us -> 13.6 us
  other arithmetic: 10.2 us -> 0.83 us
    psum x3 -> x0, waiting for transfers between devices: 418 us -> none  [the longest x2 266 us: spread(): return lax.psum(block, axis)]
    reduce_scatter x1 -> x0, waiting for transfers between devices: 71.8 us -> none  [on_device(): lax.psum_scatter(jnp.concatenate(outputs, axis=0).astype(jnp.bfloat16), '...]
    ppermute x0 -> x6, waiting for transfers between devices: none -> 31.3 us  [the longest x1 15.1 us: on_device(): over_zl = lax.ppermute(own, 'zl', swap)]
    all_to_all x0 -> x2, blocking collectives: none -> 25.3 us  [the longest x1 14.8 us: on_device(): got = lax.all_to_all(packed, 'x', 0, 0, tiled=True)]
    all_gather x1 -> x0, blocking collectives: 20.4 us -> none  [on_device(): bias_band = lax.all_gather(pair_bias, 'col', axis=2, tiled=True)]
    all_to_all x0 -> x2, starting transfers between devices: none -> 19.3 us  [the longest x1 10.3 us: on_device(): bias_rows = lax.all_to_all(band, 'row', 0, 0, tiled=True)]
    dot_general x10 -> x0, matrix products: 18.3 us -> none  [the longest x2 6.2 us: block_terms(): jnp.einsum('ijhd,ikhd->ihjk', grad_heads, value_heads, preferred_element_...]
    pallas_call x0 -> x5, Pallas kernels: none -> 13.6 us  [the longest x1 10.7 us: on_device(): call(functools.partial(main_kernel, size ** (-0.5)), 'main', (struct((4,...]
  transfers between devices with their start and end apart: 5 -> 8, of which waited for: 4 -> 5; matrix products, arithmetic and copies ran while one was open for 3% -> 0% of each run, Pallas kernels for 0% -> 0%
where the time goes in v1:
time: 101 us; the launch traced here: 99.8 us
  waiting for transfers between devices  32 us (32%)
  blocking collectives  25.3 us (25%)
  starting transfers between devices  22.3 us (22%)
  Pallas kernels  13.6 us (13%)
  local copies, waits for them, and re-layouts  5.03 us (5%)
    ppermute x1, waiting for transfers between devices, on_device(): over_zl = lax.ppermute(own, 'zl', swap)  15.1 us
    all_to_all x1, blocking collectives, on_device(): got = lax.all_to_all(packed, 'x', 0, 0, tiled=True)  14.8 us
    ppermute x1, waiting for transfers between devices, on_device(): r3 = lax.ppermute(dq[3], ('zl', 'core'), both)  10.8 us
    pallas_call x1, Pallas kernels, on_device(): call(functools.partial(main_kernel, size ** (-0.5)), 'main', (struct((4,...  10.7 us
    all_to_all x1, blocking collectives, on_device(): back = lax.all_to_all(merged, 'x', 0, 0, tiled=True)  10.5 us
    all_to_all x1, starting transfers between devices, on_device(): bias_rows = lax.all_to_all(band, 'row', 0, 0, tiled=True)  10.3 us
    all_to_all x1, starting transfers between devices, on_device(): parts_in = lax.all_to_all(dbias, 'row', 0, 0, tiled=True)  8.95 us
    unnamed x10, local copies, waits for them, and re-layouts  4.19 us
  transfers between devices with their start and end apart: 8, of which 5 were waited for; matrix products, arithmetic and copies ran while one was open for 0% of the time, Pallas kernels for 0%

profile of v1, /device:TPU:32, one launch (start us, length us, event | category | flops | bytes accessed | tf_op | source)
XLA Modules:
  0.0 99.8 jit_solution(17081292212454444586)
XLA Ops:
  0.6 0.0 copy-start.1
  0.7 0.8 copy.10.norm_ref
  1.4 0.7 copy.11.delta_ref
  2.2 0.8 fusion.mask_ref
  2.9 0.0 copy-done.1
  2.9 0.0 copy-start
  2.9 1.0 copy-done
  3.9 0.0 copy-start.2
  3.9 0.9 copy-done.2
  4.8 0.0 copy-start.3
  4.8 0.8 copy-done.3
  5.6 0.6 pack.1
  6.2 14.8 %all_to_all.20.got_ref = bf16[4,13,48,128]{3,2,1,0:T(8,128)(2,1)S(1)} all-to-all(bf16[4,13,48,128]{3,2,1,0:T(8,128)(2,1)S(1)} %pack.1), channel_id=1, replica_groups=mesh['row'=16,'x'=4,'zl'=2,'core'=2] {'x'}, dimensions={0} | all-to-all | bytes 1277952 | tf_op jit(solution)/shard_map/all_to_all | solution.py:250
  21.0 0.9 unpack.1
  21.9 10.3 %all-to-all-start.1 = ((bf16[16,48,256]{2,1,0:T(8,128)(2,1)}), bf16[16,48,256]{2,1,0:T(8,128)(2,1)S(1)}, u32[]{:S(2)}, u32[]{:S(2)}) async-start(bf16[16,48,256]{2,1,0:T(8,128)(2,1)} %get-tuple-element.9), calls=%async_computation.1 | async-start | bytes 786432 | tf_op jit(solution)/shard_map/all_to_all | solution.py:259
  32.2 1.1 %collective-permute-start.1 = (bf16[7,192,128]{2,1,0:T(8,128)(2,1)S(1)}, bf16[7,192,128]{2,1,0:T(8,128)(2,1)S(1)}, u32[]{:S(2)}, u32[]{:S(2)}) collective-permute-start(bf16[7,192,128]{2,1,0:T(8,128)(2,1)S(1)} %get-tuple-element.8.a0_ref), channel_id=1, source_target_pairs={{0,2},{2,0},{1,3},{3,1},{4,6},{6,4},{5,7},{7,5},{8,10},{10,8},{9,1... | collective-permute-start | bytes 1032200 | tf_op jit(solution)/shard_map/ppermute | solution.py:258
  33.3 0.0 collective-permute-start
  33.3 15.1 %collective-permute-done.1.a2_ref = bf16[7,192,128]{2,1,0:T(8,128)(2,1)S(1)} collective-permute-done((bf16[7,192,128]{2,1,0:T(8,128)(2,1)S(1)}, bf16[7,192,128]{2,1,0:T(8,128)(2,1)S(1)}, u32[]{:S(2)}, u32[]{:S(2)}) %collective-permute-start.1) | collective-permute-done | bytes 344096 | tf_op jit(solution)/shard_map/ppermute | solution.py:258
  48.3 0.0 collective-permute-start.2
  48.4 0.1 pad_add_fusion.place_ref
  48.4 0.0 collective-permute-done.a1_ref
  48.4 1.6 %collective-permute-done.2.a3_ref = bf16[7,192,128]{2,1,0:T(8,128)(2,1)S(1)} collective-permute-done((bf16[7,192,128]{2,1,0:T(8,128)(2,1)S(1)}, bf16[7,192,128]{2,1,0:T(8,128)(2,1)S(1)}, u32[]{:S(2)}, u32[]{:S(2)}) %collective-permute-start.2) | collective-permute-done | bytes 344096 | tf_op jit(solution)/shard_map/ppermute | solution.py:260
  50.0 0.0 all-to-all-done.1.bias_ref
  50.0 10.7 %main.1 = (bf16[4,3,192,128]{3,2,1,0:T(8,128)(2,1)S(1)}, bf16[6,192,128]{2,1,0:T(8,128)(2,1)S(1)}, bf16[16,48,256]{2,1,0:T(8,128)(2,1)}) custom-call(s32[2]{0:T(128)S(1)} %pad_add_fusion.place_ref, bf16[4,13,48,128]{3,2,1,0:T(8,128)(2,1)S(1)} %all_to_all.20.got_ref, bf16[7,192,128]{2,1,0:T(8,128)(2,1)S(1)} %get-tuple-element.8.a0_ref, ...), custom_call_target="tpu_custom_call" | custom-call | tf_op jit(solution)/shard_map/main/pallas_call | solution.py:261
  60.8 8.9 %all-to-all-start.2 = ((bf16[16,48,256]{2,1,0:T(8,128)(2,1)}), bf16[16,48,256]{2,1,0:T(8,128)(2,1)S(1)}, u32[]{:S(2)}, u32[]{:S(2)}) async-start(bf16[16,48,256]{2,1,0:T(8,128)(2,1)} %get-tuple-element.12), calls=%async_computation.2 | async-start | bytes 786432 | tf_op jit(solution)/shard_map/all_to_all | solution.py:282
  69.8 0.6 collective-permute-start.5
  70.3 1.0 %collective-permute-start.4 = (bf16[3,192,128]{2,1,0:T(8,128)(2,1)S(1)}, bf16[3,192,128]{2,1,0:T(8,128)(2,1)S(1)}, u32[]{:S(2)}, u32[]{:S(2)}) collective-permute-start(bf16[3,192,128]{2,1,0:T(8,128)(2,1)S(1)} %get-tuple-element.17), channel_id=1, source_target_pairs={{0,2},{2,0},{1,3},{3,1},{4,6},{6,4},{5,7},{7,5},{8,10},{10,8},{9,1... | collective-permute-start | bytes 442376 | tf_op jit(solution)/shard_map/ppermute | solution.py:280
  71.3 0.4 collective-permute-start.3
  71.7 10.8 %collective-permute-done.5.r3_ref = bf16[3,192,128]{2,1,0:T(8,128)(2,1)S(1)} collective-permute-done((bf16[3,192,128]{2,1,0:T(8,128)(2,1)S(1)}, bf16[3,192,128]{2,1,0:T(8,128)(2,1)S(1)}, u32[]{:S(2)}, u32[]{:S(2)}) %collective-permute-start.5) | collective-permute-done | bytes 147488 | tf_op jit(solution)/shard_map/ppermute | solution.py:281
  82.5 3.8 %collective-permute-done.4.r2_ref = bf16[3,192,128]{2,1,0:T(8,128)(2,1)S(1)} collective-permute-done((bf16[3,192,128]{2,1,0:T(8,128)(2,1)S(1)}, bf16[3,192,128]{2,1,0:T(8,128)(2,1)S(1)}, u32[]{:S(2)}, u32[]{:S(2)}) %collective-permute-start.4) | collective-permute-done | bytes 147488 | tf_op jit(solution)/shard_map/ppermute | solution.py:280
  86.3 0.0 collective-permute-done.3.r1_ref
  86.3 0.7 all-to-all-done.2.db_ref
  87.1 0.2 merge.1
  87.2 10.5 %all_to_all.21.got_ref = bf16[4,10,48,128]{3,2,1,0:T(8,128)(2,1)S(1)} all-to-all(bf16[4,10,48,128]{3,2,1,0:T(8,128)(2,1)S(1)} %merge.1), channel_id=1, replica_groups=mesh['row'=16,'x'=4,'zl'=2,'core'=2] {'x'}, dimensions={0} | all-to-all | bytes 983040 | tf_op jit(solution)/shard_map/all_to_all | solution.py:289
  97.8 1.3 %final.1 = (bf16[12,48,128]{2,1,0:T(8,128)(2,1)}, bf16[48,12,256]{2,1,0:T(8,128)(2,1)S(1)}, f32[4,48,48]{2,1,0:T(8,128)}) custom-call(bf16[4,10,48,128]{3,2,1,0:T(8,128)(2,1)S(1)} %all_to_all.21.got_ref), custom_call_target="tpu_custom_call" | custom-call | tf_op jit(solution)/shard_map/final/pallas_call | solution.py:290
  99.0 0.8 copy.12
  (1 shorter events, 0.0 us)
Async XLA Ops:
  0.6 2.3 %copy-start.1 = (bf16[12,48,128]{2,1,0:T(8,128)(2,1)S(1)}, bf16[12,48,128]{2,1,0:T(8,128)(2,1)}, u32[]{:S(2)}) copy-start(bf16[12,48,128]{2,1,0:T(8,128)(2,1)} %q_ref.1) | copy-start | bytes 442372
  2.9 1.0 copy-start
  3.9 0.9 copy-start.2
  4.8 0.8 copy-start.3
  21.9 28.1 %all-to-all-start.1 = ((bf16[16,48,256]{2,1,0:T(8,128)(2,1)}), bf16[16,48,256]{2,1,0:T(8,128)(2,1)S(1)}, u32[]{:S(2)}, u32[]{:S(2)}) async-start(bf16[16,48,256]{2,1,0:T(8,128)(2,1)} %get-tuple-element.9), calls=%async_computation.1 | async-start | bytes 786432 | tf_op jit(solution)/shard_map/all_to_all | solution.py:259
  32.2 16.2 %collective-permute-start.1 = (bf16[7,192,128]{2,1,0:T(8,128)(2,1)S(1)}, bf16[7,192,128]{2,1,0:T(8,128)(2,1)S(1)}, u32[]{:S(2)}, u32[]{:S(2)}) collective-permute-start(bf16[7,192,128]{2,1,0:T(8,128)(2,1)S(1)} %get-tuple-element.8.a0_ref), channel_id=1, source_target_pairs={{0,2},{2,0},{1,3},{3,1},{4,6},{6,4},{5,7},{7,5},{8,10},{10,8},{9,1... | collective-permute-start | bytes 1032200 | tf_op jit(solution)/shard_map/ppermute | solution.py:258
  33.3 15.2 %collective-permute-start = (bf16[7,192,128]{2,1,0:T(8,128)(2,1)S(1)}, bf16[7,192,128]{2,1,0:T(8,128)(2,1)S(1)}, u32[]{:S(2)}, u32[]{:S(2)}) collective-permute-start(bf16[7,192,128]{2,1,0:T(8,128)(2,1)S(1)} %get-tuple-element.8.a0_ref), channel_id=1, source_target_pairs={{0,1},{1,0},{2,3},{3,2},{4,5},{5,4},{6,7},{7,6},{8,9},{9,8},{10,11... | collective-permute-start | bytes 1032200 | tf_op jit(solution)/shard_map/ppermute | solution.py:257
  48.3 1.7 %collective-permute-start.2 = (bf16[7,192,128]{2,1,0:T(8,128)(2,1)S(1)}, bf16[7,192,128]{2,1,0:T(8,128)(2,1)S(1)}, u32[]{:S(2)}, u32[]{:S(2)}) collective-permute-start(bf16[7,192,128]{2,1,0:T(8,128)(2,1)S(1)} %collective-permute-done.1.a2_ref), channel_id=1, source_target_pairs={{0,1},{1,0},{2,3},{3,2},{4,5},{5,4},{6,7},{7,6},{8,9},{9,8},{10,11... | collective-permute-start | bytes 1032200 | tf_op jit(solution)/shard_map/ppermute | solution.py:260
  60.8 26.3 %all-to-all-start.2 = ((bf16[16,48,256]{2,1,0:T(8,128)(2,1)}), bf16[16,48,256]{2,1,0:T(8,128)(2,1)S(1)}, u32[]{:S(2)}, u32[]{:S(2)}) async-start(bf16[16,48,256]{2,1,0:T(8,128)(2,1)} %get-tuple-element.12), calls=%async_computation.2 | async-start | bytes 786432 | tf_op jit(solution)/shard_map/all_to_all | solution.py:282
  69.8 12.7 %collective-permute-start.5 = (bf16[3,192,128]{2,1,0:T(8,128)(2,1)S(1)}, bf16[3,192,128]{2,1,0:T(8,128)(2,1)S(1)}, u32[]{:S(2)}, u32[]{:S(2)}) collective-permute-start(bf16[3,192,128]{2,1,0:T(8,128)(2,1)S(1)} %get-tuple-element.16), channel_id=1, source_target_pairs={{0,3},{1,2},{2,1},{3,0},{4,7},{5,6},{6,5},{7,4},{8,11},{9,10},{10,... | collective-permute-start | bytes 442376 | tf_op jit(solution)/shard_map/ppermute | solution.py:281
  70.3 16.0 %collective-permute-start.4 = (bf16[3,192,128]{2,1,0:T(8,128)(2,1)S(1)}, bf16[3,192,128]{2,1,0:T(8,128)(2,1)S(1)}, u32[]{:S(2)}, u32[]{:S(2)}) collective-permute-start(bf16[3,192,128]{2,1,0:T(8,128)(2,1)S(1)} %get-tuple-element.17), channel_id=1, source_target_pairs={{0,2},{2,0},{1,3},{3,1},{4,6},{6,4},{5,7},{7,5},{8,10},{10,8},{9,1... | collective-permute-start | bytes 442376 | tf_op jit(solution)/shard_map/ppermute | solution.py:280
  71.3 15.0 %collective-permute-start.3 = (bf16[3,192,128]{2,1,0:T(8,128)(2,1)S(1)}, bf16[3,192,128]{2,1,0:T(8,128)(2,1)S(1)}, u32[]{:S(2)}, u32[]{:S(2)}) collective-permute-start(bf16[3,192,128]{2,1,0:T(8,128)(2,1)S(1)} %get-tuple-element.18), channel_id=1, source_target_pairs={{0,1},{1,0},{2,3},{3,2},{4,5},{5,4},{6,7},{7,6},{8,9},{9,8},{10,11... | collective-permute-start | bytes 442376 | tf_op jit(solution)/shard_map/ppermute | solution.py:279

commit v2 on v1

v2 whole, which is shorter than its diff:
```python
import functools
import math

import jax
import jax.numpy as jnp
from jax import lax
from jax.experimental import pallas as pl
from jax.experimental.pallas import tpu as pltpu
from jax.sharding import PartitionSpec as P

BF = jnp.bfloat16
F32 = jnp.float32
LANES = 128
HEAD_GROUPS = [[0, 2, 12, 14], [1, 3, 13, 15], [4, 6, 8, 10], [5, 7, 9, 11]]


JOIN_COST = pl.CostEstimate(flops=2_000_000_000, bytes_accessed=1_000_000, transcendentals=0)
SUM_COST = pl.CostEstimate(flops=1_000_000_000, bytes_accessed=1_000_000, transcendentals=0)


def flip(bits):
    return [(c, c ^ bits) for c in range(16)]


def call(body, name, out_shape, scratch=(), n_in=1, space=pltpu.VMEM, limit=48 << 20, cost=None):
    spaces = space if isinstance(space, tuple) else (space,) * n_in
    in_specs = [pl.BlockSpec(memory_space=each) for each in spaces]
    out_specs = jax.tree.map(lambda _: pl.BlockSpec(memory_space=pltpu.VMEM), out_shape)
    return pl.pallas_call(
        body,
        name=name,
        out_shape=out_shape,
        in_specs=in_specs,
        out_specs=out_specs,
        scratch_shapes=list(scratch),
        compiler_params=pltpu.CompilerParams(vmem_limit_bytes=limit),
        cost_estimate=cost,
    )


def place():
    c = lax.axis_index("col")
    x = c // 4
    return c, jnp.bitwise_and(jnp.bitwise_xor(x, x // 2), 1), c % 2


def row_of(b, s):
    _, pair, core = place()
    there = jnp.bitwise_xor(pair, b // 2)
    x = there if s < 2 else 3 - there
    return x * 4 + (s % 2) * 2 + jnp.bitwise_xor(core, b % 2)


def pack_kernel(root, *refs):
    hbm, (out_ref, rows) = refs[:7], refs[7:9]
    local, sems = refs[9:16], refs[16]
    copies = [
        pltpu.make_async_copy(src, dst, sems.at[k])
        for k, (src, dst) in enumerate(zip(hbm, local))
    ]
    for copy in copies:
        copy.start()
    for copy in copies:
        copy.wait()
    q_ref, kv_ref, g_ref, bias_ref, norm_ref, delta_ref, valid_ref = local
    heads, cols, _ = bias_ref.shape
    n_i, _, width = q_ref.shape
    size = width // heads
    pairs = n_i // 2
    count = valid_ref.shape[0]
    valid = jnp.broadcast_to(valid_ref[...].reshape(1, count), (8, count))
    mask = jnp.where(valid == 1, 0.0, -10000.0).astype(F32)
    back = count - place()[0] * cols
    mask = pltpu.roll(mask, back, 1)[0:1, 0:cols]
    for h in range(heads):
        lo, hi = h * size, (h + 1) * size
        for p in range(pairs):
            out_ref[h, p] = jnp.concatenate(
                [
                    q_ref[2 * p, :, lo:hi],
                    g_ref[2 * p, :, lo:hi],
                    q_ref[2 * p + 1, :, lo:hi],
                    g_ref[2 * p + 1, :, lo:hi],
                ],
                axis=-1,
            )
            out_ref[h, pairs + p] = jnp.concatenate(
                [
                    kv_ref[2 * p, :, lo:hi],
                    kv_ref[2 * p, :, width + lo : width + hi],
                    kv_ref[2 * p + 1, :, lo:hi],
                    kv_ref[2 * p + 1, :, width + lo : width + hi],
                ],
                axis=-1,
            )
        rows[...] = jnp.zeros_like(rows)
        norm = norm_ref[:, h, :] * root
        high = norm.astype(BF).astype(F32)
        rows[0:n_i, 0:cols] = high
        rows[16 : 16 + n_i, 0:cols] = norm - high
        delta = delta_ref[:, h, :]
        high = delta.astype(BF).astype(F32)
        rows[32 : 32 + n_i, 0:cols] = high
        rows[48 : 48 + n_i, 0:cols] = delta - high
        turned = jnp.transpose(rows[...])[0:cols]
        tile = bias_ref[h].astype(F32) + mask
        out_ref[h, 2 * pairs] = jnp.concatenate(
            [turned[:, 0:64], tile, jnp.zeros((cols, 64 - cols), F32)], axis=-1
        ).astype(BF)


def own_kernel(got_ref, a_ref):
    parts, blocks, cols, _ = got_ref.shape
    pairs = blocks // 2
    for p in range(pairs):
        a_ref[p] = got_ref[:, p].reshape(parts * cols, LANES)
    a_ref[pairs] = got_ref[:, blocks - 1].reshape(parts * cols, LANES)


def fold(tile):
    tail = tile[:, LANES : LANES + 64]
    return jnp.concatenate(
        [
            tile[:, 0:LANES],
            jnp.concatenate([tail[0:16], tail[16:32]], axis=1),
            jnp.concatenate([tail[32:48], jnp.zeros((16, 64), tile.dtype)], axis=1),
        ],
        axis=0,
    )


def unfold(tile):
    side = tile[48:64]
    tail = jnp.concatenate([side, pltpu.roll(side, 64, 1), tile[64:80]], axis=0)
    return jnp.concatenate([tile[0:48], tail], axis=1)


def band_kernel(got_ref, bias_ref):
    parts, blocks, cols, _ = got_ref.shape
    pieces = [got_ref[x, blocks - 1, :, 64 : 64 + cols].astype(F32) for x in range(parts)]
    band = fold(jnp.concatenate(pieces, axis=-1)).astype(BF)
    for r in range(bias_ref.shape[0]):
        bias_ref[r] = band


def join_kernel(a0_ref, a1_ref, a2_ref, a3_ref, out_ref):
    keys = a0_ref.shape[1]
    for b, a in enumerate((a0_ref, a1_ref, a2_ref, a3_ref)):
        out_ref[:, b * keys : (b + 1) * keys] = a[...]


def main_kernel(
    inv_root,
    got_ref,
    a_ref,
    bias_ref,
    dq0_ref,
    dq2_ref,
    dqc_ref,
    dkv_ref,
    acc,
    rows,
    bias_t,
    dq_t,
):
    parts, blocks, cols, _ = got_ref.shape
    pairs = blocks // 2
    keys = parts * cols
    total = 4 * keys
    size = 32
    log2e = math.log2(math.e)
    dq_refs = (dq0_ref, dqc_ref.at[0], dq2_ref, dqc_ref.at[1])

    for b in range(4):
        for x in range(parts):
            at = b * keys + x * cols
            rows[at : at + cols] = unfold(bias_ref[row_of(b, x)].astype(F32))
    for t in range(0, total, LANES):
        bias_t[:, t : t + LANES] = (
            jnp.transpose(rows[t : t + LANES])[0:keys] * log2e
        )
    acc[...] = jnp.zeros_like(acc)
    lane = lax.broadcasted_iota(jnp.int32, (keys, LANES), 1)
    quarter = lax.broadcasted_iota(jnp.int32, (total, LANES), 1) // size
    extra = a_ref[pairs]
    scale_row = jnp.where((lane // size) % 2 == 0, inv_root, 1.0)
    chunk = 256
    for p in range(pairs):
        qp = a_ref[p]
        qx = jnp.concatenate([qp, extra], axis=1)
        kp = got_ref[:, pairs + p].reshape(keys, LANES)
        kt = jnp.transpose(kp.astype(F32)).astype(BF)
        zero = jnp.zeros_like(kp)
        left = []
        for s in range(4):
            i = 2 * p + s // 2
            base = 32 * (s % 2)
            ones = jnp.where((lane == base + i) | (lane == base + 16 + i), -1.0, 0.0).astype(BF)
            left.append(
                jnp.concatenate([jnp.where(lane // size == s, kp, zero), ones], axis=1)
            )
        qm = [jnp.where(quarter == s, qp, jnp.zeros_like(qp)) for s in range(4)]
        out = jnp.zeros((keys, LANES), F32)
        for t in range(0, total, chunk):
            here = qx[t : t + chunk]
            for e in range(2):
                scores = lax.dot_general(
                    left[2 * e], here, (((1,), (1,)), ((), ())), preferred_element_type=F32
                )
                grads = lax.dot_general(
                    left[2 * e + 1], here, (((1,), (1,)), ((), ())), preferred_element_type=F32
                )
                probs = jnp.exp2(scores * (inv_root * log2e) + bias_t[:, t : t + chunk])
                ds = probs * grads
                acc[:, t : t + chunk] += ds
                ds_low = ds.astype(BF)
                out += jnp.dot(ds_low, qm[2 * e][t : t + chunk], preferred_element_type=F32)
                out += jnp.dot(
                    probs.astype(BF), qm[2 * e + 1][t : t + chunk], preferred_element_type=F32
                )
                i = 2 * p + e
                dq_t[i * size : (i + 1) * size, t : t + chunk] = jnp.dot(
                    kt[2 * e * size : (2 * e + 1) * size], ds_low, preferred_element_type=F32
                )
        dkv_ref[p] = (out * scale_row).astype(BF)
    for quad in range(2 * pairs // 4):
        turned = jnp.transpose(dq_t[quad * LANES : (quad + 1) * LANES]) * inv_root
        for b in range(4):
            dq_refs[b][quad] = turned[b * keys : (b + 1) * keys].astype(BF)


def turn_kernel(cols, acc, dbias_ref, rows):
    keys, total = acc.shape
    for t in range(0, total, LANES):
        rows[t : t + LANES, 0:keys] = jnp.transpose(acc[:, t : t + LANES])
    for b in range(4):
        for x in range(keys // cols):
            at = b * keys + x * cols
            dbias_ref[row_of(b, x)] = fold(rows[at : at + cols]).astype(BF)


def fold_core_kernel(dq0_ref, dq2_ref, got_ref, keep_ref, send_ref):
    keep_ref[...] = dq0_ref[...].astype(F32) + got_ref[0].astype(F32)
    send_ref[...] = (dq2_ref[...].astype(F32) + got_ref[1].astype(F32)).astype(BF)


def sum_kernel(keep_ref, got_ref, out_ref):
    out_ref[...] = (keep_ref[...] + got_ref[...].astype(F32)).astype(BF)


def merge_kernel(total, dkv_ref, db_ref, out_ref):
    parts, _, cols, _ = out_ref.shape
    quads = total.shape[0]
    pairs = dkv_ref.shape[0]
    bias = db_ref[0].astype(F32)
    for r in range(1, db_ref.shape[0]):
        bias = bias + db_ref[r].astype(F32)
    bias = unfold(bias)
    for x in range(parts):
        lo, hi = x * cols, (x + 1) * cols
        for quad in range(quads):
            out_ref[x, quad] = total[quad, lo:hi]
        for p in range(pairs):
            out_ref[x, quads + p] = dkv_ref[p, lo:hi]
        out_ref[x, quads + pairs] = jnp.concatenate(
            [bias[:, lo:hi], jnp.zeros((cols, LANES - cols), F32)], axis=-1
        ).astype(BF)


def final_kernel(got_ref, dq_ref, dkv_ref, db_ref):
    heads, blocks, cols, _ = got_ref.shape
    size = 32
    n_i = dq_ref.shape[0]
    quads = n_i // 4
    for i in range(n_i):
        at = (i % 4) * size
        dq_ref[i] = jnp.concatenate(
            [got_ref[h, i // 4, :, at : at + size] for h in range(heads)], axis=-1
        )
        at = (i % 2) * 2 * size
        dkv_ref[i] = jnp.concatenate(
            [got_ref[h, quads + i // 2, :, at : at + size] for h in range(heads)]
            + [got_ref[h, quads + i // 2, :, at + size : at + 2 * size] for h in range(heads)],
            axis=-1,
        )
    for h in range(heads):
        db_ref[h] = got_ref[h, blocks - 1, :, 0:cols].astype(F32)


def on_device(queries, keys_values, out_grad, pair_bias, log_norm, delta_rows, token_valid):
    n_i, cols, width = queries.shape
    heads = pair_bias.shape[0]
    size = width // heads
    pairs = n_i // 2
    quads = n_i // 4
    n_rows = lax.axis_size("row")
    parts = heads
    keys = parts * cols
    wide = 2 * LANES
    struct = jax.ShapeDtypeStruct
    inputs = (
        queries,
        keys_values,
        out_grad,
        pair_bias,
        jnp.transpose(log_norm, (1, 0, 2)),
        jnp.transpose(delta_rows, (1, 0, 2)),
        token_valid,
    )

    packed = call(
        functools.partial(pack_kernel, math.sqrt(size)),
        "pack",
        struct((heads, 2 * pairs + 1, cols, LANES), BF),
        scratch=[pltpu.VMEM((64, LANES), F32)]
        + [pltpu.VMEM(v.shape, v.dtype) for v in inputs]
        + [pltpu.SemaphoreType.DMA((len(inputs),))],
        n_in=len(inputs),
        space=pltpu.HBM,
        limit=62 << 20,
    )(*inputs)
    got = lax.all_to_all(packed, "col", 0, 0, tiled=True, axis_index_groups=HEAD_GROUPS)
    own = call(own_kernel, "own", struct((pairs + 1, keys, LANES), BF))(got)
    over_x = lax.ppermute(own, "col", flip(4))
    over_core = lax.ppermute(own, "col", flip(1))
    folded = struct((n_rows, 80, LANES), BF)
    dq_block = struct((quads, keys, LANES), BF)
    band = call(band_kernel, "band", folded)(got)
    bias_rows = lax.all_to_all(band, "row", 0, 0, tiled=True)
    over_both = lax.ppermute(over_x, "col", flip(1))
    joined = call(
        join_kernel,
        "join",
        struct((pairs + 1, 4 * keys, LANES), BF),
        n_in=4,
        cost=JOIN_COST,
    )(own, over_core, over_x, over_both)
    dq0, dq2, dq_core, dkv, acc = call(
        functools.partial(main_kernel, size**-0.5),
        "main",
        (
            dq_block,
            dq_block,
            struct((2, quads, keys, LANES), BF),
            struct((pairs, keys, LANES), BF),
            struct((keys, 4 * keys), F32),
        ),
        scratch=[
            pltpu.VMEM((4 * keys, wide), F32),
            pltpu.VMEM((keys, 4 * keys), F32),
            pltpu.VMEM((n_i * size, 4 * keys), F32),
        ],
        n_in=3,
    )(got, joined, bias_rows)
    over_core = lax.ppermute(dq_core, "col", flip(1))
    dbias = call(
        functools.partial(turn_kernel, cols),
        "turn",
        folded,
        scratch=[pltpu.VMEM((4 * keys, wide), F32)],
    )(acc)
    keep, send = call(
        fold_core_kernel,
        "fold_core",
        (struct((quads, keys, LANES), F32), dq_block),
        n_in=3,
    )(dq0, dq2, over_core)
    over_x = lax.ppermute(send, "col", flip(4))
    parts_in = lax.all_to_all(dbias, "row", 0, 0, tiled=True)
    total = call(sum_kernel, "sum", dq_block, n_in=2, cost=SUM_COST)(keep, over_x)
    merged = call(
        merge_kernel,
        "merge",
        struct((parts, quads + pairs + 1, cols, LANES), BF),
        n_in=3,
    )(total, dkv, parts_in)
    back = lax.all_to_all(merged, "col", 0, 0, tiled=True, axis_index_groups=HEAD_GROUPS)
    query_grad, kv_grad, bias_grad = call(
        final_kernel,
        "final",
        (
            struct((n_i, cols, width), BF),
            struct((n_i, cols, 2 * width), BF),
            struct((heads, cols, cols), F32),
        ),
    )(back)
    kv_grad = jnp.transpose(kv_grad, (1, 0, 2))
    return query_grad, kv_grad, bias_grad


def solution(mesh):
    placed = (
        P("row", "col", None),
        P("row", "col", None),
        P("row", "col", None),
        P(None, "row", "col"),
        P(None, "row", "col"),
        P(None, "row", "col"),
        P(),
    )
    return jax.shard_map(
        on_device,
        mesh=mesh,
        in_specs=placed,
        out_specs=(P("row", "col", None), P("col", "row", None), P(None, "row", "col")),
        check_vma=False,
    )
```

time: 101 us -> 82.4 us (0.82)
  waiting for transfers between devices: 32 us -> 23.5 us
  starting transfers between devices: 22.3 us -> 16.4 us
  local copies, waits for them, and re-layouts: 5.03 us -> 0 us
  Pallas kernels: 13.6 us -> 15.5 us
    ppermute x6 -> x5, waiting for transfers between devices: 31.3 us -> 7.36 us  [the longest x1 4.16 us: on_device(): over_x = lax.ppermute(send, 'col', flip(4))]
    all_to_all x1, waiting for transfers between devices: 0.01 us -> 11.2 us  [on_device(): bias_rows = lax.all_to_all(band, 'row', 0, 0, tiled=True)]
    all_to_all x1, starting transfers between devices: 8.95 us -> 3.54 us  [on_device(): parts_in = lax.all_to_all(dbias, 'row', 0, 0, tiled=True)]
    all_to_all x1, waiting for transfers between devices: 0.74 us -> 4.93 us  [on_device(): parts_in = lax.all_to_all(dbias, 'row', 0, 0, tiled=True)]
    unnamed x10 -> x0, local copies, waits for them, and re-layouts: 4.19 us -> none
    pallas_call x1, Pallas kernels: 0.59 us -> 2.63 us  [on_device(): call(functools.partial(pack_kernel, math.sqrt(size)), 'pack', struct((hea...]
    ppermute x6 -> x5, starting transfers between devices: 3.05 us -> 2.58 us  [the longest x1 1.82 us: on_device(): over_x = lax.ppermute(send, 'col', flip(4))]
    pallas_call x3 -> x8, Pallas kernels: 12.9 us -> 12.7 us  [the longest x1 9.39 us: on_device(): call(functools.partial(main_kernel, size ** (-0.5)), 'main', (dq_block, d...]
  transfers between devices with their start and end apart: 8 -> 7, of which waited for: 5 -> 6; matrix products, arithmetic and copies ran while one was open for 0% -> 0% of each run, Pallas kernels for 0% -> 1%
where the time goes in v2:
time: 82.4 us; the launch traced here: 82 us
  blocking collectives  25.9 us (31%)
  waiting for transfers between devices  23.5 us (29%)
  starting transfers between devices  16.4 us (20%)
  Pallas kernels  15.5 us (19%)
    all_to_all x1, blocking collectives, on_device(): lax.all_to_all(packed, 'col', 0, 0, tiled=True, axis_index_groups=HEAD_GR...  15.4 us
    all_to_all x1, waiting for transfers between devices, on_device(): bias_rows = lax.all_to_all(band, 'row', 0, 0, tiled=True)  11.2 us
    all_to_all x1, blocking collectives, on_device(): lax.all_to_all(merged, 'col', 0, 0, tiled=True, axis_index_groups=HEAD_GR...  10.6 us
    all_to_all x1, starting transfers between devices, on_device(): bias_rows = lax.all_to_all(band, 'row', 0, 0, tiled=True)  10.3 us
    pallas_call x1, Pallas kernels, on_device(): call(functools.partial(main_kernel, size ** (-0.5)), 'main', (dq_block, d...  9.39 us
    all_to_all x1, waiting for transfers between devices, on_device(): parts_in = lax.all_to_all(dbias, 'row', 0, 0, tiled=True)  4.93 us
    ppermute x1, waiting for transfers between devices, on_device(): over_x = lax.ppermute(send, 'col', flip(4))  4.16 us
    all_to_all x1, starting transfers between devices, on_device(): parts_in = lax.all_to_all(dbias, 'row', 0, 0, tiled=True)  3.54 us
  transfers between devices with their start and end apart: 7, of which 6 were waited for; matrix products, arithmetic and copies ran while one was open for 0% of the time, Pallas kernels for 1%

profile of v2, /device:TPU:32, one launch (start us, length us, event | category | flops | bytes accessed | tf_op | source)
XLA Modules:
  0.0 82.0 jit_solution(10874182574603555614)
XLA Ops:
  0.6 2.6 %pack.1 = bf16[4,13,48,128]{3,2,1,0:T(8,128)(2,1)} custom-call(bf16[12,48,128]{2,1,0:T(8,128)(2,1)} %refs_0_.1, bf16[12,48,256]{2,1,0:T(8,128)(2,1)} %refs_1_.1, bf16[12,48,128]{2,1,0:T(8,128)(2,1)} %refs_2_.1, bf16[4,48,48]{2,1,0:T(8,128)(2,1)} %refs_3_.1, f32[12,4,48]{2,1,0:T(4,128)} %bitcast.3, f32[12,4,48]{2,1,0:T(4,128)} %bitcast.4, s32[768]{0:T(1024)} %refs_6_.1), custom_call_target="tpu_custom_call" | custom-call | tf_op jit(solution)/shard_map/pack/pallas_call | solution.py:311
  3.3 15.4 %all_to_all.20.got_ref = bf16[4,13,48,128]{3,2,1,0:T(8,128)(2,1)S(1)} all-to-all(bf16[4,13,48,128]{3,2,1,0:T(8,128)(2,1)} %pack.1), channel_id=1, replica_groups={{0,2,12,14},{1,3,13,15},{4,6,8,10},{5,7,9,11},{16,18,28,30},{17,19,29,3..., dimensions={0} | all-to-all | bytes 1277952 | tf_op jit(solution)/shard_map/all_to_all | solution.py:322
  18.6 0.1 collective-permute-start.1
  18.7 0.9 %band.1 = bf16[16,80,128]{2,1,0:T(8,128)(2,1)} custom-call(bf16[4,13,48,128]{3,2,1,0:T(8,128)(2,1)S(1)} %all_to_all.20.got_ref), custom_call_target="tpu_custom_call" | custom-call | tf_op jit(solution)/shard_map/band/pallas_call | solution.py:328
  19.6 10.3 %all-to-all-start.1 = ((bf16[16,80,128]{2,1,0:T(8,128)(2,1)}), bf16[16,80,128]{2,1,0:T(8,128)(2,1)S(1)}, u32[]{:S(2)}, u32[]{:S(2)}) async-start(bf16[16,80,128]{2,1,0:T(8,128)(2,1)} %band.1), calls=%async_computation.1 | async-start | bytes 655360 | tf_op jit(solution)/shard_map/all_to_all | solution.py:329
  29.9 0.1 collective-permute-start
  30.0 0.0 collective-permute-done.1.a2_ref
  30.0 0.5 collective-permute-start.2
  30.5 1.1 %collective-permute-done.a1_ref = bf16[7,192,128]{2,1,0:T(8,128)(2,1)S(1)} collective-permute-done((bf16[7,192,128]{2,1,0:T(8,128)(2,1)S(1)}, bf16[7,192,128]{2,1,0:T(8,128)(2,1)S(1)}, u32[]{:S(2)}, u32[]{:S(2)}) %collective-permute-start) | collective-permute-done | bytes 344096 | tf_op jit(solution)/shard_map/ppermute | solution.py:325
  31.7 0.5 collective-permute-done.2.a3_ref
  32.2 0.1 join.1.a_ref
  32.3 11.2 %all-to-all-done.1.bias_ref = bf16[16,80,128]{2,1,0:T(8,128)(2,1)S(1)} async-done(((bf16[16,80,128]{2,1,0:T(8,128)(2,1)}), bf16[16,80,128]{2,1,0:T(8,128)(2,1)S(1)}, u32[]{:S(2)}, u32[]{:S(2)}) %all-to-all-start.1) | async-done | bytes 327712 | tf_op jit(solution)/shard_map/all_to_all | solution.py:329
  43.4 9.4 %main.1 = (bf16[3,192,128]{2,1,0:T(8,128)(2,1)S(1)}, bf16[3,192,128]{2,1,0:T(8,128)(2,1)S(1)}, bf16[2,3,192,128]{3,2,1,0:T(8,128)(2,1)S(1)}, bf16[6,192,128]{2,1,0:T(8,128)(2,1)S(1)}, f32[192,768]{1,0:T(8,128)S(1)}) custom-call(bf16[4,13,48,128]{3,2,1,0:T(8,128)(2,1)S(1)} %all_to_all.20.got_ref, bf16[7,768,128]{2,1,0:T(8,128)(2,1)S(1)} %join.1.a_ref, ...), custom_call_target="tpu_custom_call" | custom-call | tf_op jit(solution)/shard_map/main/pallas_call | solution.py:338
  52.8 1.1 %turn.1 = bf16[16,80,128]{2,1,0:T(8,128)(2,1)} custom-call(f32[192,768]{1,0:T(8,128)S(1)} %get-tuple-element.19.acc), custom_call_target="tpu_custom_call" | custom-call | tf_op jit(solution)/shard_map/turn/pallas_call | solution.py:356
  53.9 3.5 %all-to-all-start.2 = ((bf16[16,80,128]{2,1,0:T(8,128)(2,1)}), bf16[16,80,128]{2,1,0:T(8,128)(2,1)S(1)}, u32[]{:S(2)}, u32[]{:S(2)}) async-start(bf16[16,80,128]{2,1,0:T(8,128)(2,1)} %turn.1), calls=%async_computation.2 | async-start | bytes 655360 | tf_op jit(solution)/shard_map/all_to_all | solution.py:369
  57.5 0.1 collective-permute-start.3
  57.6 1.6 %collective-permute-done.3.got_ref = bf16[2,3,192,128]{3,2,1,0:T(8,128)(2,1)S(1)} collective-permute-done((bf16[2,3,192,128]{3,2,1,0:T(8,128)(2,1)S(1)}, bf16[2,3,192,128]{3,2,1,0:T(8,128)(2,1)S(1)}, u32[]{:S(2)}, u32[]{:S(2)}) %collective-permute-start.3) | collective-permute-done | bytes 294944 | tf_op jit(solution)/shard_map/ppermute | solution.py:355
  59.1 0.1 fold_core.1
  59.2 1.8 %collective-permute-start.4 = (bf16[3,192,128]{2,1,0:T(8,128)(2,1)S(1)}, bf16[3,192,128]{2,1,0:T(8,128)(2,1)S(1)}, u32[]{:S(2)}, u32[]{:S(2)}) collective-permute-start(bf16[3,192,128]{2,1,0:T(8,128)(2,1)S(1)} %get-tuple-element.17), channel_id=1, source_target_pairs={{0,4},{1,5},{2,6},{3,7},{4,0},{5,1},{6,2},{7,3},{8,12},{9,13},{10,... | collective-permute-start | bytes 442376 | tf_op jit(solution)/shard_map/ppermute | solution.py:368
  61.0 4.2 %collective-permute-done.4.got_ref = bf16[3,192,128]{2,1,0:T(8,128)(2,1)S(1)} collective-permute-done((bf16[3,192,128]{2,1,0:T(8,128)(2,1)S(1)}, bf16[3,192,128]{2,1,0:T(8,128)(2,1)S(1)}, u32[]{:S(2)}, u32[]{:S(2)}) %collective-permute-start.4) | collective-permute-done | bytes 147488 | tf_op jit(solution)/shard_map/ppermute | solution.py:368
  65.2 4.9 %all-to-all-done.2.db_ref = bf16[16,80,128]{2,1,0:T(8,128)(2,1)S(1)} async-done(((bf16[16,80,128]{2,1,0:T(8,128)(2,1)}), bf16[16,80,128]{2,1,0:T(8,128)(2,1)S(1)}, u32[]{:S(2)}, u32[]{:S(2)}) %all-to-all-start.2) | async-done | bytes 327712 | tf_op jit(solution)/shard_map/all_to_all | solution.py:369
  70.1 0.2 merge.1
  70.3 10.6 %all_to_all.21.got_ref = bf16[4,10,48,128]{3,2,1,0:T(8,128)(2,1)S(1)} all-to-all(bf16[4,10,48,128]{3,2,1,0:T(8,128)(2,1)S(1)} %merge.1), channel_id=1, replica_groups={{0,2,12,14},{1,3,13,15},{4,6,8,10},{5,7,9,11},{16,18,28,30},{17,19,29,3..., dimensions={0} | all-to-all | bytes 983040 | tf_op jit(solution)/shard_map/all_to_all | solution.py:377
  80.9 1.2 %final.1 = (bf16[12,48,128]{2,1,0:T(8,128)(2,1)}, bf16[12,48,256]{2,1,0:T(8,128)(2,1)}, f32[4,48,48]{2,1,0:T(8,128)}) custom-call(bf16[4,10,48,128]{3,2,1,0:T(8,128)(2,1)S(1)} %all_to_all.21.got_ref), custom_call_target="tpu_custom_call" | custom-call | tf_op jit(solution)/shard_map/final/pallas_call | solution.py:378
  (2 shorter events, 0.1 us)
Async XLA Ops:
  18.6 11.4 %collective-permute-start.1 = (bf16[7,192,128]{2,1,0:T(8,128)(2,1)S(1)}, bf16[7,192,128]{2,1,0:T(8,128)(2,1)S(1)}, u32[]{:S(2)}, u32[]{:S(2)}) collective-permute-start(bf16[7,192,128]{2,1,0:T(8,128)(2,1)S(1)} %own.1.a0_ref), channel_id=1, source_target_pairs={{0,4},{1,5},{2,6},{3,7},{4,0},{5,1},{6,2},{7,3},{8,12},{9,13},{10,... | collective-permute-start | bytes 1032200 | tf_op jit(solution)/shard_map/ppermute | solution.py:324
  19.6 23.8 %all-to-all-start.1 = ((bf16[16,80,128]{2,1,0:T(8,128)(2,1)}), bf16[16,80,128]{2,1,0:T(8,128)(2,1)S(1)}, u32[]{:S(2)}, u32[]{:S(2)}) async-start(bf16[16,80,128]{2,1,0:T(8,128)(2,1)} %band.1), calls=%async_computation.1 | async-start | bytes 655360 | tf_op jit(solution)/shard_map/all_to_all | solution.py:329
  29.9 1.7 %collective-permute-start = (bf16[7,192,128]{2,1,0:T(8,128)(2,1)S(1)}, bf16[7,192,128]{2,1,0:T(8,128)(2,1)S(1)}, u32[]{:S(2)}, u32[]{:S(2)}) collective-permute-start(bf16[7,192,128]{2,1,0:T(8,128)(2,1)S(1)} %own.1.a0_ref), channel_id=1, source_target_pairs={{0,1},{1,0},{2,3},{3,2},{4,5},{5,4},{6,7},{7,6},{8,9},{9,8},{10,11... | collective-permute-start | bytes 1032200 | tf_op jit(solution)/shard_map/ppermute | solution.py:325
  30.0 2.1 %collective-permute-start.2 = (bf16[7,192,128]{2,1,0:T(8,128)(2,1)S(1)}, bf16[7,192,128]{2,1,0:T(8,128)(2,1)S(1)}, u32[]{:S(2)}, u32[]{:S(2)}) collective-permute-start(bf16[7,192,128]{2,1,0:T(8,128)(2,1)S(1)} %collective-permute-done.1.a2_ref), channel_id=1, source_target_pairs={{0,1},{1,0},{2,3},{3,2},{4,5},{5,4},{6,7},{7,6},{8,9},{9,8},{10,11... | collective-permute-start | bytes 1032200 | tf_op jit(solution)/shard_map/ppermute | solution.py:330
  53.9 16.2 %all-to-all-start.2 = ((bf16[16,80,128]{2,1,0:T(8,128)(2,1)}), bf16[16,80,128]{2,1,0:T(8,128)(2,1)S(1)}, u32[]{:S(2)}, u32[]{:S(2)}) async-start(bf16[16,80,128]{2,1,0:T(8,128)(2,1)} %turn.1), calls=%async_computation.2 | async-start | bytes 655360 | tf_op jit(solution)/shard_map/all_to_all | solution.py:369
  57.5 1.7 %collective-permute-start.3 = (bf16[2,3,192,128]{3,2,1,0:T(8,128)(2,1)S(1)}, bf16[2,3,192,128]{3,2,1,0:T(8,128)(2,1)S(1)}, u32[]{:S(2)}, u32[]{:S(2)}) collective-permute-start(bf16[2,3,192,128]{3,2,1,0:T(8,128)(2,1)S(1)} %get-tuple-element.15), channel_id=1, source_target_pairs={{0,1},{1,0},{2,3},{3,2},{4,5},{5,4},{6,7},{7,6},{8,9},{9,8},{10,11... | collective-permute-start | bytes 884744 | tf_op jit(solution)/shard_map/ppermute | solution.py:355
  59.2 6.0 %collective-permute-start.4 = (bf16[3,192,128]{2,1,0:T(8,128)(2,1)S(1)}, bf16[3,192,128]{2,1,0:T(8,128)(2,1)S(1)}, u32[]{:S(2)}, u32[]{:S(2)}) collective-permute-start(bf16[3,192,128]{2,1,0:T(8,128)(2,1)S(1)} %get-tuple-element.17), channel_id=1, source_target_pairs={{0,4},{1,5},{2,6},{3,7},{4,0},{5,1},{6,2},{7,3},{8,12},{9,13},{10,... | collective-permute-start | bytes 442376 | tf_op jit(solution)/shard_map/ppermute | solution.py:368

commit v3 on v2

--- a/solution.py
+++ b/solution.py
@@ -20,6 +20,10 @@
 
 def flip(bits):
     return [(c, c ^ bits) for c in range(16)]
+
+
+def trade(step):
+    return [(group[p], group[p ^ step]) for group in HEAD_GROUPS for p in range(4)]
 
 
 def call(body, name, out_shape, scratch=(), n_in=1, space=pltpu.VMEM, limit=48 << 20, cost=None):
@@ -41,19 +45,21 @@
 def place():
     c = lax.axis_index("col")
     x = c // 4
-    return c, jnp.bitwise_and(jnp.bitwise_xor(x, x // 2), 1), c % 2
-
-
-def row_of(b, s):
-    _, pair, core = place()
+    pair = jnp.bitwise_and(jnp.bitwise_xor(x, x // 2), 1)
+    return c, pair, c % 2, (x // 2) * 2 + (c // 2) % 2
+
+
+def row_of(b, step):
+    _, pair, core, position = place()
     there = jnp.bitwise_xor(pair, b // 2)
-    x = there if s < 2 else 3 - there
-    return x * 4 + (s % 2) * 2 + jnp.bitwise_xor(core, b % 2)
+    to = jnp.bitwise_xor(position, step)
+    x = jnp.where(to >= 2, 3 - there, there)
+    return x * 4 + (to % 2) * 2 + jnp.bitwise_xor(core, b % 2)
 
 
 def pack_kernel(root, *refs):
-    hbm, (out_ref, rows) = refs[:7], refs[7:9]
-    local, sems = refs[9:16], refs[16]
+    hbm, out_refs, staged, rows = refs[:7], refs[7:11], refs[11], refs[12]
+    local, sems = refs[13:20], refs[20]
     copies = [
         pltpu.make_async_copy(src, dst, sems.at[k])
         for k, (src, dst) in enumerate(zip(hbm, local))
@@ -70,12 +76,14 @@
     count = valid_ref.shape[0]
     valid = jnp.broadcast_to(valid_ref[...].reshape(1, count), (8, count))
     mask = jnp.where(valid == 1, 0.0, -10000.0).astype(F32)
-    back = count - place()[0] * cols
+    c, _, _, position = place()
+    back = count - c * cols
     mask = pltpu.roll(mask, back, 1)[0:1, 0:cols]
     for h in range(heads):
         lo, hi = h * size, (h + 1) * size
+        to = jnp.bitwise_xor(position, h)
         for p in range(pairs):
-            out_ref[h, p] = jnp.concatenate(
+            staged[to, p] = jnp.concatenate(
                 [
                     q_ref[2 * p, :, lo:hi],
                     g_ref[2 * p, :, lo:hi],
@@ -84,7 +92,7 @@
                 ],
                 axis=-1,
             )
-            out_ref[h, pairs + p] = jnp.concatenate(
+            staged[to, pairs + p] = jnp.concatenate(
                 [
                     kv_ref[2 * p, :, lo:hi],
                     kv_ref[2 * p, :, width + lo : width + hi],
@@ -104,17 +112,27 @@
         rows[48 : 48 + n_i, 0:cols] = delta - high
         turned = jnp.transpose(rows[...])[0:cols]
         tile = bias_ref[h].astype(F32) + mask
-        out_ref[h, 2 * pairs] = jnp.concatenate(
+        staged[to, 2 * pairs] = jnp.concatenate(
             [turned[:, 0:64], tile, jnp.zeros((cols, 64 - cols), F32)], axis=-1
         ).astype(BF)
-
-
-def own_kernel(got_ref, a_ref):
-    parts, blocks, cols, _ = got_ref.shape
+    for step in range(heads):
+        out_refs[step][...] = staged[step]
+
+
+def hold_kernel(src_ref, out_ref, sem):
+    copy = pltpu.make_async_copy(src_ref, out_ref, sem)
+    copy.start()
+    copy.wait()
+
+
+def own_kernel(*refs):
+    got, own_ref = refs[0:4], refs[4]
+    blocks, cols, _ = got[0].shape
     pairs = blocks // 2
-    for p in range(pairs):
-        a_ref[p] = got_ref[:, p].reshape(parts * cols, LANES)
-    a_ref[pairs] = got_ref[:, blocks - 1].reshape(parts * cols, LANES)
+    for step in range(4):
+        lo, hi = step * cols, (step + 1) * cols
+        own_ref[0:pairs, lo:hi] = got[step][0:pairs]
+        own_ref[pairs, lo:hi] = got[step][blocks - 1]
 
 
 def fold(tile):
@@ -135,12 +153,13 @@
     return jnp.concatenate([tile[0:48], tail], axis=1)
 
 
-def band_kernel(got_ref, bias_ref):
-    parts, blocks, cols, _ = got_ref.shape
-    pieces = [got_ref[x, blocks - 1, :, 64 : 64 + cols].astype(F32) for x in range(parts)]
-    band = fold(jnp.concatenate(pieces, axis=-1)).astype(BF)
+def band_kernel(*refs):
+    got, bias_ref = refs[0:4], refs[4]
+    blocks, cols, _ = got[0].shape
+    tiles = [one[blocks - 1, :, 64 : 64 + cols].astype(F32) for one in got]
+    band = fold(jnp.concatenate(tiles, axis=-1))
     for r in range(bias_ref.shape[0]):
-        bias_ref[r] = band
+        bias_ref[r] = band.astype(BF)
 
 
 def join_kernel(a0_ref, a1_ref, a2_ref, a3_ref, out_ref):
@@ -149,28 +168,18 @@
         out_ref[:, b * keys : (b + 1) * keys] = a[...]
 
 
-def main_kernel(
-    inv_root,
-    got_ref,
-    a_ref,
-    bias_ref,
-    dq0_ref,
-    dq2_ref,
-    dqc_ref,
-    dkv_ref,
-    acc,
-    rows,
-    bias_t,
-    dq_t,
-):
-    parts, blocks, cols, _ = got_ref.shape
+def main_kernel(inv_root, *refs):
+    ab_refs, a_ref, bias_ref = refs[0:4], refs[4], refs[5]
+    dq0_ref, dq2_ref, dqc_ref, dkv_ref, dbias_ref = refs[6:11]
+    rows, bias_t, acc, dq_t = refs[11:]
+    blocks, cols, _ = ab_refs[0].shape
+    parts = len(ab_refs)
     pairs = blocks // 2
     keys = parts * cols
     total = 4 * keys
     size = 32
     log2e = math.log2(math.e)
     dq_refs = (dq0_ref, dqc_ref.at[0], dq2_ref, dqc_ref.at[1])
-
     for b in range(4):
         for x in range(parts):
             at = b * keys + x * cols
@@ -184,11 +193,10 @@
     quarter = lax.broadcasted_iota(jnp.int32, (total, LANES), 1) // size
     extra = a_ref[pairs]
     scale_row = jnp.where((lane // size) % 2 == 0, inv_root, 1.0)
-    chunk = 256
     for p in range(pairs):
         qp = a_ref[p]
         qx = jnp.concatenate([qp, extra], axis=1)
-        kp = got_ref[:, pairs + p].reshape(keys, LANES)
+        kp = jnp.concatenate([ab[pairs + p] for ab in ab_refs], axis=0)
         kt = jnp.transpose(kp.astype(F32)).astype(BF)
         zero = jnp.zeros_like(kp)
         left = []
@@ -199,42 +207,36 @@
             left.append(
                 jnp.concatenate([jnp.where(lane // size == s, kp, zero), ones], axis=1)
             )
-        qm = [jnp.where(quarter == s, qp, jnp.zeros_like(qp)) for s in range(4)]
+        low = []
+        for e in range(2):
+            both = lax.dot_general(
+                jnp.concatenate(left[2 * e : 2 * e + 2], axis=0),
+                qx,
+                (((1,), (1,)), ((), ())),
+                preferred_element_type=F32,
+            )
+            probs = jnp.exp2(both[0:keys] * (inv_root * log2e) + bias_t[...])
+            ds = probs * both[keys:]
+            acc[...] += ds
+            low += [ds.astype(BF), probs.astype(BF)]
+            i = 2 * p + e
+            dq_t[i * size : (i + 1) * size] = jnp.dot(
+                kt[2 * e * size : (2 * e + 1) * size], low[2 * e], preferred_element_type=F32
+            )
         out = jnp.zeros((keys, LANES), F32)
-        for t in range(0, total, chunk):
-            here = qx[t : t + chunk]
-            for e in range(2):
-                scores = lax.dot_general(
-                    left[2 * e], here, (((1,), (1,)), ((), ())), preferred_element_type=F32
-                )
-                grads = lax.dot_general(
-                    left[2 * e + 1], here, (((1,), (1,)), ((), ())), preferred_element_type=F32
-                )
-                probs = jnp.exp2(scores * (inv_root * log2e) + bias_t[:, t : t + chunk])
-                ds = probs * grads
-                acc[:, t : t + chunk] += ds
-                ds_low = ds.astype(BF)
-                out += jnp.dot(ds_low, qm[2 * e][t : t + chunk], preferred_element_type=F32)
-                out += jnp.dot(
-                    probs.astype(BF), qm[2 * e + 1][t : t + chunk], preferred_element_type=F32
-                )
-                i = 2 * p + e
-                dq_t[i * size : (i + 1) * size, t : t + chunk] = jnp.dot(
-                    kt[2 * e * size : (2 * e + 1) * size], ds_low, preferred_element_type=F32
-                )
+        for s in range(4):
+            out += jnp.dot(
+                low[s], jnp.where(quarter == s, qp, jnp.zeros_like(qp)), preferred_element_type=F32
+            )
         dkv_ref[p] = (out * scale_row).astype(BF)
     for quad in range(2 * pairs // 4):
         turned = jnp.transpose(dq_t[quad * LANES : (quad + 1) * LANES]) * inv_root
         for b in range(4):
             dq_refs[b][quad] = turned[b * keys : (b + 1) * keys].astype(BF)
-
-
-def turn_kernel(cols, acc, dbias_ref, rows):
-    keys, total = acc.shape
     for t in range(0, total, LANES):
         rows[t : t + LANES, 0:keys] = jnp.transpose(acc[:, t : t + LANES])
     for b in range(4):
-        for x in range(keys // cols):
+        for x in range(parts):
             at = b * keys + x * cols
             dbias_ref[row_of(b, x)] = fold(rows[at : at + cols]).astype(BF)
 
@@ -256,8 +258,10 @@
     for r in range(1, db_ref.shape[0]):
         bias = bias + db_ref[r].astype(F32)
     bias = unfold(bias)
-    for x in range(parts):
-        lo, hi = x * cols, (x + 1) * cols
+    position = place()[3]
+    for step in range(parts):
+        x = jnp.bitwise_xor(position, step)
+        lo, hi = step * cols, (step + 1) * cols
         for quad in range(quads):
             out_ref[x, quad] = total[quad, lo:hi]
         for p in range(pairs):
@@ -294,8 +298,7 @@
     pairs = n_i // 2
     quads = n_i // 4
     n_rows = lax.axis_size("row")
-    parts = heads
-    keys = parts * cols
+    keys = heads * cols
     wide = 2 * LANES
     struct = jax.ShapeDtypeStruct
     inputs = (
@@ -308,24 +311,37 @@
         token_valid,
     )
 
-    packed = call(
+    def traded(blocks):
+        return [blocks[0]] + [lax.ppermute(blocks[k], "col", trade(k)) for k in (1, 2, 3)]
+
+    sent = call(
         functools.partial(pack_kernel, math.sqrt(size)),
         "pack",
-        struct((heads, 2 * pairs + 1, cols, LANES), BF),
-        scratch=[pltpu.VMEM((64, LANES), F32)]
+        (struct((2 * pairs + 1, cols, LANES), BF),) * 4,
+        scratch=[
+            pltpu.VMEM((heads, 2 * pairs + 1, cols, LANES), BF),
+            pltpu.VMEM((64, LANES), F32),
+        ]
         + [pltpu.VMEM(v.shape, v.dtype) for v in inputs]
         + [pltpu.SemaphoreType.DMA((len(inputs),))],
         n_in=len(inputs),
         space=pltpu.HBM,
         limit=62 << 20,
     )(*inputs)
-    got = lax.all_to_all(packed, "col", 0, 0, tiled=True, axis_index_groups=HEAD_GROUPS)
-    own = call(own_kernel, "own", struct((pairs + 1, keys, LANES), BF))(got)
+    held = call(
+        hold_kernel,
+        "hold",
+        struct(sent[0].shape, BF),
+        scratch=[pltpu.SemaphoreType.DMA],
+        space=pltpu.HBM,
+    )(sent[0])
+    blocks = [held] + traded(sent)[1:]
+    own = call(own_kernel, "own", struct((pairs + 1, keys, LANES), BF), n_in=4)(*blocks)
     over_x = lax.ppermute(own, "col", flip(4))
     over_core = lax.ppermute(own, "col", flip(1))
     folded = struct((n_rows, 80, LANES), BF)
     dq_block = struct((quads, keys, LANES), BF)
-    band = call(band_kernel, "band", folded)(got)
+    band = call(band_kernel, "band", folded, n_in=4)(*blocks)
     bias_rows = lax.all_to_all(band, "row", 0, 0, tiled=True)
     over_both = lax.ppermute(over_x, "col", flip(1))
     joined = call(
@@ -335,7 +351,7 @@
         n_in=4,
         cost=JOIN_COST,
     )(own, over_core, over_x, over_both)
-    dq0, dq2, dq_core, dkv, acc = call(
+    dq0, dq2, dq_core, dkv, dbias = call(
         functools.partial(main_kernel, size**-0.5),
         "main",
         (
@@ -343,22 +359,17 @@
             dq_block,
             struct((2, quads, keys, LANES), BF),
             struct((pairs, keys, LANES), BF),
-            struct((keys, 4 * keys), F32),
+            folded,
         ),
         scratch=[
             pltpu.VMEM((4 * keys, wide), F32),
             pltpu.VMEM((keys, 4 * keys), F32),
+            pltpu.VMEM((keys, 4 * keys), F32),
             pltpu.VMEM((n_i * size, 4 * keys), F32),
         ],
-        n_in=3,
-    )(got, joined, bias_rows)
+        n_in=6,
+    )(*blocks, joined, bias_rows)
     over_core = lax.ppermute(dq_core, "col", flip(1))
-    dbias = call(
-        functools.partial(turn_kernel, cols),
-        "turn",
-        folded,
-        scratch=[pltpu.VMEM((4 * keys, wide), F32)],
-    )(acc)
     keep, send = call(
         fold_core_kernel,
         "fold_core",
@@ -371,7 +382,7 @@
     merged = call(
         merge_kernel,
         "merge",
-        struct((parts, quads + pairs + 1, cols, LANES), BF),
+        struct((heads, quads + pairs + 1, cols, LANES), BF),
         n_in=3,
     )(total, dkv, parts_in)
     back = lax.all_to_all(merged, "col", 0, 0, tiled=True, axis_index_groups=HEAD_GROUPS)

time: 82.4 us -> 77 us (0.934)
  blocking collectives: 25.9 us -> 12.3 us
  waiting for transfers between devices: 23.5 us -> 29.8 us
  starting transfers between devices: 16.4 us -> 20.9 us
  Pallas kernels: 15.5 us -> 12.1 us
  local copies, waits for them, and re-layouts: 0 us -> 0.91 us
    all_to_all x1 -> x0, blocking collectives: 15.4 us -> none  [on_device(): lax.all_to_all(packed, 'col', 0, 0, tiled=True, axis_index_groups=HEAD_GR...]
    ppermute x0 -> x3, waiting for transfers between devices: none -> 6.16 us  [traded(): lax.ppermute(blocks[k], 'col', trade(k))]
    ppermute x0 -> x3, starting transfers between devices: none -> 4.79 us  [traded(): lax.ppermute(blocks[k], 'col', trade(k))]
    pallas_call x1, Pallas kernels: 9.39 us -> 6.85 us  [on_device(): call(functools.partial(main_kernel, size ** (-0.5)), 'main', (dq_block, d...]
    all_to_all x1, blocking collectives: 10.6 us -> 12.3 us  [on_device(): lax.all_to_all(merged, 'col', 0, 0, tiled=True, axis_index_groups=HEAD_GR...]
    unnamed x0 -> x2, local copies, waits for them, and re-layouts: none -> 0.91 us
    pallas_call x5, Pallas kernels: 4.77 us -> 3.87 us  [the longest x1 2.62 us: on_device(): call(functools.partial(pack_kernel, math.sqrt(size)), 'pack', (struct((2...]
  transfers between devices with their start and end apart: 7 -> 10, of which waited for: 6 -> 8; matrix products, arithmetic and copies ran while one was open for 0% -> 0% of each run, Pallas kernels for 1% -> 2%
where the time goes in v3:
time: 77 us; the launch traced here: 76.6 us
  waiting for transfers between devices  29.8 us (39%)
  starting transfers between devices  20.9 us (27%)
  blocking collectives  12.3 us (16%)
  Pallas kernels  12.1 us (16%)
  local copies, waits for them, and re-layouts  0.91 us (1%)
    all_to_all x1, blocking collectives, on_device(): lax.all_to_all(merged, 'col', 0, 0, tiled=True, axis_index_groups=HEAD_GR...  12.3 us
    all_to_all x1, waiting for transfers between devices, on_device(): bias_rows = lax.all_to_all(band, 'row', 0, 0, tiled=True)  11.4 us
    all_to_all x1, starting transfers between devices, on_device(): bias_rows = lax.all_to_all(band, 'row', 0, 0, tiled=True)  10.2 us
    pallas_call x1, Pallas kernels, on_device(): call(functools.partial(main_kernel, size ** (-0.5)), 'main', (dq_block, d...  6.85 us
    ppermute x3, waiting for transfers between devices, traded(): lax.ppermute(blocks[k], 'col', trade(k))  6.16 us
    ppermute x3, starting transfers between devices, traded(): lax.ppermute(blocks[k], 'col', trade(k))  4.79 us
    all_to_all x1, waiting for transfers between devices, on_device(): parts_in = lax.all_to_all(dbias, 'row', 0, 0, tiled=True)  4.61 us
    ppermute x1, waiting for transfers between devices, on_device(): over_x = lax.ppermute(send, 'col', flip(4))  4.4 us
  transfers between devices with their start and end apart: 10, of which 8 were waited for; matrix products, arithmetic and copies ran while one was open for 0% of the time, Pallas kernels for 2%

profile of v3, /device:TPU:32, one launch (start us, length us, event | category | flops | bytes accessed | tf_op | source)
XLA Modules:
  0.0 76.6 jit_solution(4280130402276951213)
XLA Ops:
  0.6 2.6 %pack.1 = (bf16[13,48,128]{2,1,0:T(8,128)(2,1)}, bf16[13,48,128]{2,1,0:T(8,128)(2,1)}, bf16[13,48,128]{2,1,0:T(8,128)(2,1)}, bf16[13,48,128]{2,1,0:T(8,128)(2,1)}) custom-call(bf16[12,48,128]{2,1,0:T(8,128)(2,1)} %refs_0_.1, bf16[12,48,256]{2,1,0:T(8,128)(2,1)} %refs_1_.1, bf16[12,48,128]{2,1,0:T(8,128)(2,1)} %refs_2_.1, bf16[4,48,48]{2,1,0:T(8,128)(2,1)} %refs_3_.1, ...), custom_call_target="tpu_custom_call" | custom-call | tf_op jit(solution)/shard_map/pack/pallas_call | solution.py:317
  3.3 1.9 %collective-permute-start = (bf16[13,48,128]{2,1,0:T(8,128)(2,1)}, bf16[13,48,128]{2,1,0:T(8,128)(2,1)S(1)}, u32[]{:S(2)}, u32[]{:S(2)}) collective-permute-start(bf16[13,48,128]{2,1,0:T(8,128)(2,1)} %get-tuple-element.18), channel_id=1, source_target_pairs={{0,2},{2,0},{12,14},{14,12},{1,3},{3,1},{13,15},{15,13},{4,6},{6,4... | collective-permute-start | bytes 479240 | tf_op jit(solution)/shard_map/ppermute | solution.py:315
  5.2 1.0 %collective-permute-start.1 = (bf16[13,48,128]{2,1,0:T(8,128)(2,1)}, bf16[13,48,128]{2,1,0:T(8,128)(2,1)S(1)}, u32[]{:S(2)}, u32[]{:S(2)}) collective-permute-start(bf16[13,48,128]{2,1,0:T(8,128)(2,1)} %get-tuple-element.19), channel_id=1, source_target_pairs={{0,12},{2,14},{12,0},{14,2},{1,13},{3,15},{13,1},{15,3},{4,8},{6,1... | collective-permute-start | bytes 479240 | tf_op jit(solution)/shard_map/ppermute | solution.py:315
  6.2 1.8 %collective-permute-start.2 = (bf16[13,48,128]{2,1,0:T(8,128)(2,1)}, bf16[13,48,128]{2,1,0:T(8,128)(2,1)S(1)}, u32[]{:S(2)}, u32[]{:S(2)}) collective-permute-start(bf16[13,48,128]{2,1,0:T(8,128)(2,1)} %get-tuple-element.20), channel_id=1, source_target_pairs={{0,14},{2,12},{12,2},{14,0},{1,15},{3,13},{13,3},{15,1},{4,10},{6,... | collective-permute-start | bytes 479240 | tf_op jit(solution)/shard_map/ppermute | solution.py:315
  8.0 0.0 copy-start
  8.1 0.9 %copy-done = bf16[13,48,128]{2,1,0:T(8,128)(2,1)S(1)} copy-done((bf16[13,48,128]{2,1,0:T(8,128)(2,1)S(1)}, bf16[13,48,128]{2,1,0:T(8,128)(2,1)}, u32[]{:S(2)}) %copy-start) | copy-done | bytes 159768
  9.0 0.2 hold.1.refs_0_
  9.2 1.1 %collective-permute-done.refs_1_ = bf16[13,48,128]{2,1,0:T(8,128)(2,1)S(1)} collective-permute-done((bf16[13,48,128]{2,1,0:T(8,128)(2,1)}, bf16[13,48,128]{2,1,0:T(8,128)(2,1)S(1)}, u32[]{:S(2)}, u32[]{:S(2)}) %collective-permute-start) | collective-permute-done | bytes 159776 | tf_op jit(solution)/shard_map/ppermute | solution.py:315
  10.3 5.0 %collective-permute-done.1.refs_2_ = bf16[13,48,128]{2,1,0:T(8,128)(2,1)S(1)} collective-permute-done((bf16[13,48,128]{2,1,0:T(8,128)(2,1)}, bf16[13,48,128]{2,1,0:T(8,128)(2,1)S(1)}, u32[]{:S(2)}, u32[]{:S(2)}) %collective-permute-start.1) | collective-permute-done | bytes 159776 | tf_op jit(solution)/shard_map/ppermute | solution.py:315
  15.3 0.0 collective-permute-done.2.refs_3_
  15.3 0.1 collective-permute-start.4
  15.4 0.9 %band.1 = bf16[16,80,128]{2,1,0:T(8,128)(2,1)} custom-call(bf16[13,48,128]{2,1,0:T(8,128)(2,1)S(1)} %hold.1.refs_0_, bf16[13,48,128]{2,1,0:T(8,128)(2,1)S(1)} %collective-permute-done.refs_1_, bf16[13,48,128]{2,1,0:T(8,128)(2,1)S(1)} %collective-permute-done.1.refs_2_, bf16[13,48,128]{2,1,0:T(8,128)(2,1)S(1)} %collective-permute-done.2.refs_3_), custom_call_target="tpu_custom_call" | custom-call | tf_op jit(solution)/shard_map/band/pallas_call | solution.py:344
  16.3 10.2 %all-to-all-start = ((bf16[16,80,128]{2,1,0:T(8,128)(2,1)}), bf16[16,80,128]{2,1,0:T(8,128)(2,1)S(1)}, u32[]{:S(2)}, u32[]{:S(2)}) async-start(bf16[16,80,128]{2,1,0:T(8,128)(2,1)} %band.1), calls=%async_computation | async-start | bytes 655360 | tf_op jit(solution)/shard_map/all_to_all | solution.py:345
  26.5 0.1 collective-permute-start.3
  26.6 0.0 collective-permute-done.4.a2_ref
  26.7 0.5 collective-permute-start.5
  27.2 1.1 %collective-permute-done.3.a1_ref = bf16[7,192,128]{2,1,0:T(8,128)(2,1)S(1)} collective-permute-done((bf16[7,192,128]{2,1,0:T(8,128)(2,1)S(1)}, bf16[7,192,128]{2,1,0:T(8,128)(2,1)S(1)}, u32[]{:S(2)}, u32[]{:S(2)}) %collective-permute-start.3) | collective-permute-done | bytes 344096 | tf_op jit(solution)/shard_map/ppermute | solution.py:341
  28.3 0.5 collective-permute-done.5.a3_ref
  28.8 0.1 join.1.refs_4_
  28.9 11.4 %all-to-all-done.refs_5_ = bf16[16,80,128]{2,1,0:T(8,128)(2,1)S(1)} async-done(((bf16[16,80,128]{2,1,0:T(8,128)(2,1)}), bf16[16,80,128]{2,1,0:T(8,128)(2,1)S(1)}, u32[]{:S(2)}, u32[]{:S(2)}) %all-to-all-start) | async-done | bytes 327712 | tf_op jit(solution)/shard_map/all_to_all | solution.py:345
  40.2 6.9 %main.1 = (bf16[3,192,128]{2,1,0:T(8,128)(2,1)S(1)}, bf16[3,192,128]{2,1,0:T(8,128)(2,1)S(1)}, bf16[2,3,192,128]{3,2,1,0:T(8,128)(2,1)S(1)}, bf16[6,192,128]{2,1,0:T(8,128)(2,1)S(1)}, bf16[16,80,128]{2,1,0:T(8,128)(2,1)}) custom-call(bf16[13,48,128]{2,1,0:T(8,128)(2,1)S(1)} %hold.1.refs_0_, bf16[13,48,128]{2,1,0:T(8,128)(2,1)S(1)} %collective-permute-done.refs_1_, ...), custom_call_target="tpu_custom_call" | custom-call | tf_op jit(solution)/shard_map/main/pallas_call | solution.py:354
  47.1 3.5 %all-to-all-start.1 = ((bf16[16,80,128]{2,1,0:T(8,128)(2,1)}), bf16[16,80,128]{2,1,0:T(8,128)(2,1)S(1)}, u32[]{:S(2)}, u32[]{:S(2)}) async-start(bf16[16,80,128]{2,1,0:T(8,128)(2,1)} %get-tuple-element.27), calls=%async_computation.1 | async-start | bytes 655360 | tf_op jit(solution)/shard_map/all_to_all | solution.py:380
  50.6 0.1 collective-permute-start.6
  50.7 1.6 %collective-permute-done.6.got_ref = bf16[2,3,192,128]{3,2,1,0:T(8,128)(2,1)S(1)} collective-permute-done((bf16[2,3,192,128]{3,2,1,0:T(8,128)(2,1)S(1)}, bf16[2,3,192,128]{3,2,1,0:T(8,128)(2,1)S(1)}, u32[]{:S(2)}, u32[]{:S(2)}) %collective-permute-start.6) | collective-permute-done | bytes 294944 | tf_op jit(solution)/shard_map/ppermute | solution.py:372
  52.3 0.1 fold_core.1
  52.4 1.6 %collective-permute-start.7 = (bf16[3,192,128]{2,1,0:T(8,128)(2,1)S(1)}, bf16[3,192,128]{2,1,0:T(8,128)(2,1)S(1)}, u32[]{:S(2)}, u32[]{:S(2)}) collective-permute-start(bf16[3,192,128]{2,1,0:T(8,128)(2,1)S(1)} %get-tuple-element.25), channel_id=1, source_target_pairs={{0,4},{1,5},{2,6},{3,7},{4,0},{5,1},{6,2},{7,3},{8,12},{9,13},{10,... | collective-permute-start | bytes 442376 | tf_op jit(solution)/shard_map/ppermute | solution.py:379
  54.0 4.4 %collective-permute-done.7.got_ref = bf16[3,192,128]{2,1,0:T(8,128)(2,1)S(1)} collective-permute-done((bf16[3,192,128]{2,1,0:T(8,128)(2,1)S(1)}, bf16[3,192,128]{2,1,0:T(8,128)(2,1)S(1)}, u32[]{:S(2)}, u32[]{:S(2)}) %collective-permute-start.7) | collective-permute-done | bytes 147488 | tf_op jit(solution)/shard_map/ppermute | solution.py:379
  58.4 4.6 %all-to-all-done.1.db_ref = bf16[16,80,128]{2,1,0:T(8,128)(2,1)S(1)} async-done(((bf16[16,80,128]{2,1,0:T(8,128)(2,1)}), bf16[16,80,128]{2,1,0:T(8,128)(2,1)S(1)}, u32[]{:S(2)}, u32[]{:S(2)}) %all-to-all-start.1) | async-done | bytes 327712 | tf_op jit(solution)/shard_map/all_to_all | solution.py:380
  63.0 0.2 merge.1
  63.2 12.3 %all_to_all.15.got_ref = bf16[4,10,48,128]{3,2,1,0:T(8,128)(2,1)S(1)} all-to-all(bf16[4,10,48,128]{3,2,1,0:T(8,128)(2,1)S(1)} %merge.1), channel_id=1, replica_groups={{0,2,12,14},{1,3,13,15},{4,6,8,10},{5,7,9,11},{16,18,28,30},{17,19,29,3..., dimensions={0} | all-to-all | bytes 983040 | tf_op jit(solution)/shard_map/all_to_all | solution.py:388
  75.4 1.2 %final.1 = (bf16[12,48,128]{2,1,0:T(8,128)(2,1)}, bf16[12,48,256]{2,1,0:T(8,128)(2,1)}, f32[4,48,48]{2,1,0:T(8,128)}) custom-call(bf16[4,10,48,128]{3,2,1,0:T(8,128)(2,1)S(1)} %all_to_all.15.got_ref), custom_call_target="tpu_custom_call" | custom-call | tf_op jit(solution)/shard_map/final/pallas_call | solution.py:389
  (2 shorter events, 0.1 us)
Async XLA Ops:
  3.3 7.0 %collective-permute-start = (bf16[13,48,128]{2,1,0:T(8,128)(2,1)}, bf16[13,48,128]{2,1,0:T(8,128)(2,1)S(1)}, u32[]{:S(2)}, u32[]{:S(2)}) collective-permute-start(bf16[13,48,128]{2,1,0:T(8,128)(2,1)} %get-tuple-element.18), channel_id=1, source_target_pairs={{0,2},{2,0},{12,14},{14,12},{1,3},{3,1},{13,15},{15,13},{4,6},{6,4... | collective-permute-start | bytes 479240 | tf_op jit(solution)/shard_map/ppermute | solution.py:315
  5.2 10.1 %collective-permute-start.1 = (bf16[13,48,128]{2,1,0:T(8,128)(2,1)}, bf16[13,48,128]{2,1,0:T(8,128)(2,1)S(1)}, u32[]{:S(2)}, u32[]{:S(2)}) collective-permute-start(bf16[13,48,128]{2,1,0:T(8,128)(2,1)} %get-tuple-element.19), channel_id=1, source_target_pairs={{0,12},{2,14},{12,0},{14,2},{1,13},{3,15},{13,1},{15,3},{4,8},{6,1... | collective-permute-start | bytes 479240 | tf_op jit(solution)/shard_map/ppermute | solution.py:315
  6.2 9.1 %collective-permute-start.2 = (bf16[13,48,128]{2,1,0:T(8,128)(2,1)}, bf16[13,48,128]{2,1,0:T(8,128)(2,1)S(1)}, u32[]{:S(2)}, u32[]{:S(2)}) collective-permute-start(bf16[13,48,128]{2,1,0:T(8,128)(2,1)} %get-tuple-element.20), channel_id=1, source_target_pairs={{0,14},{2,12},{12,2},{14,0},{1,15},{3,13},{13,3},{15,1},{4,10},{6,... | collective-permute-start | bytes 479240 | tf_op jit(solution)/shard_map/ppermute | solution.py:315
  8.0 0.9 %copy-start = (bf16[13,48,128]{2,1,0:T(8,128)(2,1)S(1)}, bf16[13,48,128]{2,1,0:T(8,128)(2,1)}, u32[]{:S(2)}) copy-start(bf16[13,48,128]{2,1,0:T(8,128)(2,1)} %get-tuple-element.17.src_ref) | copy-start | bytes 479236
  15.3 11.3 %collective-permute-start.4 = (bf16[7,192,128]{2,1,0:T(8,128)(2,1)S(1)}, bf16[7,192,128]{2,1,0:T(8,128)(2,1)S(1)}, u32[]{:S(2)}, u32[]{:S(2)}) collective-permute-start(bf16[7,192,128]{2,1,0:T(8,128)(2,1)S(1)} %own.1.a0_ref), channel_id=1, source_target_pairs={{0,4},{1,5},{2,6},{3,7},{4,0},{5,1},{6,2},{7,3},{8,12},{9,13},{10,... | collective-permute-start | bytes 1032200 | tf_op jit(solution)/shard_map/ppermute | solution.py:340
  16.3 23.9 %all-to-all-start = ((bf16[16,80,128]{2,1,0:T(8,128)(2,1)}), bf16[16,80,128]{2,1,0:T(8,128)(2,1)S(1)}, u32[]{:S(2)}, u32[]{:S(2)}) async-start(bf16[16,80,128]{2,1,0:T(8,128)(2,1)} %band.1), calls=%async_computation | async-start | bytes 655360 | tf_op jit(solution)/shard_map/all_to_all | solution.py:345
  26.5 1.7 %collective-permute-start.3 = (bf16[7,192,128]{2,1,0:T(8,128)(2,1)S(1)}, bf16[7,192,128]{2,1,0:T(8,128)(2,1)S(1)}, u32[]{:S(2)}, u32[]{:S(2)}) collective-permute-start(bf16[7,192,128]{2,1,0:T(8,128)(2,1)S(1)} %own.1.a0_ref), channel_id=1, source_target_pairs={{0,1},{1,0},{2,3},{3,2},{4,5},{5,4},{6,7},{7,6},{8,9},{9,8},{10,11... | collective-permute-start | bytes 1032200 | tf_op jit(solution)/shard_map/ppermute | solution.py:341
  26.7 2.1 %collective-permute-start.5 = (bf16[7,192,128]{2,1,0:T(8,128)(2,1)S(1)}, bf16[7,192,128]{2,1,0:T(8,128)(2,1)S(1)}, u32[]{:S(2)}, u32[]{:S(2)}) collective-permute-start(bf16[7,192,128]{2,1,0:T(8,128)(2,1)S(1)} %collective-permute-done.4.a2_ref), channel_id=1, source_target_pairs={{0,1},{1,0},{2,3},{3,2},{4,5},{5,4},{6,7},{7,6},{8,9},{9,8},{10,11... | collective-permute-start | bytes 1032200 | tf_op jit(solution)/shard_map/ppermute | solution.py:346
  47.1 15.9 %all-to-all-start.1 = ((bf16[16,80,128]{2,1,0:T(8,128)(2,1)}), bf16[16,80,128]{2,1,0:T(8,128)(2,1)S(1)}, u32[]{:S(2)}, u32[]{:S(2)}) async-start(bf16[16,80,128]{2,1,0:T(8,128)(2,1)} %get-tuple-element.27), calls=%async_computation.1 | async-start | bytes 655360 | tf_op jit(solution)/shard_map/all_to_all | solution.py:380
  50.6 1.7 %collective-permute-start.6 = (bf16[2,3,192,128]{3,2,1,0:T(8,128)(2,1)S(1)}, bf16[2,3,192,128]{3,2,1,0:T(8,128)(2,1)S(1)}, u32[]{:S(2)}, u32[]{:S(2)}) collective-permute-start(bf16[2,3,192,128]{3,2,1,0:T(8,128)(2,1)S(1)} %get-tuple-element.23), channel_id=1, source_target_pairs={{0,1},{1,0},{2,3},{3,2},{4,5},{5,4},{6,7},{7,6},{8,9},{9,8},{10,11... | collective-permute-start | bytes 884744 | tf_op jit(solution)/shard_map/ppermute | solution.py:372
  52.4 6.0 %collective-permute-start.7 = (bf16[3,192,128]{2,1,0:T(8,128)(2,1)S(1)}, bf16[3,192,128]{2,1,0:T(8,128)(2,1)S(1)}, u32[]{:S(2)}, u32[]{:S(2)}) collective-permute-start(bf16[3,192,128]{2,1,0:T(8,128)(2,1)S(1)} %get-tuple-element.25), channel_id=1, source_target_pairs={{0,4},{1,5},{2,6},{3,7},{4,0},{5,1},{6,2},{7,3},{8,12},{9,13},{10,... | collective-permute-start | bytes 442376 | tf_op jit(solution)/shard_map/ppermute | solution.py:379

commit v4 on v3

--- a/solution.py
+++ b/solution.py
@@ -170,8 +170,9 @@
 
 def main_kernel(inv_root, *refs):
     ab_refs, a_ref, bias_ref = refs[0:4], refs[4], refs[5]
-    dq0_ref, dq2_ref, dqc_ref, dkv_ref, dbias_ref = refs[6:11]
-    rows, bias_t, acc, dq_t = refs[11:]
+    dq0_ref, dq2_ref, dqc_ref = refs[6:9]
+    dkv_refs, dbias_ref = refs[9:13], refs[13]
+    rows, bias_t, acc, dq_t = refs[14:]
     blocks, cols, _ = ab_refs[0].shape
     parts = len(ab_refs)
     pairs = blocks // 2
@@ -228,7 +229,9 @@
             out += jnp.dot(
                 low[s], jnp.where(quarter == s, qp, jnp.zeros_like(qp)), preferred_element_type=F32
             )
-        dkv_ref[p] = (out * scale_row).astype(BF)
+        out = (out * scale_row).astype(BF)
+        for step in range(parts):
+            dkv_refs[step][p] = out[step * cols : (step + 1) * cols]
     for quad in range(2 * pairs // 4):
         turned = jnp.transpose(dq_t[quad * LANES : (quad + 1) * LANES]) * inv_root
         for b in range(4):
@@ -250,45 +253,46 @@
     out_ref[...] = (keep_ref[...] + got_ref[...].astype(F32)).astype(BF)
 
 
-def merge_kernel(total, dkv_ref, db_ref, out_ref):
-    parts, _, cols, _ = out_ref.shape
+def merge_kernel(total, db_ref, *out_refs):
     quads = total.shape[0]
-    pairs = dkv_ref.shape[0]
+    cols = out_refs[0].shape[1]
     bias = db_ref[0].astype(F32)
     for r in range(1, db_ref.shape[0]):
         bias = bias + db_ref[r].astype(F32)
     bias = unfold(bias)
-    position = place()[3]
-    for step in range(parts):
-        x = jnp.bitwise_xor(position, step)
+    for step, out_ref in enumerate(out_refs):
         lo, hi = step * cols, (step + 1) * cols
-        for quad in range(quads):
-            out_ref[x, quad] = total[quad, lo:hi]
-        for p in range(pairs):
-            out_ref[x, quads + p] = dkv_ref[p, lo:hi]
-        out_ref[x, quads + pairs] = jnp.concatenate(
+        out_ref[0:quads] = total[:, lo:hi]
+        out_ref[quads] = jnp.concatenate(
             [bias[:, lo:hi], jnp.zeros((cols, LANES - cols), F32)], axis=-1
         ).astype(BF)
 
 
-def final_kernel(got_ref, dq_ref, dkv_ref, db_ref):
-    heads, blocks, cols, _ = got_ref.shape
+def final_kernel(*refs):
+    f_refs, kv_refs = refs[0:4], refs[4:8]
+    dq_ref, dkv_ref, db_ref, f_all, kv_all = refs[8:]
+    heads, cols = len(f_refs), dq_ref.shape[1]
     size = 32
     n_i = dq_ref.shape[0]
     quads = n_i // 4
+    position = place()[3]
+    for step in range(heads):
+        h = jnp.bitwise_xor(position, step)
+        f_all[h] = f_refs[step][...]
+        kv_all[h] = kv_refs[step][...]
     for i in range(n_i):
         at = (i % 4) * size
         dq_ref[i] = jnp.concatenate(
-            [got_ref[h, i // 4, :, at : at + size] for h in range(heads)], axis=-1
+            [f_all[h, i // 4, :, at : at + size] for h in range(heads)], axis=-1
         )
         at = (i % 2) * 2 * size
         dkv_ref[i] = jnp.concatenate(
-            [got_ref[h, quads + i // 2, :, at : at + size] for h in range(heads)]
-            + [got_ref[h, quads + i // 2, :, at + size : at + 2 * size] for h in range(heads)],
+            [kv_all[h, i // 2, :, at : at + size] for h in range(heads)]
+            + [kv_all[h, i // 2, :, at + size : at + 2 * size] for h in range(heads)],
             axis=-1,
         )
     for h in range(heads):
-        db_ref[h] = got_ref[h, blocks - 1, :, 0:cols].astype(F32)
+        db_ref[h] = f_all[h, quads, :, 0:cols].astype(F32)
 
 
 def on_device(queries, keys_values, out_grad, pair_bias, log_norm, delta_rows, token_valid):
@@ -351,16 +355,16 @@
         n_in=4,
         cost=JOIN_COST,
     )(own, over_core, over_x, over_both)
-    dq0, dq2, dq_core, dkv, dbias = call(
+    dq0, dq2, dq_core, *dkv, dbias = call(
         functools.partial(main_kernel, size**-0.5),
         "main",
         (
             dq_block,
             dq_block,
             struct((2, quads, keys, LANES), BF),
-            struct((pairs, keys, LANES), BF),
-            folded,
-        ),
+        )
+        + (struct((pairs, cols, LANES), BF),) * 4
+        + (folded,),
         scratch=[
             pltpu.VMEM((4 * keys, wide), F32),
             pltpu.VMEM((keys, 4 * keys), F32),
@@ -382,10 +386,9 @@
     merged = call(
         merge_kernel,
         "merge",
-        struct((heads, quads + pairs + 1, cols, LANES), BF),
-        n_in=3,
-    )(total, dkv, parts_in)
-    back = lax.all_to_all(merged, "col", 0, 0, tiled=True, axis_index_groups=HEAD_GROUPS)
+        (struct((quads + 1, cols, LANES), BF),) * 4,
+        n_in=2,
+    )(total, parts_in)
     query_grad, kv_grad, bias_grad = call(
         final_kernel,
         "final",
@@ -394,7 +397,12 @@
             struct((n_i, cols, 2 * width), BF),
             struct((heads, cols, cols), F32),
         ),
-    )(back)
+        scratch=[
+            pltpu.VMEM((heads, quads + 1, cols, LANES), BF),
+            pltpu.VMEM((heads, pairs, cols, LANES), BF),
+        ],
+        n_in=8,
+    )(*traded(merged), *traded(dkv))
     kv_grad = jnp.transpose(kv_grad, (1, 0, 2))
     return query_grad, kv_grad, bias_grad
 

time: 77 us -> 74.2 us (0.964)
  blocking collectives: 12.3 us -> 0 us
  starting transfers between devices: 20.9 us -> 30.3 us
    all_to_all x1 -> x0, blocking collectives: 12.3 us -> none  [on_device(): lax.all_to_all(merged, 'col', 0, 0, tiled=True, axis_index_groups=HEAD_GR...]
    ppermute x3 -> x9, starting transfers between devices: 4.79 us -> 14.2 us  [traded(): lax.ppermute(blocks[k], 'col', trade(k))]
    ppermute x3 -> x9, waiting for transfers between devices: 6.16 us -> 10.8 us  [traded(): lax.ppermute(blocks[k], 'col', trade(k))]
    ppermute x1, waiting for transfers between devices: 4.4 us -> 0.01 us  [on_device(): over_x = lax.ppermute(send, 'col', flip(4))]
  transfers between devices with their start and end apart: 10 -> 16, of which waited for: 8 -> 10; matrix products, arithmetic and copies ran while one was open for 0% -> 0% of each run, Pallas kernels for 2% -> 2%
where the time goes in v4:
time: 74.2 us; the launch traced here: 73.9 us
  starting transfers between devices  30.3 us (41%)
  waiting for transfers between devices  29.8 us (40%)
  Pallas kernels  12.1 us (16%)
  local copies, waits for them, and re-layouts  0.91 us (1%)
    ppermute x9, starting transfers between devices, traded(): lax.ppermute(blocks[k], 'col', trade(k))  14.2 us
    all_to_all x1, waiting for transfers between devices, on_device(): bias_rows = lax.all_to_all(band, 'row', 0, 0, tiled=True)  11.4 us
    ppermute x9, waiting for transfers between devices, traded(): lax.ppermute(blocks[k], 'col', trade(k))  10.8 us
    all_to_all x1, starting transfers between devices, on_device(): bias_rows = lax.all_to_all(band, 'row', 0, 0, tiled=True)  10.2 us
    pallas_call x1, Pallas kernels, on_device(): call(functools.partial(main_kernel, size ** (-0.5)), 'main', (dq_block, d...  6.84 us
    all_to_all x1, waiting for transfers between devices, on_device(): parts_in = lax.all_to_all(dbias, 'row', 0, 0, tiled=True)  4.4 us
    all_to_all x1, starting transfers between devices, on_device(): parts_in = lax.all_to_all(dbias, 'row', 0, 0, tiled=True)  3.54 us
    pallas_call x1, Pallas kernels, on_device(): call(functools.partial(pack_kernel, math.sqrt(size)), 'pack', (struct((2...  2.6 us
  transfers between devices with their start and end apart: 16, of which 10 were waited for; matrix products, arithmetic and copies ran while one was open for 0% of the time, Pallas kernels for 2%

profile of v4, /device:TPU:32, one launch (start us, length us, event | category | flops | bytes accessed | tf_op | source)
XLA Modules:
  0.0 73.9 jit_solution(422655400017202935)
XLA Ops:
  0.6 2.6 %pack.1 = (bf16[13,48,128]{2,1,0:T(8,128)(2,1)}, bf16[13,48,128]{2,1,0:T(8,128)(2,1)}, bf16[13,48,128]{2,1,0:T(8,128)(2,1)}, bf16[13,48,128]{2,1,0:T(8,128)(2,1)}) custom-call(bf16[12,48,128]{2,1,0:T(8,128)(2,1)} %refs_0_.1, bf16[12,48,256]{2,1,0:T(8,128)(2,1)} %refs_1_.1, bf16[12,48,128]{2,1,0:T(8,128)(2,1)} %refs_2_.1, bf16[4,48,48]{2,1,0:T(8,128)(2,1)} %refs_3_.1, ...), custom_call_target="tpu_custom_call" | custom-call | tf_op jit(solution)/shard_map/pack/pallas_call | solution.py:321
  3.2 1.9 %collective-permute-start = (bf16[13,48,128]{2,1,0:T(8,128)(2,1)}, bf16[13,48,128]{2,1,0:T(8,128)(2,1)S(1)}, u32[]{:S(2)}, u32[]{:S(2)}) collective-permute-start(bf16[13,48,128]{2,1,0:T(8,128)(2,1)} %get-tuple-element.25), channel_id=1, source_target_pairs={{0,2},{2,0},{12,14},{14,12},{1,3},{3,1},{13,15},{15,13},{4,6},{6,4... | collective-permute-start | bytes 479240 | tf_op jit(solution)/shard_map/ppermute | solution.py:319
  5.2 1.0 %collective-permute-start.1 = (bf16[13,48,128]{2,1,0:T(8,128)(2,1)}, bf16[13,48,128]{2,1,0:T(8,128)(2,1)S(1)}, u32[]{:S(2)}, u32[]{:S(2)}) collective-permute-start(bf16[13,48,128]{2,1,0:T(8,128)(2,1)} %get-tuple-element.26), channel_id=1, source_target_pairs={{0,12},{2,14},{12,0},{14,2},{1,13},{3,15},{13,1},{15,3},{4,8},{6,1... | collective-permute-start | bytes 479240 | tf_op jit(solution)/shard_map/ppermute | solution.py:319
  6.2 1.8 %collective-permute-start.2 = (bf16[13,48,128]{2,1,0:T(8,128)(2,1)}, bf16[13,48,128]{2,1,0:T(8,128)(2,1)S(1)}, u32[]{:S(2)}, u32[]{:S(2)}) collective-permute-start(bf16[13,48,128]{2,1,0:T(8,128)(2,1)} %get-tuple-element.27), channel_id=1, source_target_pairs={{0,14},{2,12},{12,2},{14,0},{1,15},{3,13},{13,3},{15,1},{4,10},{6,... | collective-permute-start | bytes 479240 | tf_op jit(solution)/shard_map/ppermute | solution.py:319
  8.0 0.0 copy-start
  8.0 0.9 %copy-done = bf16[13,48,128]{2,1,0:T(8,128)(2,1)S(1)} copy-done((bf16[13,48,128]{2,1,0:T(8,128)(2,1)S(1)}, bf16[13,48,128]{2,1,0:T(8,128)(2,1)}, u32[]{:S(2)}) %copy-start) | copy-done | bytes 159768
  8.9 0.2 hold.1.refs_0_
  9.1 1.1 %collective-permute-done.refs_1_ = bf16[13,48,128]{2,1,0:T(8,128)(2,1)S(1)} collective-permute-done((bf16[13,48,128]{2,1,0:T(8,128)(2,1)}, bf16[13,48,128]{2,1,0:T(8,128)(2,1)S(1)}, u32[]{:S(2)}, u32[]{:S(2)}) %collective-permute-start) | collective-permute-done | bytes 159776 | tf_op jit(solution)/shard_map/ppermute | solution.py:319
  10.3 5.0 %collective-permute-done.1.refs_2_ = bf16[13,48,128]{2,1,0:T(8,128)(2,1)S(1)} collective-permute-done((bf16[13,48,128]{2,1,0:T(8,128)(2,1)}, bf16[13,48,128]{2,1,0:T(8,128)(2,1)S(1)}, u32[]{:S(2)}, u32[]{:S(2)}) %collective-permute-start.1) | collective-permute-done | bytes 159776 | tf_op jit(solution)/shard_map/ppermute | solution.py:319
  15.3 0.0 collective-permute-done.2.refs_3_
  15.3 0.1 collective-permute-start.4
  15.4 0.9 %band.1 = bf16[16,80,128]{2,1,0:T(8,128)(2,1)} custom-call(bf16[13,48,128]{2,1,0:T(8,128)(2,1)S(1)} %hold.1.refs_0_, bf16[13,48,128]{2,1,0:T(8,128)(2,1)S(1)} %collective-permute-done.refs_1_, bf16[13,48,128]{2,1,0:T(8,128)(2,1)S(1)} %collective-permute-done.1.refs_2_, bf16[13,48,128]{2,1,0:T(8,128)(2,1)S(1)} %collective-permute-done.2.refs_3_), custom_call_target="tpu_custom_call" | custom-call | tf_op jit(solution)/shard_map/band/pallas_call | solution.py:348
  16.3 10.2 %all-to-all-start = ((bf16[16,80,128]{2,1,0:T(8,128)(2,1)}), bf16[16,80,128]{2,1,0:T(8,128)(2,1)S(1)}, u32[]{:S(2)}, u32[]{:S(2)}) async-start(bf16[16,80,128]{2,1,0:T(8,128)(2,1)} %band.1), calls=%async_computation | async-start | bytes 655360 | tf_op jit(solution)/shard_map/all_to_all | solution.py:349
  26.5 0.1 collective-permute-start.3
  26.6 0.0 collective-permute-done.4.a2_ref
  26.6 0.5 collective-permute-start.5
  27.1 1.1 %collective-permute-done.3.a1_ref = bf16[7,192,128]{2,1,0:T(8,128)(2,1)S(1)} collective-permute-done((bf16[7,192,128]{2,1,0:T(8,128)(2,1)S(1)}, bf16[7,192,128]{2,1,0:T(8,128)(2,1)S(1)}, u32[]{:S(2)}, u32[]{:S(2)}) %collective-permute-start.3) | collective-permute-done | bytes 344096 | tf_op jit(solution)/shard_map/ppermute | solution.py:345
  28.3 0.5 collective-permute-done.5.a3_ref
  28.8 0.1 join.1.refs_4_
  28.8 11.4 %all-to-all-done.refs_5_ = bf16[16,80,128]{2,1,0:T(8,128)(2,1)S(1)} async-done(((bf16[16,80,128]{2,1,0:T(8,128)(2,1)}), bf16[16,80,128]{2,1,0:T(8,128)(2,1)S(1)}, u32[]{:S(2)}, u32[]{:S(2)}) %all-to-all-start) | async-done | bytes 327712 | tf_op jit(solution)/shard_map/all_to_all | solution.py:349
  40.2 6.8 %main.1 = (bf16[3,192,128]{2,1,0:T(8,128)(2,1)S(1)}, bf16[3,192,128]{2,1,0:T(8,128)(2,1)S(1)}, bf16[2,3,192,128]{3,2,1,0:T(8,128)(2,1)S(1)}, bf16[6,48,128]{2,1,...) custom-call(bf16[13,48,128]{2,1,0:T(8,128)(2,1)S(1)} %hold.1.refs_0_, ...), custom_call_target="tpu_custom_call" | custom-call | tf_op jit(solution)/shard_map/main/pallas_call | solution.py:358
  47.1 3.5 %all-to-all-start.1 = ((bf16[16,80,128]{2,1,0:T(8,128)(2,1)}), bf16[16,80,128]{2,1,0:T(8,128)(2,1)S(1)}, u32[]{:S(2)}, u32[]{:S(2)}) async-start(bf16[16,80,128]{2,1,0:T(8,128)(2,1)} %get-tuple-element.33), calls=%async_computation.1 | async-start | bytes 655360 | tf_op jit(solution)/shard_map/all_to_all | solution.py:384
  50.6 0.1 collective-permute-start.6
  50.7 1.6 %collective-permute-done.6.got_ref = bf16[2,3,192,128]{3,2,1,0:T(8,128)(2,1)S(1)} collective-permute-done((bf16[2,3,192,128]{3,2,1,0:T(8,128)(2,1)S(1)}, bf16[2,3,192,128]{3,2,1,0:T(8,128)(2,1)S(1)}, u32[]{:S(2)}, u32[]{:S(2)}) %collective-permute-start.6) | collective-permute-done | bytes 294944 | tf_op jit(solution)/shard_map/ppermute | solution.py:376
  52.3 0.1 fold_core.1
  52.4 1.6 %collective-permute-start.7 = (bf16[3,192,128]{2,1,0:T(8,128)(2,1)S(1)}, bf16[3,192,128]{2,1,0:T(8,128)(2,1)S(1)}, u32[]{:S(2)}, u32[]{:S(2)}) collective-permute-start(bf16[3,192,128]{2,1,0:T(8,128)(2,1)S(1)} %get-tuple-element.32), channel_id=1, source_target_pairs={{0,4},{1,5},{2,6},{3,7},{4,0},{5,1},{6,2},{7,3},{8,12},{9,13},{10,... | collective-permute-start | bytes 442376 | tf_op jit(solution)/shard_map/ppermute | solution.py:383
  53.9 0.8 %collective-permute-start.11 = (bf16[6,48,128]{2,1,0:T(8,128)(2,1)S(1)}, bf16[6,48,128]{2,1,0:T(8,128)(2,1)S(1)}, u32[]{:S(2)}, u32[]{:S(2)}) collective-permute-start(bf16[6,48,128]{2,1,0:T(8,128)(2,1)S(1)} %get-tuple-element.39), channel_id=1, source_target_pairs={{0,2},{2,0},{12,14},{14,12},{1,3},{3,1},{13,15},{15,13},{4,6},{6,4... | collective-permute-start | bytes 221192 | tf_op jit(solution)/shard_map/ppermute | solution.py:319
  54.7 2.6 %collective-permute-start.12 = (bf16[6,48,128]{2,1,0:T(8,128)(2,1)S(1)}, bf16[6,48,128]{2,1,0:T(8,128)(2,1)S(1)}, u32[]{:S(2)}, u32[]{:S(2)}) collective-permute-start(bf16[6,48,128]{2,1,0:T(8,128)(2,1)S(1)} %get-tuple-element.40), channel_id=1, source_target_pairs={{0,12},{2,14},{12,0},{14,2},{1,13},{3,15},{13,1},{15,3},{4,8},{6,1... | collective-permute-start | bytes 221192 | tf_op jit(solution)/shard_map/ppermute | solution.py:319
  57.3 1.3 %collective-permute-start.13 = (bf16[6,48,128]{2,1,0:T(8,128)(2,1)S(1)}, bf16[6,48,128]{2,1,0:T(8,128)(2,1)S(1)}, u32[]{:S(2)}, u32[]{:S(2)}) collective-permute-start(bf16[6,48,128]{2,1,0:T(8,128)(2,1)S(1)} %get-tuple-element.41), channel_id=1, source_target_pairs={{0,14},{2,12},{12,2},{14,0},{1,15},{3,13},{13,3},{15,1},{4,10},{6,... | collective-permute-start | bytes 221192 | tf_op jit(solution)/shard_map/ppermute | solution.py:319
  58.6 0.0 collective-permute-done.7.got_ref
  58.7 4.4 %all-to-all-done.1.db_ref = bf16[16,80,128]{2,1,0:T(8,128)(2,1)S(1)} async-done(((bf16[16,80,128]{2,1,0:T(8,128)(2,1)}), bf16[16,80,128]{2,1,0:T(8,128)(2,1)S(1)}, u32[]{:S(2)}, u32[]{:S(2)}) %all-to-all-start.1) | async-done | bytes 327712 | tf_op jit(solution)/shard_map/all_to_all | solution.py:384
  63.1 0.2 merge.1
  63.2 3.2 %collective-permute-start.10 = (bf16[4,48,128]{2,1,0:T(8,128)(2,1)S(1)}, bf16[4,48,128]{2,1,0:T(8,128)(2,1)S(1)}, u32[]{:S(2)}, u32[]{:S(2)}) collective-permute-start(bf16[4,48,128]{2,1,0:T(8,128)(2,1)S(1)} %get-tuple-element.37), channel_id=1, source_target_pairs={{0,14},{2,12},{12,2},{14,0},{1,15},{3,13},{13,3},{15,1},{4,10},{6,... | collective-permute-start | bytes 147464 | tf_op jit(solution)/shard_map/ppermute | solution.py:319
  66.4 0.9 %collective-permute-start.8 = (bf16[4,48,128]{2,1,0:T(8,128)(2,1)S(1)}, bf16[4,48,128]{2,1,0:T(8,128)(2,1)S(1)}, u32[]{:S(2)}, u32[]{:S(2)}) collective-permute-start(bf16[4,48,128]{2,1,0:T(8,128)(2,1)S(1)} %get-tuple-element.35), channel_id=1, source_target_pairs={{0,2},{2,0},{12,14},{14,12},{1,3},{3,1},{13,15},{15,13},{4,6},{6,4... | collective-permute-start | bytes 147464 | tf_op jit(solution)/shard_map/ppermute | solution.py:319
  67.3 0.0 collective-permute-done.11.refs_5_
  67.3 0.7 collective-permute-start.9
  68.0 0.0 collective-permute-done.12.refs_6_
  68.0 0.0 collective-permute-done.13.refs_7_
  68.0 1.5 %collective-permute-done.10.refs_3_ = bf16[4,48,128]{2,1,0:T(8,128)(2,1)S(1)} collective-permute-done((bf16[4,48,128]{2,1,0:T(8,128)(2,1)S(1)}, bf16[4,48,128]{2,1,0:T(8,128)(2,1)S(1)}, u32[]{:S(2)}, u32[]{:S(2)}) %collective-permute-start.10) | collective-permute-done | bytes 49184 | tf_op jit(solution)/shard_map/ppermute | solution.py:319
  69.5 1.0 %collective-permute-done.8.refs_1_ = bf16[4,48,128]{2,1,0:T(8,128)(2,1)S(1)} collective-permute-done((bf16[4,48,128]{2,1,0:T(8,128)(2,1)S(1)}, bf16[4,48,128]{2,1,0:T(8,128)(2,1)S(1)}, u32[]{:S(2)}, u32[]{:S(2)}) %collective-permute-start.8) | collective-permute-done | bytes 49184 | tf_op jit(solution)/shard_map/ppermute | solution.py:319
  70.5 2.1 %collective-permute-done.9.refs_2_ = bf16[4,48,128]{2,1,0:T(8,128)(2,1)S(1)} collective-permute-done((bf16[4,48,128]{2,1,0:T(8,128)(2,1)S(1)}, bf16[4,48,128]{2,1,0:T(8,128)(2,1)S(1)}, u32[]{:S(2)}, u32[]{:S(2)}) %collective-permute-start.9) | collective-permute-done | bytes 49184 | tf_op jit(solution)/shard_map/ppermute | solution.py:319
  72.6 1.2 %final.1 = (bf16[12,48,128]{2,1,0:T(8,128)(2,1)}, bf16[12,48,256]{2,1,0:T(8,128)(2,1)}, f32[4,48,48]{2,1,0:T(8,128)}) custom-call(bf16[4,48,128]{2,1,0:T(8,128)(2,1)S(1)} %get-tuple-element.34.refs_0_, bf16[4,48,128]{2,1,0:T(8,128)(2,1)S(1)} %collective-permute-done.8.refs_1_, bf16[4,48,128]{2,1,0:T(8,128)(2,1)S(1)} %collective-permute-done.9.refs_2_, ...), custom_call_target="tpu_custom_call" | custom-call | tf_op jit(solution)/shard_map/final/pallas_call | solution.py:392
  (2 shorter events, 0.1 us)
Async XLA Ops:
  3.2 7.0 %collective-permute-start = (bf16[13,48,128]{2,1,0:T(8,128)(2,1)}, bf16[13,48,128]{2,1,0:T(8,128)(2,1)S(1)}, u32[]{:S(2)}, u32[]{:S(2)}) collective-permute-start(bf16[13,48,128]{2,1,0:T(8,128)(2,1)} %get-tuple-element.25), channel_id=1, source_target_pairs={{0,2},{2,0},{12,14},{14,12},{1,3},{3,1},{13,15},{15,13},{4,6},{6,4... | collective-permute-start | bytes 479240 | tf_op jit(solution)/shard_map/ppermute | solution.py:319
  5.2 10.1 %collective-permute-start.1 = (bf16[13,48,128]{2,1,0:T(8,128)(2,1)}, bf16[13,48,128]{2,1,0:T(8,128)(2,1)S(1)}, u32[]{:S(2)}, u32[]{:S(2)}) collective-permute-start(bf16[13,48,128]{2,1,0:T(8,128)(2,1)} %get-tuple-element.26), channel_id=1, source_target_pairs={{0,12},{2,14},{12,0},{14,2},{1,13},{3,15},{13,1},{15,3},{4,8},{6,1... | collective-permute-start | bytes 479240 | tf_op jit(solution)/shard_map/ppermute | solution.py:319
  6.2 9.1 %collective-permute-start.2 = (bf16[13,48,128]{2,1,0:T(8,128)(2,1)}, bf16[13,48,128]{2,1,0:T(8,128)(2,1)S(1)}, u32[]{:S(2)}, u32[]{:S(2)}) collective-permute-start(bf16[13,48,128]{2,1,0:T(8,128)(2,1)} %get-tuple-element.27), channel_id=1, source_target_pairs={{0,14},{2,12},{12,2},{14,0},{1,15},{3,13},{13,3},{15,1},{4,10},{6,... | collective-permute-start | bytes 479240 | tf_op jit(solution)/shard_map/ppermute | solution.py:319
  8.0 0.9 %copy-start = (bf16[13,48,128]{2,1,0:T(8,128)(2,1)S(1)}, bf16[13,48,128]{2,1,0:T(8,128)(2,1)}, u32[]{:S(2)}) copy-start(bf16[13,48,128]{2,1,0:T(8,128)(2,1)} %get-tuple-element.24.src_ref) | copy-start | bytes 479236
  15.3 11.3 %collective-permute-start.4 = (bf16[7,192,128]{2,1,0:T(8,128)(2,1)S(1)}, bf16[7,192,128]{2,1,0:T(8,128)(2,1)S(1)}, u32[]{:S(2)}, u32[]{:S(2)}) collective-permute-start(bf16[7,192,128]{2,1,0:T(8,128)(2,1)S(1)} %own.1.a0_ref), channel_id=1, source_target_pairs={{0,4},{1,5},{2,6},{3,7},{4,0},{5,1},{6,2},{7,3},{8,12},{9,13},{10,... | collective-permute-start | bytes 1032200 | tf_op jit(solution)/shard_map/ppermute | solution.py:344
  16.3 23.9 %all-to-all-start = ((bf16[16,80,128]{2,1,0:T(8,128)(2,1)}), bf16[16,80,128]{2,1,0:T(8,128)(2,1)S(1)}, u32[]{:S(2)}, u32[]{:S(2)}) async-start(bf16[16,80,128]{2,1,0:T(8,128)(2,1)} %band.1), calls=%async_computation | async-start | bytes 655360 | tf_op jit(solution)/shard_map/all_to_all | solution.py:349
  26.5 1.7 %collective-permute-start.3 = (bf16[7,192,128]{2,1,0:T(8,128)(2,1)S(1)}, bf16[7,192,128]{2,1,0:T(8,128)(2,1)S(1)}, u32[]{:S(2)}, u32[]{:S(2)}) collective-permute-start(bf16[7,192,128]{2,1,0:T(8,128)(2,1)S(1)} %own.1.a0_ref), channel_id=1, source_target_pairs={{0,1},{1,0},{2,3},{3,2},{4,5},{5,4},{6,7},{7,6},{8,9},{9,8},{10,11... | collective-permute-start | bytes 1032200 | tf_op jit(solution)/shard_map/ppermute | solution.py:345
  26.6 2.1 %collective-permute-start.5 = (bf16[7,192,128]{2,1,0:T(8,128)(2,1)S(1)}, bf16[7,192,128]{2,1,0:T(8,128)(2,1)S(1)}, u32[]{:S(2)}, u32[]{:S(2)}) collective-permute-start(bf16[7,192,128]{2,1,0:T(8,128)(2,1)S(1)} %collective-permute-done.4.a2_ref), channel_id=1, source_target_pairs={{0,1},{1,0},{2,3},{3,2},{4,5},{5,4},{6,7},{7,6},{8,9},{9,8},{10,11... | collective-permute-start | bytes 1032200 | tf_op jit(solution)/shard_map/ppermute | solution.py:350
  47.1 16.0 %all-to-all-start.1 = ((bf16[16,80,128]{2,1,0:T(8,128)(2,1)}), bf16[16,80,128]{2,1,0:T(8,128)(2,1)S(1)}, u32[]{:S(2)}, u32[]{:S(2)}) async-start(bf16[16,80,128]{2,1,0:T(8,128)(2,1)} %get-tuple-element.33), calls=%async_computation.1 | async-start | bytes 655360 | tf_op jit(solution)/shard_map/all_to_all | solution.py:384
  50.6 1.7 %collective-permute-start.6 = (bf16[2,3,192,128]{3,2,1,0:T(8,128)(2,1)S(1)}, bf16[2,3,192,128]{3,2,1,0:T(8,128)(2,1)S(1)}, u32[]{:S(2)}, u32[]{:S(2)}) collective-permute-start(bf16[2,3,192,128]{3,2,1,0:T(8,128)(2,1)S(1)} %get-tuple-element.30), channel_id=1, source_target_pairs={{0,1},{1,0},{2,3},{3,2},{4,5},{5,4},{6,7},{7,6},{8,9},{9,8},{10,11... | collective-permute-start | bytes 884744 | tf_op jit(solution)/shard_map/ppermute | solution.py:376
  52.4 6.3 %collective-permute-start.7 = (bf16[3,192,128]{2,1,0:T(8,128)(2,1)S(1)}, bf16[3,192,128]{2,1,0:T(8,128)(2,1)S(1)}, u32[]{:S(2)}, u32[]{:S(2)}) collective-permute-start(bf16[3,192,128]{2,1,0:T(8,128)(2,1)S(1)} %get-tuple-element.32), channel_id=1, source_target_pairs={{0,4},{1,5},{2,6},{3,7},{4,0},{5,1},{6,2},{7,3},{8,12},{9,13},{10,... | collective-permute-start | bytes 442376 | tf_op jit(solution)/shard_map/ppermute | solution.py:383
  53.9 13.4 %collective-permute-start.11 = (bf16[6,48,128]{2,1,0:T(8,128)(2,1)S(1)}, bf16[6,48,128]{2,1,0:T(8,128)(2,1)S(1)}, u32[]{:S(2)}, u32[]{:S(2)}) collective-permute-start(bf16[6,48,128]{2,1,0:T(8,128)(2,1)S(1)} %get-tuple-element.39), channel_id=1, source_target_pairs={{0,2},{2,0},{12,14},{14,12},{1,3},{3,1},{13,15},{15,13},{4,6},{6,4... | collective-permute-start | bytes 221192 | tf_op jit(solution)/shard_map/ppermute | solution.py:319
  54.7 13.3 %collective-permute-start.12 = (bf16[6,48,128]{2,1,0:T(8,128)(2,1)S(1)}, bf16[6,48,128]{2,1,0:T(8,128)(2,1)S(1)}, u32[]{:S(2)}, u32[]{:S(2)}) collective-permute-start(bf16[6,48,128]{2,1,0:T(8,128)(2,1)S(1)} %get-tuple-element.40), channel_id=1, source_target_pairs={{0,12},{2,14},{12,0},{14,2},{1,13},{3,15},{13,1},{15,3},{4,8},{6,1... | collective-permute-start | bytes 221192 | tf_op jit(solution)/shard_map/ppermute | solution.py:319
  57.3 10.7 %collective-permute-start.13 = (bf16[6,48,128]{2,1,0:T(8,128)(2,1)S(1)}, bf16[6,48,128]{2,1,0:T(8,128)(2,1)S(1)}, u32[]{:S(2)}, u32[]{:S(2)}) collective-permute-start(bf16[6,48,128]{2,1,0:T(8,128)(2,1)S(1)} %get-tuple-element.41), channel_id=1, source_target_pairs={{0,14},{2,12},{12,2},{14,0},{1,15},{3,13},{13,3},{15,1},{4,10},{6,... | collective-permute-start | bytes 221192 | tf_op jit(solution)/shard_map/ppermute | solution.py:319
  63.2 6.3 %collective-permute-start.10 = (bf16[4,48,128]{2,1,0:T(8,128)(2,1)S(1)}, bf16[4,48,128]{2,1,0:T(8,128)(2,1)S(1)}, u32[]{:S(2)}, u32[]{:S(2)}) collective-permute-start(bf16[4,48,128]{2,1,0:T(8,128)(2,1)S(1)} %get-tuple-element.37), channel_id=1, source_target_pairs={{0,14},{2,12},{12,2},{14,0},{1,15},{3,13},{13,3},{15,1},{4,10},{6,... | collective-permute-start | bytes 147464 | tf_op jit(solution)/shard_map/ppermute | solution.py:319
  66.4 4.1 %collective-permute-start.8 = (bf16[4,48,128]{2,1,0:T(8,128)(2,1)S(1)}, bf16[4,48,128]{2,1,0:T(8,128)(2,1)S(1)}, u32[]{:S(2)}, u32[]{:S(2)}) collective-permute-start(bf16[4,48,128]{2,1,0:T(8,128)(2,1)S(1)} %get-tuple-element.35), channel_id=1, source_target_pairs={{0,2},{2,0},{12,14},{14,12},{1,3},{3,1},{13,15},{15,13},{4,6},{6,4... | collective-permute-start | bytes 147464 | tf_op jit(solution)/shard_map/ppermute | solution.py:319
  67.3 5.3 %collective-permute-start.9 = (bf16[4,48,128]{2,1,0:T(8,128)(2,1)S(1)}, bf16[4,48,128]{2,1,0:T(8,128)(2,1)S(1)}, u32[]{:S(2)}, u32[]{:S(2)}) collective-permute-start(bf16[4,48,128]{2,1,0:T(8,128)(2,1)S(1)} %get-tuple-element.36), channel_id=1, source_target_pairs={{0,12},{2,14},{12,0},{14,2},{1,13},{3,15},{13,1},{15,3},{4,8},{6,1... | collective-permute-start | bytes 147464 | tf_op jit(solution)/shard_map/ppermute | solution.py:319

commit v5 on v4

--- a/solution.py
+++ b/solution.py
@@ -189,12 +189,11 @@
         bias_t[:, t : t + LANES] = (
             jnp.transpose(rows[t : t + LANES])[0:keys] * log2e
         )
-    acc[...] = jnp.zeros_like(acc)
     lane = lax.broadcasted_iota(jnp.int32, (keys, LANES), 1)
     quarter = lax.broadcasted_iota(jnp.int32, (total, LANES), 1) // size
     extra = a_ref[pairs]
     scale_row = jnp.where((lane // size) % 2 == 0, inv_root, 1.0)
-    for p in range(pairs):
+    def both_of(p):
         qp = a_ref[p]
         qx = jnp.concatenate([qp, extra], axis=1)
         kp = jnp.concatenate([ab[pairs + p] for ab in ab_refs], axis=0)
@@ -208,17 +207,29 @@
             left.append(
                 jnp.concatenate([jnp.where(lane // size == s, kp, zero), ones], axis=1)
             )
-        low = []
-        for e in range(2):
-            both = lax.dot_general(
+        return qp, kt, [
+            lax.dot_general(
                 jnp.concatenate(left[2 * e : 2 * e + 2], axis=0),
                 qx,
                 (((1,), (1,)), ((), ())),
                 preferred_element_type=F32,
             )
-            probs = jnp.exp2(both[0:keys] * (inv_root * log2e) + bias_t[...])
-            ds = probs * both[keys:]
-            acc[...] += ds
+            for e in range(2)
+        ]
+
+    coming = both_of(0)
+    for p in range(pairs):
+        qp, kt, both = coming
+        if p + 1 < pairs:
+            coming = both_of(p + 1)
+        low = []
+        for e in range(2):
+            probs = jnp.exp2(both[e][0:keys] * (inv_root * log2e) + bias_t[...])
+            ds = probs * both[e][keys:]
+            if p + e == 0:
+                acc[...] = ds
+            else:
+                acc[...] += ds
             low += [ds.astype(BF), probs.astype(BF)]
             i = 2 * p + e
             dq_t[i * size : (i + 1) * size] = jnp.dot(

time: 74.2 us -> 73.3 us (0.988)
  Pallas kernels: 12.1 us -> 11.2 us
    pallas_call x1, Pallas kernels: 6.84 us -> 5.97 us  [on_device(): call(functools.partial(main_kernel, size ** (-0.5)), 'main', (dq_block, d...]
where the time goes in v5:
time: 73.3 us; the launch traced here: 73 us
  starting transfers between devices  30.4 us (41%)
  waiting for transfers between devices  29.8 us (41%)
  Pallas kernels  11.2 us (15%)
  local copies, waits for them, and re-layouts  0.91 us (1%)
    ppermute x9, starting transfers between devices, traded(): lax.ppermute(blocks[k], 'col', trade(k))  14.2 us
    all_to_all x1, waiting for transfers between devices, on_device(): bias_rows = lax.all_to_all(band, 'row', 0, 0, tiled=True)  11.4 us
    ppermute x9, waiting for transfers between devices, traded(): lax.ppermute(blocks[k], 'col', trade(k))  10.8 us
    all_to_all x1, starting transfers between devices, on_device(): bias_rows = lax.all_to_all(band, 'row', 0, 0, tiled=True)  10.2 us
    pallas_call x1, Pallas kernels, on_device(): call(functools.partial(main_kernel, size ** (-0.5)), 'main', (dq_block, d...  5.97 us
    all_to_all x1, waiting for transfers between devices, on_device(): parts_in = lax.all_to_all(dbias, 'row', 0, 0, tiled=True)  4.41 us
    all_to_all x1, starting transfers between devices, on_device(): parts_in = lax.all_to_all(dbias, 'row', 0, 0, tiled=True)  3.54 us
    pallas_call x1, Pallas kernels, on_device(): call(functools.partial(pack_kernel, math.sqrt(size)), 'pack', (struct((2...  2.6 us
  transfers between devices with their start and end apart: 16, of which 10 were waited for; matrix products, arithmetic and copies ran while one was open for 0% of the time, Pallas kernels for 2%

profile of v5, /device:TPU:32, one launch (start us, length us, event | category | flops | bytes accessed | tf_op | source)
XLA Modules:
  0.0 73.0 jit_solution(5929902229851192535)
XLA Ops:
  0.6 2.6 %pack.1 = (bf16[13,48,128]{2,1,0:T(8,128)(2,1)}, bf16[13,48,128]{2,1,0:T(8,128)(2,1)}, bf16[13,48,128]{2,1,0:T(8,128)(2,1)}, bf16[13,48,128]{2,1,0:T(8,128)(2,1)}) custom-call(bf16[12,48,128]{2,1,0:T(8,128)(2,1)} %refs_0_.1, bf16[12,48,256]{2,1,0:T(8,128)(2,1)} %refs_1_.1, bf16[12,48,128]{2,1,0:T(8,128)(2,1)} %refs_2_.1, bf16[4,48,48]{2,1,0:T(8,128)(2,1)} %refs_3_.1, ...), custom_call_target="tpu_custom_call" | custom-call | tf_op jit(solution)/shard_map/pack/pallas_call | solution.py:332
  3.2 1.9 %collective-permute-start = (bf16[13,48,128]{2,1,0:T(8,128)(2,1)}, bf16[13,48,128]{2,1,0:T(8,128)(2,1)S(1)}, u32[]{:S(2)}, u32[]{:S(2)}) collective-permute-start(bf16[13,48,128]{2,1,0:T(8,128)(2,1)} %get-tuple-element.25), channel_id=1, source_target_pairs={{0,2},{2,0},{12,14},{14,12},{1,3},{3,1},{13,15},{15,13},{4,6},{6,4... | collective-permute-start | bytes 479240 | tf_op jit(solution)/shard_map/ppermute | solution.py:330
  5.2 1.0 %collective-permute-start.1 = (bf16[13,48,128]{2,1,0:T(8,128)(2,1)}, bf16[13,48,128]{2,1,0:T(8,128)(2,1)S(1)}, u32[]{:S(2)}, u32[]{:S(2)}) collective-permute-start(bf16[13,48,128]{2,1,0:T(8,128)(2,1)} %get-tuple-element.26), channel_id=1, source_target_pairs={{0,12},{2,14},{12,0},{14,2},{1,13},{3,15},{13,1},{15,3},{4,8},{6,1... | collective-permute-start | bytes 479240 | tf_op jit(solution)/shard_map/ppermute | solution.py:330
  6.2 1.8 %collective-permute-start.2 = (bf16[13,48,128]{2,1,0:T(8,128)(2,1)}, bf16[13,48,128]{2,1,0:T(8,128)(2,1)S(1)}, u32[]{:S(2)}, u32[]{:S(2)}) collective-permute-start(bf16[13,48,128]{2,1,0:T(8,128)(2,1)} %get-tuple-element.27), channel_id=1, source_target_pairs={{0,14},{2,12},{12,2},{14,0},{1,15},{3,13},{13,3},{15,1},{4,10},{6,... | collective-permute-start | bytes 479240 | tf_op jit(solution)/shard_map/ppermute | solution.py:330
  8.0 0.0 copy-start
  8.0 0.9 %copy-done = bf16[13,48,128]{2,1,0:T(8,128)(2,1)S(1)} copy-done((bf16[13,48,128]{2,1,0:T(8,128)(2,1)S(1)}, bf16[13,48,128]{2,1,0:T(8,128)(2,1)}, u32[]{:S(2)}) %copy-start) | copy-done | bytes 159768
  8.9 0.2 hold.1.refs_0_
  9.1 1.1 %collective-permute-done.refs_1_ = bf16[13,48,128]{2,1,0:T(8,128)(2,1)S(1)} collective-permute-done((bf16[13,48,128]{2,1,0:T(8,128)(2,1)}, bf16[13,48,128]{2,1,0:T(8,128)(2,1)S(1)}, u32[]{:S(2)}, u32[]{:S(2)}) %collective-permute-start) | collective-permute-done | bytes 159776 | tf_op jit(solution)/shard_map/ppermute | solution.py:330
  10.3 5.0 %collective-permute-done.1.refs_2_ = bf16[13,48,128]{2,1,0:T(8,128)(2,1)S(1)} collective-permute-done((bf16[13,48,128]{2,1,0:T(8,128)(2,1)}, bf16[13,48,128]{2,1,0:T(8,128)(2,1)S(1)}, u32[]{:S(2)}, u32[]{:S(2)}) %collective-permute-start.1) | collective-permute-done | bytes 159776 | tf_op jit(solution)/shard_map/ppermute | solution.py:330
  15.3 0.0 collective-permute-done.2.refs_3_
  15.3 0.1 collective-permute-start.4
  15.4 0.9 %band.1 = bf16[16,80,128]{2,1,0:T(8,128)(2,1)} custom-call(bf16[13,48,128]{2,1,0:T(8,128)(2,1)S(1)} %hold.1.refs_0_, bf16[13,48,128]{2,1,0:T(8,128)(2,1)S(1)} %collective-permute-done.refs_1_, bf16[13,48,128]{2,1,0:T(8,128)(2,1)S(1)} %collective-permute-done.1.refs_2_, bf16[13,48,128]{2,1,0:T(8,128)(2,1)S(1)} %collective-permute-done.2.refs_3_), custom_call_target="tpu_custom_call" | custom-call | tf_op jit(solution)/shard_map/band/pallas_call | solution.py:359
  16.3 10.2 %all-to-all-start = ((bf16[16,80,128]{2,1,0:T(8,128)(2,1)}), bf16[16,80,128]{2,1,0:T(8,128)(2,1)S(1)}, u32[]{:S(2)}, u32[]{:S(2)}) async-start(bf16[16,80,128]{2,1,0:T(8,128)(2,1)} %band.1), calls=%async_computation | async-start | bytes 655360 | tf_op jit(solution)/shard_map/all_to_all | solution.py:360
  26.5 0.1 collective-permute-start.3
  26.6 0.0 collective-permute-done.4.a2_ref
  26.6 0.5 collective-permute-start.5
  27.1 1.1 %collective-permute-done.3.a1_ref = bf16[7,192,128]{2,1,0:T(8,128)(2,1)S(1)} collective-permute-done((bf16[7,192,128]{2,1,0:T(8,128)(2,1)S(1)}, bf16[7,192,128]{2,1,0:T(8,128)(2,1)S(1)}, u32[]{:S(2)}, u32[]{:S(2)}) %collective-permute-start.3) | collective-permute-done | bytes 344096 | tf_op jit(solution)/shard_map/ppermute | solution.py:356
  28.3 0.5 collective-permute-done.5.a3_ref
  28.8 0.1 join.1.refs_4_
  28.8 11.4 %all-to-all-done.refs_5_ = bf16[16,80,128]{2,1,0:T(8,128)(2,1)S(1)} async-done(((bf16[16,80,128]{2,1,0:T(8,128)(2,1)}), bf16[16,80,128]{2,1,0:T(8,128)(2,1)S(1)}, u32[]{:S(2)}, u32[]{:S(2)}) %all-to-all-start) | async-done | bytes 327712 | tf_op jit(solution)/shard_map/all_to_all | solution.py:360
  40.2 6.0 %main.1 = (bf16[3,192,128]{2,1,0:T(8,128)(2,1)S(1)}, bf16[3,192,128]{2,1,0:T(8,128)(2,1)S(1)}, bf16[2,3,192,128]{3,2,1,0:T(8,128)(2,1)S(1)}, bf16[6,48,128]{2,1,...) custom-call(bf16[13,48,128]{2,1,0:T(8,128)(2,1)S(1)} %hold.1.refs_0_, ...), custom_call_target="tpu_custom_call" | custom-call | tf_op jit(solution)/shard_map/main/pallas_call | solution.py:369
  46.2 3.5 %all-to-all-start.1 = ((bf16[16,80,128]{2,1,0:T(8,128)(2,1)}), bf16[16,80,128]{2,1,0:T(8,128)(2,1)S(1)}, u32[]{:S(2)}, u32[]{:S(2)}) async-start(bf16[16,80,128]{2,1,0:T(8,128)(2,1)} %get-tuple-element.33), calls=%async_computation.1 | async-start | bytes 655360 | tf_op jit(solution)/shard_map/all_to_all | solution.py:395
  49.7 0.1 collective-permute-start.6
  49.8 1.6 %collective-permute-done.6.got_ref = bf16[2,3,192,128]{3,2,1,0:T(8,128)(2,1)S(1)} collective-permute-done((bf16[2,3,192,128]{3,2,1,0:T(8,128)(2,1)S(1)}, bf16[2,3,192,128]{3,2,1,0:T(8,128)(2,1)S(1)}, u32[]{:S(2)}, u32[]{:S(2)}) %collective-permute-start.6) | collective-permute-done | bytes 294944 | tf_op jit(solution)/shard_map/ppermute | solution.py:387
  51.4 0.1 fold_core.1
  51.5 1.6 %collective-permute-start.7 = (bf16[3,192,128]{2,1,0:T(8,128)(2,1)S(1)}, bf16[3,192,128]{2,1,0:T(8,128)(2,1)S(1)}, u32[]{:S(2)}, u32[]{:S(2)}) collective-permute-start(bf16[3,192,128]{2,1,0:T(8,128)(2,1)S(1)} %get-tuple-element.32), channel_id=1, source_target_pairs={{0,4},{1,5},{2,6},{3,7},{4,0},{5,1},{6,2},{7,3},{8,12},{9,13},{10,... | collective-permute-start | bytes 442376 | tf_op jit(solution)/shard_map/ppermute | solution.py:394
  53.1 0.8 %collective-permute-start.11 = (bf16[6,48,128]{2,1,0:T(8,128)(2,1)S(1)}, bf16[6,48,128]{2,1,0:T(8,128)(2,1)S(1)}, u32[]{:S(2)}, u32[]{:S(2)}) collective-permute-start(bf16[6,48,128]{2,1,0:T(8,128)(2,1)S(1)} %get-tuple-element.39), channel_id=1, source_target_pairs={{0,2},{2,0},{12,14},{14,12},{1,3},{3,1},{13,15},{15,13},{4,6},{6,4... | collective-permute-start | bytes 221192 | tf_op jit(solution)/shard_map/ppermute | solution.py:330
  53.9 2.6 %collective-permute-start.12 = (bf16[6,48,128]{2,1,0:T(8,128)(2,1)S(1)}, bf16[6,48,128]{2,1,0:T(8,128)(2,1)S(1)}, u32[]{:S(2)}, u32[]{:S(2)}) collective-permute-start(bf16[6,48,128]{2,1,0:T(8,128)(2,1)S(1)} %get-tuple-element.40), channel_id=1, source_target_pairs={{0,12},{2,14},{12,0},{14,2},{1,13},{3,15},{13,1},{15,3},{4,8},{6,1... | collective-permute-start | bytes 221192 | tf_op jit(solution)/shard_map/ppermute | solution.py:330
  56.5 1.3 %collective-permute-start.13 = (bf16[6,48,128]{2,1,0:T(8,128)(2,1)S(1)}, bf16[6,48,128]{2,1,0:T(8,128)(2,1)S(1)}, u32[]{:S(2)}, u32[]{:S(2)}) collective-permute-start(bf16[6,48,128]{2,1,0:T(8,128)(2,1)S(1)} %get-tuple-element.41), channel_id=1, source_target_pairs={{0,14},{2,12},{12,2},{14,0},{1,15},{3,13},{13,3},{15,1},{4,10},{6,... | collective-permute-start | bytes 221192 | tf_op jit(solution)/shard_map/ppermute | solution.py:330
  57.8 0.0 collective-permute-done.7.got_ref
  57.8 4.4 %all-to-all-done.1.db_ref = bf16[16,80,128]{2,1,0:T(8,128)(2,1)S(1)} async-done(((bf16[16,80,128]{2,1,0:T(8,128)(2,1)}), bf16[16,80,128]{2,1,0:T(8,128)(2,1)S(1)}, u32[]{:S(2)}, u32[]{:S(2)}) %all-to-all-start.1) | async-done | bytes 327712 | tf_op jit(solution)/shard_map/all_to_all | solution.py:395
  62.2 0.2 merge.1
  62.4 3.1 %collective-permute-start.10 = (bf16[4,48,128]{2,1,0:T(8,128)(2,1)S(1)}, bf16[4,48,128]{2,1,0:T(8,128)(2,1)S(1)}, u32[]{:S(2)}, u32[]{:S(2)}) collective-permute-start(bf16[4,48,128]{2,1,0:T(8,128)(2,1)S(1)} %get-tuple-element.37), channel_id=1, source_target_pairs={{0,14},{2,12},{12,2},{14,0},{1,15},{3,13},{13,3},{15,1},{4,10},{6,... | collective-permute-start | bytes 147464 | tf_op jit(solution)/shard_map/ppermute | solution.py:330
  65.5 0.9 %collective-permute-start.8 = (bf16[4,48,128]{2,1,0:T(8,128)(2,1)S(1)}, bf16[4,48,128]{2,1,0:T(8,128)(2,1)S(1)}, u32[]{:S(2)}, u32[]{:S(2)}) collective-permute-start(bf16[4,48,128]{2,1,0:T(8,128)(2,1)S(1)} %get-tuple-element.35), channel_id=1, source_target_pairs={{0,2},{2,0},{12,14},{14,12},{1,3},{3,1},{13,15},{15,13},{4,6},{6,4... | collective-permute-start | bytes 147464 | tf_op jit(solution)/shard_map/ppermute | solution.py:330
  66.5 0.0 collective-permute-done.11.refs_5_
  66.5 0.7 collective-permute-start.9
  67.1 0.0 collective-permute-done.12.refs_6_
  67.1 0.0 collective-permute-done.13.refs_7_
  67.1 1.5 %collective-permute-done.10.refs_3_ = bf16[4,48,128]{2,1,0:T(8,128)(2,1)S(1)} collective-permute-done((bf16[4,48,128]{2,1,0:T(8,128)(2,1)S(1)}, bf16[4,48,128]{2,1,0:T(8,128)(2,1)S(1)}, u32[]{:S(2)}, u32[]{:S(2)}) %collective-permute-start.10) | collective-permute-done | bytes 49184 | tf_op jit(solution)/shard_map/ppermute | solution.py:330
  68.6 1.0 %collective-permute-done.8.refs_1_ = bf16[4,48,128]{2,1,0:T(8,128)(2,1)S(1)} collective-permute-done((bf16[4,48,128]{2,1,0:T(8,128)(2,1)S(1)}, bf16[4,48,128]{2,1,0:T(8,128)(2,1)S(1)}, u32[]{:S(2)}, u32[]{:S(2)}) %collective-permute-start.8) | collective-permute-done | bytes 49184 | tf_op jit(solution)/shard_map/ppermute | solution.py:330
  69.6 2.2 %collective-permute-done.9.refs_2_ = bf16[4,48,128]{2,1,0:T(8,128)(2,1)S(1)} collective-permute-done((bf16[4,48,128]{2,1,0:T(8,128)(2,1)S(1)}, bf16[4,48,128]{2,1,0:T(8,128)(2,1)S(1)}, u32[]{:S(2)}, u32[]{:S(2)}) %collective-permute-start.9) | collective-permute-done | bytes 49184 | tf_op jit(solution)/shard_map/ppermute | solution.py:330
  71.8 1.2 %final.1 = (bf16[12,48,128]{2,1,0:T(8,128)(2,1)}, bf16[12,48,256]{2,1,0:T(8,128)(2,1)}, f32[4,48,48]{2,1,0:T(8,128)}) custom-call(bf16[4,48,128]{2,1,0:T(8,128)(2,1)S(1)} %get-tuple-element.34.refs_0_, bf16[4,48,128]{2,1,0:T(8,128)(2,1)S(1)} %collective-permute-done.8.refs_1_, bf16[4,48,128]{2,1,0:T(8,128)(2,1)S(1)} %collective-permute-done.9.refs_2_, ...), custom_call_target="tpu_custom_call" | custom-call | tf_op jit(solution)/shard_map/final/pallas_call | solution.py:403
  (2 shorter events, 0.1 us)
Async XLA Ops:
  3.2 7.0 %collective-permute-start = (bf16[13,48,128]{2,1,0:T(8,128)(2,1)}, bf16[13,48,128]{2,1,0:T(8,128)(2,1)S(1)}, u32[]{:S(2)}, u32[]{:S(2)}) collective-permute-start(bf16[13,48,128]{2,1,0:T(8,128)(2,1)} %get-tuple-element.25), channel_id=1, source_target_pairs={{0,2},{2,0},{12,14},{14,12},{1,3},{3,1},{13,15},{15,13},{4,6},{6,4... | collective-permute-start | bytes 479240 | tf_op jit(solution)/shard_map/ppermute | solution.py:330
  5.2 10.1 %collective-permute-start.1 = (bf16[13,48,128]{2,1,0:T(8,128)(2,1)}, bf16[13,48,128]{2,1,0:T(8,128)(2,1)S(1)}, u32[]{:S(2)}, u32[]{:S(2)}) collective-permute-start(bf16[13,48,128]{2,1,0:T(8,128)(2,1)} %get-tuple-element.26), channel_id=1, source_target_pairs={{0,12},{2,14},{12,0},{14,2},{1,13},{3,15},{13,1},{15,3},{4,8},{6,1... | collective-permute-start | bytes 479240 | tf_op jit(solution)/shard_map/ppermute | solution.py:330
  6.2 9.1 %collective-permute-start.2 = (bf16[13,48,128]{2,1,0:T(8,128)(2,1)}, bf16[13,48,128]{2,1,0:T(8,128)(2,1)S(1)}, u32[]{:S(2)}, u32[]{:S(2)}) collective-permute-start(bf16[13,48,128]{2,1,0:T(8,128)(2,1)} %get-tuple-element.27), channel_id=1, source_target_pairs={{0,14},{2,12},{12,2},{14,0},{1,15},{3,13},{13,3},{15,1},{4,10},{6,... | collective-permute-start | bytes 479240 | tf_op jit(solution)/shard_map/ppermute | solution.py:330
  8.0 0.9 %copy-start = (bf16[13,48,128]{2,1,0:T(8,128)(2,1)S(1)}, bf16[13,48,128]{2,1,0:T(8,128)(2,1)}, u32[]{:S(2)}) copy-start(bf16[13,48,128]{2,1,0:T(8,128)(2,1)} %get-tuple-element.24.src_ref) | copy-start | bytes 479236
  15.3 11.3 %collective-permute-start.4 = (bf16[7,192,128]{2,1,0:T(8,128)(2,1)S(1)}, bf16[7,192,128]{2,1,0:T(8,128)(2,1)S(1)}, u32[]{:S(2)}, u32[]{:S(2)}) collective-permute-start(bf16[7,192,128]{2,1,0:T(8,128)(2,1)S(1)} %own.1.a0_ref), channel_id=1, source_target_pairs={{0,4},{1,5},{2,6},{3,7},{4,0},{5,1},{6,2},{7,3},{8,12},{9,13},{10,... | collective-permute-start | bytes 1032200 | tf_op jit(solution)/shard_map/ppermute | solution.py:355
  16.3 23.9 %all-to-all-start = ((bf16[16,80,128]{2,1,0:T(8,128)(2,1)}), bf16[16,80,128]{2,1,0:T(8,128)(2,1)S(1)}, u32[]{:S(2)}, u32[]{:S(2)}) async-start(bf16[16,80,128]{2,1,0:T(8,128)(2,1)} %band.1), calls=%async_computation | async-start | bytes 655360 | tf_op jit(solution)/shard_map/all_to_all | solution.py:360
  26.5 1.7 %collective-permute-start.3 = (bf16[7,192,128]{2,1,0:T(8,128)(2,1)S(1)}, bf16[7,192,128]{2,1,0:T(8,128)(2,1)S(1)}, u32[]{:S(2)}, u32[]{:S(2)}) collective-permute-start(bf16[7,192,128]{2,1,0:T(8,128)(2,1)S(1)} %own.1.a0_ref), channel_id=1, source_target_pairs={{0,1},{1,0},{2,3},{3,2},{4,5},{5,4},{6,7},{7,6},{8,9},{9,8},{10,11... | collective-permute-start | bytes 1032200 | tf_op jit(solution)/shard_map/ppermute | solution.py:356
  26.6 2.1 %collective-permute-start.5 = (bf16[7,192,128]{2,1,0:T(8,128)(2,1)S(1)}, bf16[7,192,128]{2,1,0:T(8,128)(2,1)S(1)}, u32[]{:S(2)}, u32[]{:S(2)}) collective-permute-start(bf16[7,192,128]{2,1,0:T(8,128)(2,1)S(1)} %collective-permute-done.4.a2_ref), channel_id=1, source_target_pairs={{0,1},{1,0},{2,3},{3,2},{4,5},{5,4},{6,7},{7,6},{8,9},{9,8},{10,11... | collective-permute-start | bytes 1032200 | tf_op jit(solution)/shard_map/ppermute | solution.py:361
  46.2 16.0 %all-to-all-start.1 = ((bf16[16,80,128]{2,1,0:T(8,128)(2,1)}), bf16[16,80,128]{2,1,0:T(8,128)(2,1)S(1)}, u32[]{:S(2)}, u32[]{:S(2)}) async-start(bf16[16,80,128]{2,1,0:T(8,128)(2,1)} %get-tuple-element.33), calls=%async_computation.1 | async-start | bytes 655360 | tf_op jit(solution)/shard_map/all_to_all | solution.py:395
  49.7 1.7 %collective-permute-start.6 = (bf16[2,3,192,128]{3,2,1,0:T(8,128)(2,1)S(1)}, bf16[2,3,192,128]{3,2,1,0:T(8,128)(2,1)S(1)}, u32[]{:S(2)}, u32[]{:S(2)}) collective-permute-start(bf16[2,3,192,128]{3,2,1,0:T(8,128)(2,1)S(1)} %get-tuple-element.30), channel_id=1, source_target_pairs={{0,1},{1,0},{2,3},{3,2},{4,5},{5,4},{6,7},{7,6},{8,9},{9,8},{10,11... | collective-permute-start | bytes 884744 | tf_op jit(solution)/shard_map/ppermute | solution.py:387
  51.5 6.3 %collective-permute-start.7 = (bf16[3,192,128]{2,1,0:T(8,128)(2,1)S(1)}, bf16[3,192,128]{2,1,0:T(8,128)(2,1)S(1)}, u32[]{:S(2)}, u32[]{:S(2)}) collective-permute-start(bf16[3,192,128]{2,1,0:T(8,128)(2,1)S(1)} %get-tuple-element.32), channel_id=1, source_target_pairs={{0,4},{1,5},{2,6},{3,7},{4,0},{5,1},{6,2},{7,3},{8,12},{9,13},{10,... | collective-permute-start | bytes 442376 | tf_op jit(solution)/shard_map/ppermute | solution.py:394
  53.1 13.4 %collective-permute-start.11 = (bf16[6,48,128]{2,1,0:T(8,128)(2,1)S(1)}, bf16[6,48,128]{2,1,0:T(8,128)(2,1)S(1)}, u32[]{:S(2)}, u32[]{:S(2)}) collective-permute-start(bf16[6,48,128]{2,1,0:T(8,128)(2,1)S(1)} %get-tuple-element.39), channel_id=1, source_target_pairs={{0,2},{2,0},{12,14},{14,12},{1,3},{3,1},{13,15},{15,13},{4,6},{6,4... | collective-permute-start | bytes 221192 | tf_op jit(solution)/shard_map/ppermute | solution.py:330
  53.9 13.3 %collective-permute-start.12 = (bf16[6,48,128]{2,1,0:T(8,128)(2,1)S(1)}, bf16[6,48,128]{2,1,0:T(8,128)(2,1)S(1)}, u32[]{:S(2)}, u32[]{:S(2)}) collective-permute-start(bf16[6,48,128]{2,1,0:T(8,128)(2,1)S(1)} %get-tuple-element.40), channel_id=1, source_target_pairs={{0,12},{2,14},{12,0},{14,2},{1,13},{3,15},{13,1},{15,3},{4,8},{6,1... | collective-permute-start | bytes 221192 | tf_op jit(solution)/shard_map/ppermute | solution.py:330
  56.5 10.7 %collective-permute-start.13 = (bf16[6,48,128]{2,1,0:T(8,128)(2,1)S(1)}, bf16[6,48,128]{2,1,0:T(8,128)(2,1)S(1)}, u32[]{:S(2)}, u32[]{:S(2)}) collective-permute-start(bf16[6,48,128]{2,1,0:T(8,128)(2,1)S(1)} %get-tuple-element.41), channel_id=1, source_target_pairs={{0,14},{2,12},{12,2},{14,0},{1,15},{3,13},{13,3},{15,1},{4,10},{6,... | collective-permute-start | bytes 221192 | tf_op jit(solution)/shard_map/ppermute | solution.py:330
  62.4 6.3 %collective-permute-start.10 = (bf16[4,48,128]{2,1,0:T(8,128)(2,1)S(1)}, bf16[4,48,128]{2,1,0:T(8,128)(2,1)S(1)}, u32[]{:S(2)}, u32[]{:S(2)}) collective-permute-start(bf16[4,48,128]{2,1,0:T(8,128)(2,1)S(1)} %get-tuple-element.37), channel_id=1, source_target_pairs={{0,14},{2,12},{12,2},{14,0},{1,15},{3,13},{13,3},{15,1},{4,10},{6,... | collective-permute-start | bytes 147464 | tf_op jit(solution)/shard_map/ppermute | solution.py:330
  65.5 4.1 %collective-permute-start.8 = (bf16[4,48,128]{2,1,0:T(8,128)(2,1)S(1)}, bf16[4,48,128]{2,1,0:T(8,128)(2,1)S(1)}, u32[]{:S(2)}, u32[]{:S(2)}) collective-permute-start(bf16[4,48,128]{2,1,0:T(8,128)(2,1)S(1)} %get-tuple-element.35), channel_id=1, source_target_pairs={{0,2},{2,0},{12,14},{14,12},{1,3},{3,1},{13,15},{15,13},{4,6},{6,4... | collective-permute-start | bytes 147464 | tf_op jit(solution)/shard_map/ppermute | solution.py:330
  66.5 5.3 %collective-permute-start.9 = (bf16[4,48,128]{2,1,0:T(8,128)(2,1)S(1)}, bf16[4,48,128]{2,1,0:T(8,128)(2,1)S(1)}, u32[]{:S(2)}, u32[]{:S(2)}) collective-permute-start(bf16[4,48,128]{2,1,0:T(8,128)(2,1)S(1)} %get-tuple-element.36), channel_id=1, source_target_pairs={{0,12},{2,14},{12,0},{14,2},{1,13},{3,15},{13,1},{15,3},{4,8},{6,1... | collective-permute-start | bytes 147464 | tf_op jit(solution)/shard_map/ppermute | solution.py:330

commit v6 on v5

--- a/solution.py
+++ b/solution.py
@@ -66,8 +66,8 @@
     ]
     for copy in copies:
         copy.start()
-    for copy in copies:
-        copy.wait()
+    for k in (3, 4, 5, 6):
+        copies[k].wait()
     q_ref, kv_ref, g_ref, bias_ref, norm_ref, delta_ref, valid_ref = local
     heads, cols, _ = bias_ref.shape
     n_i, _, width = q_ref.shape
@@ -80,27 +80,7 @@
     back = count - c * cols
     mask = pltpu.roll(mask, back, 1)[0:1, 0:cols]
     for h in range(heads):
-        lo, hi = h * size, (h + 1) * size
         to = jnp.bitwise_xor(position, h)
-        for p in range(pairs):
-            staged[to, p] = jnp.concatenate(
-                [
-                    q_ref[2 * p, :, lo:hi],
-                    g_ref[2 * p, :, lo:hi],
-                    q_ref[2 * p + 1, :, lo:hi],
-                    g_ref[2 * p + 1, :, lo:hi],
-                ],
-                axis=-1,
-            )
-            staged[to, pairs + p] = jnp.concatenate(
-                [
-                    kv_ref[2 * p, :, lo:hi],
-                    kv_ref[2 * p, :, width + lo : width + hi],
-                    kv_ref[2 * p + 1, :, lo:hi],
-                    kv_ref[2 * p + 1, :, width + lo : width + hi],
-                ],
-                axis=-1,
-            )
         rows[...] = jnp.zeros_like(rows)
         norm = norm_ref[:, h, :] * root
         high = norm.astype(BF).astype(F32)
@@ -115,6 +95,35 @@
         staged[to, 2 * pairs] = jnp.concatenate(
             [turned[:, 0:64], tile, jnp.zeros((cols, 64 - cols), F32)], axis=-1
         ).astype(BF)
+    copies[0].wait()
+    copies[2].wait()
+    for h in range(heads):
+        lo, hi = h * size, (h + 1) * size
+        to = jnp.bitwise_xor(position, h)
+        for p in range(pairs):
+            staged[to, p] = jnp.concatenate(
+                [
+                    q_ref[2 * p, :, lo:hi],
+                    g_ref[2 * p, :, lo:hi],
+                    q_ref[2 * p + 1, :, lo:hi],
+                    g_ref[2 * p + 1, :, lo:hi],
+                ],
+                axis=-1,
+            )
+    copies[1].wait()
+    for h in range(heads):
+        lo, hi = h * size, (h + 1) * size
+        to = jnp.bitwise_xor(position, h)
+        for p in range(pairs):
+            staged[to, pairs + p] = jnp.concatenate(
+                [
+                    kv_ref[2 * p, :, lo:hi],
+                    kv_ref[2 * p, :, width + lo : width + hi],
+                    kv_ref[2 * p + 1, :, lo:hi],
+                    kv_ref[2 * p + 1, :, width + lo : width + hi],
+                ],
+                axis=-1,
+            )
     for step in range(heads):
         out_refs[step][...] = staged[step]
 

time: 73.3 us -> 73.5 us (level)
  no operation moved by 1% of the time
where the time goes in v6:
time: 73.5 us; the launch traced here: 73.2 us
  starting transfers between devices  30.4 us (41%)
  waiting for transfers between devices  29.8 us (41%)
  Pallas kernels  11.4 us (16%)
  local copies, waits for them, and re-layouts  0.91 us (1%)
    ppermute x9, starting transfers between devices, traded(): lax.ppermute(blocks[k], 'col', trade(k))  14.2 us
    all_to_all x1, waiting for transfers between devices, on_device(): bias_rows = lax.all_to_all(band, 'row', 0, 0, tiled=True)  11.4 us
    ppermute x9, waiting for transfers between devices, traded(): lax.ppermute(blocks[k], 'col', trade(k))  10.8 us
    all_to_all x1, starting transfers between devices, on_device(): bias_rows = lax.all_to_all(band, 'row', 0, 0, tiled=True)  10.2 us
    pallas_call x1, Pallas kernels, on_device(): call(functools.partial(main_kernel, size ** (-0.5)), 'main', (dq_block, d...  5.97 us
    all_to_all x1, waiting for transfers between devices, on_device(): parts_in = lax.all_to_all(dbias, 'row', 0, 0, tiled=True)  4.41 us
    all_to_all x1, starting transfers between devices, on_device(): parts_in = lax.all_to_all(dbias, 'row', 0, 0, tiled=True)  3.54 us
    pallas_call x1, Pallas kernels, on_device(): call(functools.partial(pack_kernel, math.sqrt(size)), 'pack', (struct((2...  2.75 us
  transfers between devices with their start and end apart: 16, of which 10 were waited for; matrix products, arithmetic and copies ran while one was open for 0% of the time, Pallas kernels for 2%

profile of v6, /device:TPU:32, one launch (start us, length us, event | category | flops | bytes accessed | tf_op | source)
XLA Modules:
  0.0 73.2 jit_solution(12576676306113937142)
XLA Ops:
  0.6 2.8 %pack.1 = (bf16[13,48,128]{2,1,0:T(8,128)(2,1)}, bf16[13,48,128]{2,1,0:T(8,128)(2,1)}, bf16[13,48,128]{2,1,0:T(8,128)(2,1)}, bf16[13,48,128]{2,1,0:T(8,128)(2,1)}) custom-call(bf16[12,48,128]{2,1,0:T(8,128)(2,1)} %refs_0_.1, bf16[12,48,256]{2,1,0:T(8,128)(2,1)} %refs_1_.1, bf16[12,48,128]{2,1,0:T(8,128)(2,1)} %refs_2_.1, bf16[4,48,48]{2,1,0:T(8,128)(2,1)} %refs_3_.1, ...), custom_call_target="tpu_custom_call" | custom-call | tf_op jit(solution)/shard_map/pack/pallas_call | solution.py:341
  3.4 1.9 %collective-permute-start = (bf16[13,48,128]{2,1,0:T(8,128)(2,1)}, bf16[13,48,128]{2,1,0:T(8,128)(2,1)S(1)}, u32[]{:S(2)}, u32[]{:S(2)}) collective-permute-start(bf16[13,48,128]{2,1,0:T(8,128)(2,1)} %get-tuple-element.25), channel_id=1, source_target_pairs={{0,2},{2,0},{12,14},{14,12},{1,3},{3,1},{13,15},{15,13},{4,6},{6,4... | collective-permute-start | bytes 479240 | tf_op jit(solution)/shard_map/ppermute | solution.py:339
  5.3 1.0 %collective-permute-start.1 = (bf16[13,48,128]{2,1,0:T(8,128)(2,1)}, bf16[13,48,128]{2,1,0:T(8,128)(2,1)S(1)}, u32[]{:S(2)}, u32[]{:S(2)}) collective-permute-start(bf16[13,48,128]{2,1,0:T(8,128)(2,1)} %get-tuple-element.26), channel_id=1, source_target_pairs={{0,12},{2,14},{12,0},{14,2},{1,13},{3,15},{13,1},{15,3},{4,8},{6,1... | collective-permute-start | bytes 479240 | tf_op jit(solution)/shard_map/ppermute | solution.py:339
  6.3 1.8 %collective-permute-start.2 = (bf16[13,48,128]{2,1,0:T(8,128)(2,1)}, bf16[13,48,128]{2,1,0:T(8,128)(2,1)S(1)}, u32[]{:S(2)}, u32[]{:S(2)}) collective-permute-start(bf16[13,48,128]{2,1,0:T(8,128)(2,1)} %get-tuple-element.27), channel_id=1, source_target_pairs={{0,14},{2,12},{12,2},{14,0},{1,15},{3,13},{13,3},{15,1},{4,10},{6,... | collective-permute-start | bytes 479240 | tf_op jit(solution)/shard_map/ppermute | solution.py:339
  8.2 0.0 copy-start
  8.2 0.9 %copy-done = bf16[13,48,128]{2,1,0:T(8,128)(2,1)S(1)} copy-done((bf16[13,48,128]{2,1,0:T(8,128)(2,1)S(1)}, bf16[13,48,128]{2,1,0:T(8,128)(2,1)}, u32[]{:S(2)}) %copy-start) | copy-done | bytes 159768
  9.1 0.2 hold.1.refs_0_
  9.3 1.1 %collective-permute-done.refs_1_ = bf16[13,48,128]{2,1,0:T(8,128)(2,1)S(1)} collective-permute-done((bf16[13,48,128]{2,1,0:T(8,128)(2,1)}, bf16[13,48,128]{2,1,0:T(8,128)(2,1)S(1)}, u32[]{:S(2)}, u32[]{:S(2)}) %collective-permute-start) | collective-permute-done | bytes 159776 | tf_op jit(solution)/shard_map/ppermute | solution.py:339
  10.4 5.0 %collective-permute-done.1.refs_2_ = bf16[13,48,128]{2,1,0:T(8,128)(2,1)S(1)} collective-permute-done((bf16[13,48,128]{2,1,0:T(8,128)(2,1)}, bf16[13,48,128]{2,1,0:T(8,128)(2,1)S(1)}, u32[]{:S(2)}, u32[]{:S(2)}) %collective-permute-start.1) | collective-permute-done | bytes 159776 | tf_op jit(solution)/shard_map/ppermute | solution.py:339
  15.4 0.0 collective-permute-done.2.refs_3_
  15.5 0.1 collective-permute-start.4
  15.6 0.9 %band.1 = bf16[16,80,128]{2,1,0:T(8,128)(2,1)} custom-call(bf16[13,48,128]{2,1,0:T(8,128)(2,1)S(1)} %hold.1.refs_0_, bf16[13,48,128]{2,1,0:T(8,128)(2,1)S(1)} %collective-permute-done.refs_1_, bf16[13,48,128]{2,1,0:T(8,128)(2,1)S(1)} %collective-permute-done.1.refs_2_, bf16[13,48,128]{2,1,0:T(8,128)(2,1)S(1)} %collective-permute-done.2.refs_3_), custom_call_target="tpu_custom_call" | custom-call | tf_op jit(solution)/shard_map/band/pallas_call | solution.py:368
  16.4 10.2 %all-to-all-start = ((bf16[16,80,128]{2,1,0:T(8,128)(2,1)}), bf16[16,80,128]{2,1,0:T(8,128)(2,1)S(1)}, u32[]{:S(2)}, u32[]{:S(2)}) async-start(bf16[16,80,128]{2,1,0:T(8,128)(2,1)} %band.1), calls=%async_computation | async-start | bytes 655360 | tf_op jit(solution)/shard_map/all_to_all | solution.py:369
  26.7 0.1 collective-permute-start.3
  26.8 0.0 collective-permute-done.4.a2_ref
  26.8 0.5 collective-permute-start.5
  27.3 1.1 %collective-permute-done.3.a1_ref = bf16[7,192,128]{2,1,0:T(8,128)(2,1)S(1)} collective-permute-done((bf16[7,192,128]{2,1,0:T(8,128)(2,1)S(1)}, bf16[7,192,128]{2,1,0:T(8,128)(2,1)S(1)}, u32[]{:S(2)}, u32[]{:S(2)}) %collective-permute-start.3) | collective-permute-done | bytes 344096 | tf_op jit(solution)/shard_map/ppermute | solution.py:365
  28.4 0.5 collective-permute-done.5.a3_ref
  28.9 0.1 join.1.refs_4_
  29.0 11.4 %all-to-all-done.refs_5_ = bf16[16,80,128]{2,1,0:T(8,128)(2,1)S(1)} async-done(((bf16[16,80,128]{2,1,0:T(8,128)(2,1)}), bf16[16,80,128]{2,1,0:T(8,128)(2,1)S(1)}, u32[]{:S(2)}, u32[]{:S(2)}) %all-to-all-start) | async-done | bytes 327712 | tf_op jit(solution)/shard_map/all_to_all | solution.py:369
  40.4 6.0 %main.1 = (bf16[3,192,128]{2,1,0:T(8,128)(2,1)S(1)}, bf16[3,192,128]{2,1,0:T(8,128)(2,1)S(1)}, bf16[2,3,192,128]{3,2,1,0:T(8,128)(2,1)S(1)}, bf16[6,48,128]{2,1,...) custom-call(bf16[13,48,128]{2,1,0:T(8,128)(2,1)S(1)} %hold.1.refs_0_, ...), custom_call_target="tpu_custom_call" | custom-call | tf_op jit(solution)/shard_map/main/pallas_call | solution.py:378
  46.3 3.5 %all-to-all-start.1 = ((bf16[16,80,128]{2,1,0:T(8,128)(2,1)}), bf16[16,80,128]{2,1,0:T(8,128)(2,1)S(1)}, u32[]{:S(2)}, u32[]{:S(2)}) async-start(bf16[16,80,128]{2,1,0:T(8,128)(2,1)} %get-tuple-element.33), calls=%async_computation.1 | async-start | bytes 655360 | tf_op jit(solution)/shard_map/all_to_all | solution.py:404
  49.9 0.1 collective-permute-start.6
  50.0 1.6 %collective-permute-done.6.got_ref = bf16[2,3,192,128]{3,2,1,0:T(8,128)(2,1)S(1)} collective-permute-done((bf16[2,3,192,128]{3,2,1,0:T(8,128)(2,1)S(1)}, bf16[2,3,192,128]{3,2,1,0:T(8,128)(2,1)S(1)}, u32[]{:S(2)}, u32[]{:S(2)}) %collective-permute-start.6) | collective-permute-done | bytes 294944 | tf_op jit(solution)/shard_map/ppermute | solution.py:396
  51.6 0.1 fold_core.1
  51.6 1.6 %collective-permute-start.7 = (bf16[3,192,128]{2,1,0:T(8,128)(2,1)S(1)}, bf16[3,192,128]{2,1,0:T(8,128)(2,1)S(1)}, u32[]{:S(2)}, u32[]{:S(2)}) collective-permute-start(bf16[3,192,128]{2,1,0:T(8,128)(2,1)S(1)} %get-tuple-element.32), channel_id=1, source_target_pairs={{0,4},{1,5},{2,6},{3,7},{4,0},{5,1},{6,2},{7,3},{8,12},{9,13},{10,... | collective-permute-start | bytes 442376 | tf_op jit(solution)/shard_map/ppermute | solution.py:403
  53.2 0.8 %collective-permute-start.11 = (bf16[6,48,128]{2,1,0:T(8,128)(2,1)S(1)}, bf16[6,48,128]{2,1,0:T(8,128)(2,1)S(1)}, u32[]{:S(2)}, u32[]{:S(2)}) collective-permute-start(bf16[6,48,128]{2,1,0:T(8,128)(2,1)S(1)} %get-tuple-element.39), channel_id=1, source_target_pairs={{0,2},{2,0},{12,14},{14,12},{1,3},{3,1},{13,15},{15,13},{4,6},{6,4... | collective-permute-start | bytes 221192 | tf_op jit(solution)/shard_map/ppermute | solution.py:339
  54.0 2.6 %collective-permute-start.12 = (bf16[6,48,128]{2,1,0:T(8,128)(2,1)S(1)}, bf16[6,48,128]{2,1,0:T(8,128)(2,1)S(1)}, u32[]{:S(2)}, u32[]{:S(2)}) collective-permute-start(bf16[6,48,128]{2,1,0:T(8,128)(2,1)S(1)} %get-tuple-element.40), channel_id=1, source_target_pairs={{0,12},{2,14},{12,0},{14,2},{1,13},{3,15},{13,1},{15,3},{4,8},{6,1... | collective-permute-start | bytes 221192 | tf_op jit(solution)/shard_map/ppermute | solution.py:339
  56.6 1.3 %collective-permute-start.13 = (bf16[6,48,128]{2,1,0:T(8,128)(2,1)S(1)}, bf16[6,48,128]{2,1,0:T(8,128)(2,1)S(1)}, u32[]{:S(2)}, u32[]{:S(2)}) collective-permute-start(bf16[6,48,128]{2,1,0:T(8,128)(2,1)S(1)} %get-tuple-element.41), channel_id=1, source_target_pairs={{0,14},{2,12},{12,2},{14,0},{1,15},{3,13},{13,3},{15,1},{4,10},{6,... | collective-permute-start | bytes 221192 | tf_op jit(solution)/shard_map/ppermute | solution.py:339
  57.9 0.0 collective-permute-done.7.got_ref
  58.0 4.4 %all-to-all-done.1.db_ref = bf16[16,80,128]{2,1,0:T(8,128)(2,1)S(1)} async-done(((bf16[16,80,128]{2,1,0:T(8,128)(2,1)}), bf16[16,80,128]{2,1,0:T(8,128)(2,1)S(1)}, u32[]{:S(2)}, u32[]{:S(2)}) %all-to-all-start.1) | async-done | bytes 327712 | tf_op jit(solution)/shard_map/all_to_all | solution.py:404
  62.4 0.2 merge.1
  62.5 3.2 %collective-permute-start.10 = (bf16[4,48,128]{2,1,0:T(8,128)(2,1)S(1)}, bf16[4,48,128]{2,1,0:T(8,128)(2,1)S(1)}, u32[]{:S(2)}, u32[]{:S(2)}) collective-permute-start(bf16[4,48,128]{2,1,0:T(8,128)(2,1)S(1)} %get-tuple-element.37), channel_id=1, source_target_pairs={{0,14},{2,12},{12,2},{14,0},{1,15},{3,13},{13,3},{15,1},{4,10},{6,... | collective-permute-start | bytes 147464 | tf_op jit(solution)/shard_map/ppermute | solution.py:339
  65.7 0.9 %collective-permute-start.8 = (bf16[4,48,128]{2,1,0:T(8,128)(2,1)S(1)}, bf16[4,48,128]{2,1,0:T(8,128)(2,1)S(1)}, u32[]{:S(2)}, u32[]{:S(2)}) collective-permute-start(bf16[4,48,128]{2,1,0:T(8,128)(2,1)S(1)} %get-tuple-element.35), channel_id=1, source_target_pairs={{0,2},{2,0},{12,14},{14,12},{1,3},{3,1},{13,15},{15,13},{4,6},{6,4... | collective-permute-start | bytes 147464 | tf_op jit(solution)/shard_map/ppermute | solution.py:339
  66.6 0.0 collective-permute-done.11.refs_5_
  66.6 0.7 collective-permute-start.9
  67.3 0.0 collective-permute-done.12.refs_6_
  67.3 0.0 collective-permute-done.13.refs_7_
  67.3 1.5 %collective-permute-done.10.refs_3_ = bf16[4,48,128]{2,1,0:T(8,128)(2,1)S(1)} collective-permute-done((bf16[4,48,128]{2,1,0:T(8,128)(2,1)S(1)}, bf16[4,48,128]{2,1,0:T(8,128)(2,1)S(1)}, u32[]{:S(2)}, u32[]{:S(2)}) %collective-permute-start.10) | collective-permute-done | bytes 49184 | tf_op jit(solution)/shard_map/ppermute | solution.py:339
  68.8 1.0 %collective-permute-done.8.refs_1_ = bf16[4,48,128]{2,1,0:T(8,128)(2,1)S(1)} collective-permute-done((bf16[4,48,128]{2,1,0:T(8,128)(2,1)S(1)}, bf16[4,48,128]{2,1,0:T(8,128)(2,1)S(1)}, u32[]{:S(2)}, u32[]{:S(2)}) %collective-permute-start.8) | collective-permute-done | bytes 49184 | tf_op jit(solution)/shard_map/ppermute | solution.py:339
  69.8 2.2 %collective-permute-done.9.refs_2_ = bf16[4,48,128]{2,1,0:T(8,128)(2,1)S(1)} collective-permute-done((bf16[4,48,128]{2,1,0:T(8,128)(2,1)S(1)}, bf16[4,48,128]{2,1,0:T(8,128)(2,1)S(1)}, u32[]{:S(2)}, u32[]{:S(2)}) %collective-permute-start.9) | collective-permute-done | bytes 49184 | tf_op jit(solution)/shard_map/ppermute | solution.py:339
  71.9 1.2 %final.1 = (bf16[12,48,128]{2,1,0:T(8,128)(2,1)}, bf16[12,48,256]{2,1,0:T(8,128)(2,1)}, f32[4,48,48]{2,1,0:T(8,128)}) custom-call(bf16[4,48,128]{2,1,0:T(8,128)(2,1)S(1)} %get-tuple-element.34.refs_0_, bf16[4,48,128]{2,1,0:T(8,128)(2,1)S(1)} %collective-permute-done.8.refs_1_, bf16[4,48,128]{2,1,0:T(8,128)(2,1)S(1)} %collective-permute-done.9.refs_2_, ...), custom_call_target="tpu_custom_call" | custom-call | tf_op jit(solution)/shard_map/final/pallas_call | solution.py:412
  (2 shorter events, 0.1 us)
Async XLA Ops:
  3.4 7.0 %collective-permute-start = (bf16[13,48,128]{2,1,0:T(8,128)(2,1)}, bf16[13,48,128]{2,1,0:T(8,128)(2,1)S(1)}, u32[]{:S(2)}, u32[]{:S(2)}) collective-permute-start(bf16[13,48,128]{2,1,0:T(8,128)(2,1)} %get-tuple-element.25), channel_id=1, source_target_pairs={{0,2},{2,0},{12,14},{14,12},{1,3},{3,1},{13,15},{15,13},{4,6},{6,4... | collective-permute-start | bytes 479240 | tf_op jit(solution)/shard_map/ppermute | solution.py:339
  5.3 10.1 %collective-permute-start.1 = (bf16[13,48,128]{2,1,0:T(8,128)(2,1)}, bf16[13,48,128]{2,1,0:T(8,128)(2,1)S(1)}, u32[]{:S(2)}, u32[]{:S(2)}) collective-permute-start(bf16[13,48,128]{2,1,0:T(8,128)(2,1)} %get-tuple-element.26), channel_id=1, source_target_pairs={{0,12},{2,14},{12,0},{14,2},{1,13},{3,15},{13,1},{15,3},{4,8},{6,1... | collective-permute-start | bytes 479240 | tf_op jit(solution)/shard_map/ppermute | solution.py:339
  6.3 9.1 %collective-permute-start.2 = (bf16[13,48,128]{2,1,0:T(8,128)(2,1)}, bf16[13,48,128]{2,1,0:T(8,128)(2,1)S(1)}, u32[]{:S(2)}, u32[]{:S(2)}) collective-permute-start(bf16[13,48,128]{2,1,0:T(8,128)(2,1)} %get-tuple-element.27), channel_id=1, source_target_pairs={{0,14},{2,12},{12,2},{14,0},{1,15},{3,13},{13,3},{15,1},{4,10},{6,... | collective-permute-start | bytes 479240 | tf_op jit(solution)/shard_map/ppermute | solution.py:339
  8.2 0.9 %copy-start = (bf16[13,48,128]{2,1,0:T(8,128)(2,1)S(1)}, bf16[13,48,128]{2,1,0:T(8,128)(2,1)}, u32[]{:S(2)}) copy-start(bf16[13,48,128]{2,1,0:T(8,128)(2,1)} %get-tuple-element.24.src_ref) | copy-start | bytes 479236
  15.5 11.3 %collective-permute-start.4 = (bf16[7,192,128]{2,1,0:T(8,128)(2,1)S(1)}, bf16[7,192,128]{2,1,0:T(8,128)(2,1)S(1)}, u32[]{:S(2)}, u32[]{:S(2)}) collective-permute-start(bf16[7,192,128]{2,1,0:T(8,128)(2,1)S(1)} %own.1.a0_ref), channel_id=1, source_target_pairs={{0,4},{1,5},{2,6},{3,7},{4,0},{5,1},{6,2},{7,3},{8,12},{9,13},{10,... | collective-permute-start | bytes 1032200 | tf_op jit(solution)/shard_map/ppermute | solution.py:364
  16.4 23.9 %all-to-all-start = ((bf16[16,80,128]{2,1,0:T(8,128)(2,1)}), bf16[16,80,128]{2,1,0:T(8,128)(2,1)S(1)}, u32[]{:S(2)}, u32[]{:S(2)}) async-start(bf16[16,80,128]{2,1,0:T(8,128)(2,1)} %band.1), calls=%async_computation | async-start | bytes 655360 | tf_op jit(solution)/shard_map/all_to_all | solution.py:369
  26.7 1.7 %collective-permute-start.3 = (bf16[7,192,128]{2,1,0:T(8,128)(2,1)S(1)}, bf16[7,192,128]{2,1,0:T(8,128)(2,1)S(1)}, u32[]{:S(2)}, u32[]{:S(2)}) collective-permute-start(bf16[7,192,128]{2,1,0:T(8,128)(2,1)S(1)} %own.1.a0_ref), channel_id=1, source_target_pairs={{0,1},{1,0},{2,3},{3,2},{4,5},{5,4},{6,7},{7,6},{8,9},{9,8},{10,11... | collective-permute-start | bytes 1032200 | tf_op jit(solution)/shard_map/ppermute | solution.py:365
  26.8 2.1 %collective-permute-start.5 = (bf16[7,192,128]{2,1,0:T(8,128)(2,1)S(1)}, bf16[7,192,128]{2,1,0:T(8,128)(2,1)S(1)}, u32[]{:S(2)}, u32[]{:S(2)}) collective-permute-start(bf16[7,192,128]{2,1,0:T(8,128)(2,1)S(1)} %collective-permute-done.4.a2_ref), channel_id=1, source_target_pairs={{0,1},{1,0},{2,3},{3,2},{4,5},{5,4},{6,7},{7,6},{8,9},{9,8},{10,11... | collective-permute-start | bytes 1032200 | tf_op jit(solution)/shard_map/ppermute | solution.py:370
  46.3 16.0 %all-to-all-start.1 = ((bf16[16,80,128]{2,1,0:T(8,128)(2,1)}), bf16[16,80,128]{2,1,0:T(8,128)(2,1)S(1)}, u32[]{:S(2)}, u32[]{:S(2)}) async-start(bf16[16,80,128]{2,1,0:T(8,128)(2,1)} %get-tuple-element.33), calls=%async_computation.1 | async-start | bytes 655360 | tf_op jit(solution)/shard_map/all_to_all | solution.py:404
  49.9 1.7 %collective-permute-start.6 = (bf16[2,3,192,128]{3,2,1,0:T(8,128)(2,1)S(1)}, bf16[2,3,192,128]{3,2,1,0:T(8,128)(2,1)S(1)}, u32[]{:S(2)}, u32[]{:S(2)}) collective-permute-start(bf16[2,3,192,128]{3,2,1,0:T(8,128)(2,1)S(1)} %get-tuple-element.30), channel_id=1, source_target_pairs={{0,1},{1,0},{2,3},{3,2},{4,5},{5,4},{6,7},{7,6},{8,9},{9,8},{10,11... | collective-permute-start | bytes 884744 | tf_op jit(solution)/shard_map/ppermute | solution.py:396
  51.6 6.3 %collective-permute-start.7 = (bf16[3,192,128]{2,1,0:T(8,128)(2,1)S(1)}, bf16[3,192,128]{2,1,0:T(8,128)(2,1)S(1)}, u32[]{:S(2)}, u32[]{:S(2)}) collective-permute-start(bf16[3,192,128]{2,1,0:T(8,128)(2,1)S(1)} %get-tuple-element.32), channel_id=1, source_target_pairs={{0,4},{1,5},{2,6},{3,7},{4,0},{5,1},{6,2},{7,3},{8,12},{9,13},{10,... | collective-permute-start | bytes 442376 | tf_op jit(solution)/shard_map/ppermute | solution.py:403
  53.2 13.4 %collective-permute-start.11 = (bf16[6,48,128]{2,1,0:T(8,128)(2,1)S(1)}, bf16[6,48,128]{2,1,0:T(8,128)(2,1)S(1)}, u32[]{:S(2)}, u32[]{:S(2)}) collective-permute-start(bf16[6,48,128]{2,1,0:T(8,128)(2,1)S(1)} %get-tuple-element.39), channel_id=1, source_target_pairs={{0,2},{2,0},{12,14},{14,12},{1,3},{3,1},{13,15},{15,13},{4,6},{6,4... | collective-permute-start | bytes 221192 | tf_op jit(solution)/shard_map/ppermute | solution.py:339
  54.0 13.3 %collective-permute-start.12 = (bf16[6,48,128]{2,1,0:T(8,128)(2,1)S(1)}, bf16[6,48,128]{2,1,0:T(8,128)(2,1)S(1)}, u32[]{:S(2)}, u32[]{:S(2)}) collective-permute-start(bf16[6,48,128]{2,1,0:T(8,128)(2,1)S(1)} %get-tuple-element.40), channel_id=1, source_target_pairs={{0,12},{2,14},{12,0},{14,2},{1,13},{3,15},{13,1},{15,3},{4,8},{6,1... | collective-permute-start | bytes 221192 | tf_op jit(solution)/shard_map/ppermute | solution.py:339
  56.6 10.7 %collective-permute-start.13 = (bf16[6,48,128]{2,1,0:T(8,128)(2,1)S(1)}, bf16[6,48,128]{2,1,0:T(8,128)(2,1)S(1)}, u32[]{:S(2)}, u32[]{:S(2)}) collective-permute-start(bf16[6,48,128]{2,1,0:T(8,128)(2,1)S(1)} %get-tuple-element.41), channel_id=1, source_target_pairs={{0,14},{2,12},{12,2},{14,0},{1,15},{3,13},{13,3},{15,1},{4,10},{6,... | collective-permute-start | bytes 221192 | tf_op jit(solution)/shard_map/ppermute | solution.py:339
  62.5 6.3 %collective-permute-start.10 = (bf16[4,48,128]{2,1,0:T(8,128)(2,1)S(1)}, bf16[4,48,128]{2,1,0:T(8,128)(2,1)S(1)}, u32[]{:S(2)}, u32[]{:S(2)}) collective-permute-start(bf16[4,48,128]{2,1,0:T(8,128)(2,1)S(1)} %get-tuple-element.37), channel_id=1, source_target_pairs={{0,14},{2,12},{12,2},{14,0},{1,15},{3,13},{13,3},{15,1},{4,10},{6,... | collective-permute-start | bytes 147464 | tf_op jit(solution)/shard_map/ppermute | solution.py:339
  65.7 4.1 %collective-permute-start.8 = (bf16[4,48,128]{2,1,0:T(8,128)(2,1)S(1)}, bf16[4,48,128]{2,1,0:T(8,128)(2,1)S(1)}, u32[]{:S(2)}, u32[]{:S(2)}) collective-permute-start(bf16[4,48,128]{2,1,0:T(8,128)(2,1)S(1)} %get-tuple-element.35), channel_id=1, source_target_pairs={{0,2},{2,0},{12,14},{14,12},{1,3},{3,1},{13,15},{15,13},{4,6},{6,4... | collective-permute-start | bytes 147464 | tf_op jit(solution)/shard_map/ppermute | solution.py:339
  66.6 5.3 %collective-permute-start.9 = (bf16[4,48,128]{2,1,0:T(8,128)(2,1)S(1)}, bf16[4,48,128]{2,1,0:T(8,128)(2,1)S(1)}, u32[]{:S(2)}, u32[]{:S(2)}) collective-permute-start(bf16[4,48,128]{2,1,0:T(8,128)(2,1)S(1)} %get-tuple-element.36), channel_id=1, source_target_pairs={{0,12},{2,14},{12,0},{14,2},{1,13},{3,15},{13,1},{15,3},{4,8},{6,1... | collective-permute-start | bytes 147464 | tf_op jit(solution)/shard_map/ppermute | solution.py:339
